TPU v7x, 128 devices: a whole 4x4x4 slice. The times are simulated.
128 devices in a mesh: wide: 32 (over y, z, core), mp: 4 (over x).
Axes of the slice: x: 4, y: 4, z: 4, core: 2. Of those that a mesh axis runs over, the one named last changes fastest.
Arguments:
- queries: bfloat16 [32, 128, 8192], P('wide', None, 'mp'), may hold values from -6 to 6
- own_keys: bfloat16 [32, 128, 1024], P('wide', None, 'mp'), may hold values from -6 to 6
- own_values: bfloat16 [32, 128, 1024], P('wide', None, 'mp'), may hold values from -6 to 6
- cart_keys: bfloat16 [512, 128, 1024], P('wide', None, 'mp'), may hold values from -6 to 6
- cart_values: bfloat16 [512, 128, 1024], P('wide', None, 'mp'), may hold values from -6 to 6
- block_ids: int32 [32, 16], P('wide'), may hold values from 0 to 511, as said below
- block_home: int32 [512], replicated, may hold values from 0 to 511, as said below
- query_len: int32 [32], P('wide'), may hold values from 32 to 128, as said below
- grad_out: bfloat16 [32, 128, 8192], P('wide', None, 'mp'), may hold values from -6 to 6
Outputs:
- attn_out: bfloat16 [32, 128, 8192], P('wide', None, 'mp')
- grad_queries: bfloat16 [32, 128, 8192], P('wide', None, 'mp')
- key_update: float32 [512, 128, 1024], P('wide', None, 'mp')
- value_update: float32 [512, 128, 1024], P('wide', None, 'mp')
Inputs may be any that keep to these rules, and one draw needn't show every extreme that they name: `block_ids`: the 16 ids of a request are distinct, and the 1 request of one index of wide read the same 16 ids, each in an order of its own; their storage rows lie on exactly 16 owner devices, exactly 1 on each, the owner of id b being block_home[b] // 16. `block_home`: each storage row appears once. `query_len`: some request uses all 128 slots.
All inputs are finite; a program needn't handle non-finite values.
Results may differ from a plain program's by a relative error of at most 0.011.
Values may be sent and summed in bfloat16 or wider, within the bound.
No kernel may reach another device: no remote copies, remote signals or barrier semaphores. Data moves between devices by JAX's collectives and lax.ppermute only.
A program may use at most 128 MiB of HBM per device.

v0:
```python
import math

import jax
import jax.numpy as jnp
from jax import lax
from jax.sharding import PartitionSpec as P

HD = 128


def attend_head(query_rows, keys, values, key_seen, row_used, grad_rows, scale):
    length = query_rows.shape[0]
    head_size = keys.shape[1]
    repeat = query_rows.shape[1] // head_size
    query_flat = query_rows.reshape(length * repeat, head_size)
    grad_flat = grad_rows.reshape(length * repeat, head_size)
    seen_flat = jnp.repeat(key_seen, repeat, axis=0)
    used_flat = jnp.repeat(row_used, repeat, axis=0)
    scores = jnp.dot(query_flat, keys.T, preferred_element_type=jnp.float32) * scale
    scores = jnp.where(seen_flat, scores, -1e30)
    top = jnp.max(scores, axis=-1, keepdims=True)
    expo = jnp.exp(scores - top)
    prob = expo / jnp.sum(expo, axis=-1, keepdims=True)
    prob_low = prob.astype(jnp.bfloat16)
    output = jnp.dot(prob_low, values, preferred_element_type=jnp.float32)
    output = jnp.where(used_flat[:, None], output, 0.0)
    masked = jnp.where(used_flat[:, None], grad_flat, jnp.zeros_like(grad_flat))
    dprob = jnp.dot(masked, values.T, preferred_element_type=jnp.float32)
    grad_value = jnp.dot(prob_low.T, masked, preferred_element_type=jnp.float32)
    delta = jnp.sum(dprob * prob, axis=-1, keepdims=True)
    dscore = (prob * (dprob - delta)).astype(jnp.bfloat16)
    grad_query = jnp.dot(dscore, keys, preferred_element_type=jnp.float32) * scale
    grad_key = jnp.dot(dscore.T, query_flat, preferred_element_type=jnp.float32) * scale
    return (
        output.reshape(length, repeat * head_size),
        grad_query.reshape(length, repeat * head_size),
        grad_key,
        grad_value,
    )


def attend_request(query_rows, own_k, own_v, cart_k, cart_v, used_len, grad_rows, head_size):
    length = query_rows.shape[0]
    cart_rows = cart_k.shape[0]
    groups = cart_k.shape[1] // head_size
    repeat = query_rows.shape[1] // cart_k.shape[1]
    scale = 1.0 / math.sqrt(head_size)
    positions = jnp.arange(length, dtype=jnp.int32)
    causal = (positions[None, :] <= positions[:, None]) & (positions[None, :] < used_len)
    key_seen = jnp.concatenate([jnp.ones((length, cart_rows), dtype=bool), causal], axis=1)
    row_used = positions < used_len
    outputs, grad_qs, grad_ks, grad_vs = ([], [], [], [])
    for group in range(groups):
        qcol = slice(group * repeat * head_size, (group + 1) * repeat * head_size)
        kcol = slice(group * head_size, (group + 1) * head_size)
        keys = jnp.concatenate([cart_k[:, kcol], own_k[:, kcol]], axis=0)
        values = jnp.concatenate([cart_v[:, kcol], own_v[:, kcol]], axis=0)
        output, grad_query, grad_key, grad_value = attend_head(
            query_rows[:, qcol], keys, values, key_seen, row_used, grad_rows[:, qcol], scale
        )
        outputs.append(output)
        grad_qs.append(grad_query)
        grad_ks.append(grad_key[:cart_rows])
        grad_vs.append(grad_value[:cart_rows])
    return (
        jnp.concatenate(outputs, axis=1),
        jnp.concatenate(grad_qs, axis=1),
        jnp.concatenate(grad_ks, axis=1),
        jnp.concatenate(grad_vs, axis=1),
    )


def plan_table(storage, blk_dev, wide_count, capacity):
    requests, selected = storage.shape
    per_owner = requests * capacity
    table = wide_count * per_owner
    owner = storage // blk_dev
    local_row = storage % blk_dev
    positions = jnp.arange(selected, dtype=jnp.int32)
    earlier = (owner[:, :, None] == owner[:, None, :]) & (
        positions[None, None, :] < positions[None, :, None]
    )
    rank = jnp.sum(earlier.astype(jnp.int32), axis=-1)
    slot = owner * per_owner + jnp.arange(requests, dtype=jnp.int32)[:, None] * capacity + rank
    one_hot = (slot[..., None] == jnp.arange(table, dtype=jnp.int32)).astype(jnp.int32)
    ask_rows = jnp.sum(one_hot * local_row[..., None], axis=(0, 1)).reshape(wide_count, per_owner)
    ask_used = jnp.sum(one_hot, axis=(0, 1)).reshape(wide_count, per_owner)
    return (slot, ask_rows, ask_used)


def local(
    queries,
    own_keys,
    own_values,
    cart_keys,
    cart_values,
    block_ids,
    block_home,
    query_len,
    grad_out,
):
    wide_count = lax.axis_size("wide")
    blk_dev = cart_keys.shape[0]
    block_tok = cart_keys.shape[1]
    width = cart_keys.shape[2]
    requests, selected = block_ids.shape
    capacity = max(1, 2 * selected // wide_count)
    all_blocks = block_home.shape[0]
    lookup = block_ids[..., None] == jnp.arange(all_blocks, dtype=jnp.int32)
    storage = jnp.sum(jnp.where(lookup, block_home[None, None, :], 0), axis=-1)
    read_slot, ask_rows, ask_used = plan_table(storage, blk_dev, wide_count, capacity)
    per_owner = ask_rows.shape[1]
    table = wide_count * per_owner
    got_rows, got_used = (
        lax.all_to_all(ask_rows, "wide", split_axis=0, concat_axis=0, tiled=True),
        lax.all_to_all(ask_used, "wide", split_axis=0, concat_axis=0, tiled=True),
    )
    wanted = got_used > 0
    fetch_keys = jnp.where(
        wanted[..., None, None], cart_keys[got_rows], jnp.zeros((), jnp.bfloat16)
    )
    fetch_values = jnp.where(
        wanted[..., None, None], cart_values[got_rows], jnp.zeros((), jnp.bfloat16)
    )
    arrived_keys, arrived_values = (
        lax.all_to_all(fetch_keys, "wide", split_axis=0, concat_axis=0, tiled=True),
        lax.all_to_all(fetch_values, "wide", split_axis=0, concat_axis=0, tiled=True),
    )
    flat_keys = arrived_keys.reshape(table, block_tok, width)
    flat_values = arrived_values.reshape(table, block_tok, width)
    slot_range = jnp.arange(table, dtype=jnp.int32)
    outputs, grad_list = ([], [])
    cart_k = flat_keys[read_slot[0]].reshape(-1, width)
    cart_v = flat_values[read_slot[0]].reshape(-1, width)
    output, grad_query, grad_key, grad_value = attend_request(
        queries[0], own_keys[0], own_values[0], cart_k, cart_v, query_len[0], grad_out[0], HD
    )
    outputs.append(output.astype(jnp.bfloat16))
    grad_list.append(grad_query.astype(jnp.bfloat16))
    placing = (slot_range[:, None] == read_slot[0][None, :]).astype(jnp.float32)
    send_keys = jnp.dot(
        placing, grad_key.reshape(selected, block_tok * width), precision=lax.Precision.HIGHEST
    )
    send_values = jnp.dot(
        placing, grad_value.reshape(selected, block_tok * width), precision=lax.Precision.HIGHEST
    )
    back_keys, back_values = (
        lax.all_to_all(
            send_keys.reshape(wide_count, per_owner, block_tok, width).astype(jnp.bfloat16),
            "wide",
            split_axis=0,
            concat_axis=0,
            tiled=True,
        ).astype(jnp.float32),
        lax.all_to_all(
            send_values.reshape(wide_count, per_owner, block_tok, width).astype(jnp.bfloat16),
            "wide",
            split_axis=0,
            concat_axis=0,
            tiled=True,
        ).astype(jnp.float32),
    )
    back_keys = jnp.where(wanted[..., None, None], back_keys, 0.0).reshape(table, block_tok, width)
    back_values = jnp.where(wanted[..., None, None], back_values, 0.0).reshape(
        table, block_tok, width
    )
    flat_rows = got_rows.reshape(table)
    grad_k_own = jnp.zeros((blk_dev, block_tok, width), jnp.float32).at[flat_rows].add(back_keys)
    grad_v_own = jnp.zeros((blk_dev, block_tok, width), jnp.float32).at[flat_rows].add(back_values)
    squares = jnp.sum(grad_k_own * grad_k_own) + jnp.sum(grad_v_own * grad_v_own)
    total = lax.psum(squares, ("wide", "mp"))
    count = 2.0 * grad_k_own.size * wide_count * lax.axis_size("mp")
    rms = jnp.sqrt(total / count + 1e-06)
    attn_out = jnp.stack(outputs, axis=0)
    grad_queries = jnp.stack(grad_list, axis=0)
    return (attn_out, grad_queries, grad_k_own / rms, grad_v_own / rms)


def solution(mesh):
    placed = (
        P("wide", None, "mp"),
        P("wide", None, "mp"),
        P("wide", None, "mp"),
        P("wide", None, "mp"),
        P("wide", None, "mp"),
        P("wide", None),
        P(),
        P("wide"),
        P("wide", None, "mp"),
    )
    return jax.shard_map(
        local,
        mesh=mesh,
        in_specs=placed,
        out_specs=(
            P("wide", None, "mp"),
            P("wide", None, "mp"),
            P("wide", None, "mp"),
            P("wide", None, "mp"),
        ),
        check_vma=False,
    )
```

profile of v0, /device:TPU:0, one launch (start us, length us, event | category | flops | bytes accessed | tf_op | source)
XLA Modules:
  0.0 304.5 jit_solution(8345033040296486989)
XLA Ops:
  0.6 1.0 select_reduce_fusion
  2.9 8.4 %all-to-all-start.1 = ((s32[32,1,1]{2,1,0:T(1,128)}), s32[32,1,1]{2,1,0:T(1,128)S(1)}, u32[]{:S(2)}, u32[]{:S(2)}) async-start(s32[32,1,1]{2,1,0:T(1,128)} %copy.70), calls=%async_computation.1 | async-start | bytes 32768 | tf_op jit(solution)/shard_map/all_to_all | solution.py:115
  12.0 6.6 %all-to-all-done.1 = s32[32,1,1]{2,1,0:T(1,128)S(1)} async-done(((s32[32,1,1]{2,1,0:T(1,128)}), s32[32,1,1]{2,1,0:T(1,128)S(1)}, u32[]{:S(2)}, u32[]{:S(2)}) %all-to-all-start.1) | async-done | bytes 160 | tf_op jit(solution)/shard_map/all_to_all | solution.py:115
  18.6 3.8 %all-to-all-start = ((s32[32,1,1]{2,1,0:T(1,128)}), s32[32,1,1]{2,1,0:T(1,128)S(1)}, u32[]{:S(2)}, u32[]{:S(2)}) async-start(s32[32,1,1]{2,1,0:T(1,128)} %copy.69), calls=%async_computation | async-start | bytes 32768 | tf_op jit(solution)/shard_map/all_to_all | solution.py:116
  22.5 1.6 fusion.50
  24.8 3.2 %gather_fusion = bf16[32,128,256]{2,1,0:T(8,128)(2,1)} fusion(bf16[16,128,256]{2,1,0:T(8,128)(2,1)} %param.12, s32[1024]{0:T(1024)S(1)} %pad_clamp_fusion.1), kind=kCustom, calls=%fused_computation | custom fusion | bytes 4194432 | tf_op jit(solution)/shard_map/gather | solution.py:120
  28.0 1.7 all-to-all-done
  30.4 4.0 %fusion.14 = (bf16[32,1,128,256]{3,2,1,0:T(8,128)(2,1)}, bf16[32,1,128,256]{3,2,1,0:T(8,128)(2,1)}) fusion(bf16[32,128,256]{2,1,0:T(8,128)(2,1)S(1)} %gather_fusion.2, pred[32]{0:T(512)(128)(4,1)S(1)} %compare_reduce_fusion, bf16[32,128,256]{2,1,0:T(8,128)(2,1)} %gather_fusion), kind=kLoop, calls=%fused_computation.34 | loop fusion | flops 2097152 | bytes 8388640 | tf_op jit(solution)/shard_map/jit(_where)/select_n | solution.py:122
  34.4 5.7 %all-to-all-start.2 = ((bf16[32,1,128,256]{3,2,1,0:T(8,128)(2,1)}), bf16[32,1,128,256]{3,2,1,0:T(8,128)(2,1)S(1)}, u32[]{:S(2)}, u32[]{:S(2)}) async-start(bf16[32,1,128,256]{3,2,1,0:T(8,128)(2,1)} %get-tuple-element.27), calls=%async_computation.2 | async-start | bytes 4194304 | tf_op jit(solution)/shard_map/all_to_all | solution.py:126
  40.8 28.2 %all-to-all-done.2 = bf16[32,1,128,256]{3,2,1,0:T(8,128)(2,1)S(1)} async-done(((bf16[32,1,128,256]{3,2,1,0:T(8,128)(2,1)}), bf16[32,1,128,256]{3,2,1,0:T(8,128)(2,1)S(1)}, u32[]{:S(2)}, u32[]{:S(2)}) %all-to-all-start.2) | async-done | bytes 2097184 | tf_op jit(solution)/shard_map/all_to_all | solution.py:126
  69.0 5.2 %all-to-all-start.3 = ((bf16[32,1,128,256]{3,2,1,0:T(8,128)(2,1)}), bf16[32,1,128,256]{3,2,1,0:T(8,128)(2,1)}, u32[]{:S(2)}, u32[]{:S(2)}) async-start(bf16[32,1,128,256]{3,2,1,0:T(8,128)(2,1)} %get-tuple-element.26), calls=%async_computation.3 | async-start | bytes 4194304 | tf_op jit(solution)/shard_map/all_to_all | solution.py:127
  74.2 1.1 broadcast_bitcast_fusion
  75.3 2.4 copy.72
  77.9 1.2 fusion.53
  79.0 0.8 reshape.626
  80.9 0.8 reshape.625
  82.4 1.4 fusion.56
  83.8 1.4 fusion.55
  85.2 2.2 gather_fusion.1
  87.4 1.0 fusion.52
  88.4 14.7 %all-to-all-done.3 = bf16[32,1,128,256]{3,2,1,0:T(8,128)(2,1)} async-done(((bf16[32,1,128,256]{3,2,1,0:T(8,128)(2,1)}), bf16[32,1,128,256]{3,2,1,0:T(8,128)(2,1)}, u32[]{:S(2)}, u32[]{:S(2)}) %all-to-all-start.3) | async-done | bytes 2097184 | tf_op jit(solution)/shard_map/all_to_all | solution.py:127
  103.1 2.2 gather_fusion.3
  105.4 1.0 copy-done.10
  106.4 2.5 fusion.57
  108.9 1.2 fusion.3
  110.2 2.0 multiply_reduce_fusion
  112.2 5.2 %multiply_convert_fusion = (bf16[1024,2176]{0,1:T(8,128)(2,1)}, bf16[1024,2176]{0,1:T(8,128)(2,1)}) fusion(f32[1024,2176]{0,1:T(8,128)S(1)} %get-tuple-element.33, f32[1024]{0:T(1024)S(1)} %get-tuple-element.32, f32[1024]{0:T(1024)S(1)} %fusion.3, f32[1024,2176]{0,1:T(8,128)S(1)} %get-tuple-element.31, f32[1024]{0:T(1024)S(1)} %get-tuple-element.30), kind=kLoop, calls=%fused_computation.8 | loop fusion | flops 13369344 | bytes 26750976 | tf_op jit(solution)/shard_map/convert_element_type | solution.py:31
  117.4 4.8 %fusion.4 = f32[2048,128]{0,1:T(8,128)} fusion(bf16[1024,2176]{0,1:T(8,128)(2,1)} %get-tuple-element.11, bf16[1024,128]{1,0:T(8,128)(2,1)S(1)} %copy-done.21, pred[1024]{0:T(1024)(128)(4,1)S(1)} %broadcast_in_dim.114), kind=kOutput, calls=%fused_computation.19 | convolution fusion | flops 537001984 | bytes 5506048 | tf_op jit(solution)/shard_map/dot_general | solution.py:29
  122.2 1.7 fusion.58
  123.9 1.2 fusion.1
  125.2 2.0 multiply_reduce_fusion.1
  127.2 4.4 %multiply_convert_fusion.1 = (bf16[1024,2176]{0,1:T(8,128)(2,1)}, bf16[1024,2176]{0,1:T(8,128)(2,1)S(1)}) fusion(f32[1024,2176]{0,1:T(8,128)S(1)} %get-tuple-element.37, f32[1024]{0:T(1024)S(1)} %get-tuple-element.36, f32[1024]{0:T(1024)S(1)} %fusion.1, f32[1024,2176]{0,1:T(8,128)S(1)} %get-tuple-element.35, f32[1024]{0:T(1024)S(1)} %get-tuple-element.34), kind=kLoop, calls=%fused_computation.10 | loop fusion | flops 13369344 | bytes 26750976 | tf_op jit(solution)/shard_map/convert_element_type | solution.py:31
  131.6 2.0 copy-done.4
  133.6 1.6 fusion.6
  135.3 1.8 copy.83
  137.1 1.7 reshape.629
  138.9 2.3 convert_bitcast_fusion
  141.2 2.5 copy.85
  143.7 4.4 %all-to-all-start.5 = ((bf16[32,1,128,256]{3,2,1,0:T(8,128)(2,1)}), bf16[32,1,128,256]{3,2,1,0:T(8,128)(2,1)S(1)}, u32[]{:S(2)}, u32[]{:S(2)}) async-start(bf16[32,1,128,256]{3,2,1,0:T(8,128)(2,1)} %copy.85), calls=%async_computation.5 | async-start | bytes 4194304 | tf_op jit(solution)/shard_map/all_to_all | solution.py:155
  148.1 3.8 %fusion.60 = f32[2176,128]{0,1:T(8,128)S(1)} fusion(bf16[1024,2176]{0,1:T(8,128)(2,1)} %get-tuple-element.10, bf16[1024,128]{1,0:T(8,128)(2,1)S(1)} %copy-done.6), kind=kOutput, calls=%fused_computation.122 | convolution fusion | flops 570425344 | bytes 5832704 | tf_op jit(solution)/shard_map/dot_general | solution.py:33
  151.9 1.4 fusion.59
  153.6 1.5 pad_maximum_fusion
  155.1 2.9 copy.79
  158.0 2.7 reshape.627
  160.7 3.5 %convert_bitcast_fusion.1 = bf16[32,1,128,256]{3,0,2,1:T(8,128)(2,1)S(1)} fusion(f32[2,128,8,256]{3,2,1,0:T(8,128)} %bitcast.93, s32[16]{0:T(128)S(1)} %add.101), kind=kOutput, calls=%fused_computation.40 | convolution fusion | flops 202375680 | bytes 4194368 | tf_op jit(solution)/shard_map/dot_general | solution.py:141
  164.2 2.5 copy.81
  166.8 10.0 %all-to-all-done.5 = bf16[32,1,128,256]{3,2,1,0:T(8,128)(2,1)S(1)} async-done(((bf16[32,1,128,256]{3,2,1,0:T(8,128)(2,1)}), bf16[32,1,128,256]{3,2,1,0:T(8,128)(2,1)S(1)}, u32[]{:S(2)}, u32[]{:S(2)}) %all-to-all-start.5) | async-done | bytes 2097184 | tf_op jit(solution)/shard_map/all_to_all | solution.py:155
  176.7 4.8 %all-to-all-start.4 = ((bf16[32,1,128,256]{3,2,1,0:T(8,128)(2,1)}), bf16[32,1,128,256]{3,2,1,0:T(8,128)(2,1)}, u32[]{:S(2)}, u32[]{:S(2)}) async-start(bf16[32,1,128,256]{3,2,1,0:T(8,128)(2,1)} %copy.81), calls=%async_computation.4 | async-start | bytes 4194304 | tf_op jit(solution)/shard_map/all_to_all | solution.py:148
  181.6 3.7 %fusion.21 = bf16[1024,128]{1,0:T(8,128)(2,1)S(1)} fusion(bf16[1024,2176]{0,1:T(8,128)(2,1)} %get-tuple-element.11, bf16[128,128]{1,0:T(8,128)(2,1)S(1)} %copy-done.25, bf16[2048,128]{1,0:T(8,128)(2,1)S(1)} %copy-done.19, pred[1024]{0:T(1024)(128)(4,1)S(1)} %broadcast_in_dim.114), kind=kOutput, calls=%fused_computation.46 | convolution fusion | flops 571801600 | bytes 5276672 | tf_op jit(solution)/shard_map/dot_general | solution.py:25
  185.3 0.8 concatenate.57
  186.1 3.7 %fusion.20 = bf16[1024,128]{1,0:T(8,128)(2,1)S(1)} fusion(bf16[1024,2176]{0,1:T(8,128)(2,1)} %copy-done.4, bf16[128,128]{1,0:T(8,128)(2,1)S(1)} %copy-done.24, bf16[2048,128]{1,0:T(8,128)(2,1)S(1)} %copy-done.17, pred[1024]{0:T(1024)(128)(4,1)S(1)} %broadcast_in_dim.114), kind=kOutput, calls=%fused_computation.45 | convolution fusion | flops 571801600 | bytes 5276672 | tf_op jit(solution)/shard_map/dot_general | solution.py:25
  189.8 0.8 concatenate.54
  190.6 3.7 %fusion.23 = bf16[1024,128]{1,0:T(8,128)(2,1)S(1)} fusion(bf16[1024,2176]{0,1:T(8,128)(2,1)} %get-tuple-element.10, bf16[128,128]{1,0:T(8,128)(2,1)S(1)} %copy-done.23, bf16[2048,128]{1,0:T(8,128)(2,1)S(1)} %copy-done.11), kind=kOutput, calls=%fused_computation.48 | convolution fusion | flops 571801600 | bytes 5275648 | tf_op jit(solution)/shard_map/dot_general | solution.py:32
  194.5 3.6 %fusion.22 = bf16[1024,128]{1,0:T(8,128)(2,1)S(1)} fusion(bf16[1024,2176]{0,1:T(8,128)(2,1)} %get-tuple-element.8, bf16[128,128]{1,0:T(8,128)(2,1)S(1)} %copy-done.22, bf16[2048,128]{1,0:T(8,128)(2,1)S(1)} %copy-done.9), kind=kOutput, calls=%fused_computation.47 | convolution fusion | flops 571801600 | bytes 5275648 | tf_op jit(solution)/shard_map/dot_general | solution.py:32
  198.2 12.1 %all-to-all-done.4 = bf16[32,1,128,256]{3,2,1,0:T(8,128)(2,1)} async-done(((bf16[32,1,128,256]{3,2,1,0:T(8,128)(2,1)}), bf16[32,1,128,256]{3,2,1,0:T(8,128)(2,1)}, u32[]{:S(2)}, u32[]{:S(2)}) %all-to-all-start.4) | async-done | bytes 2097184 | tf_op jit(solution)/shard_map/all_to_all | solution.py:148
  210.4 6.0 %select_bitcast_fusion = (f32[32,128,256]{2,1,0:T(8,128)}, f32[32,128,256]{2,1,0:T(8,128)}) fusion(bf16[32,1,128,256]{3,2,1,0:T(8,128)(2,1)S(1)} %all-to-all-done.5, pred[32]{0:T(512)(128)(4,1)S(1)} %compare_reduce_fusion, bf16[32,1,128,256]{3,2,1,0:T(8,128)(2,1)} %all-to-all-done.4), kind=kLoop, calls=%fused_computation.23 | loop fusion | flops 4194304 | bytes 12582944 | tf_op jit(solution)/shard_map/reshape | solution.py:164
  216.6 6.4 %scatter_fusion = f32[16,128,256]{2,1,0:T(8,128)S(1)} fusion(f32[16,128,256]{2,1,0:T(8,128)S(1)} %broadcast.507.clone, s32[32]{0:T(128)S(1)} %fusion.35, f32[32,128,256]{2,1,0:T(8,128)} %get-tuple-element.25), kind=kCustom, calls=%fused_computation.4 | custom fusion | flops 1048576 | bytes 12583040 | tf_op jit(solution)/shard_map/scatter-add | solution.py:168
  223.0 1.2 multiply_reduce_fusion.3
  224.6 6.4 %scatter_fusion.1 = f32[16,128,256]{2,1,0:T(8,128)S(1)} fusion(f32[16,128,256]{2,1,0:T(8,128)S(1)} %broadcast.507.clone.1, s32[32]{0:T(128)S(1)} %fusion.35, f32[32,128,256]{2,1,0:T(8,128)} %get-tuple-element.24), kind=kCustom, calls=%fused_computation.5 | custom fusion | flops 1048576 | bytes 12583040 | tf_op jit(solution)/shard_map/scatter-add | solution.py:169
  231.0 1.1 multiply_reduce_fusion.2
  233.4 1.1 pad_maximum_fusion.6
  234.5 64.3 %psum.7 = f32[]{:T(128)} all-reduce(f32[]{:T(128)S(6)} %add.107), channel_id=1, replica_groups=mesh['wide'=32,'mp'=4] {'wide','mp'}, use_global_device_ids=true, to_apply=%region_14.15 | all-reduce | flops 1 | bytes 8 | tf_op jit(solution)/shard_map/psum | solution.py:171
  299.5 3.2 %broadcast_divide_fusion.1 = f32[16,128,256]{2,1,0:T(8,128)} fusion(f32[16,128,256]{2,1,0:T(8,128)} %copy-done.2, f32[]{:T(128)S(6)} %sqrt.3), kind=kLoop, calls=%fused_computation.52 | loop fusion | flops 524288 | bytes 4194308 | tf_op jit(solution)/shard_map/div | solution.py:176
  302.7 1.6 broadcast_divide_fusion
  (88 shorter events, 6.5 us)
Async XLA Ops:
  0.6 23.5 %copy-start = (bf16[16,128,256]{2,1,0:T(8,128)(2,1)S(1)}, bf16[16,128,256]{2,1,0:T(8,128)(2,1)}, u32[]{:S(2)}) copy-start(bf16[16,128,256]{2,1,0:T(8,128)(2,1)} %param.13) | copy-start | bytes 3145732
  1.6 0.5 copy-start.27
  1.8 1.1 copy-start.28
  2.9 15.7 %all-to-all-start.1 = ((s32[32,1,1]{2,1,0:T(1,128)}), s32[32,1,1]{2,1,0:T(1,128)S(1)}, u32[]{:S(2)}, u32[]{:S(2)}) async-start(s32[32,1,1]{2,1,0:T(1,128)} %copy.70), calls=%async_computation.1 | async-start | bytes 32768 | tf_op jit(solution)/shard_map/all_to_all | solution.py:115
  18.6 11.1 %all-to-all-start = ((s32[32,1,1]{2,1,0:T(1,128)}), s32[32,1,1]{2,1,0:T(1,128)S(1)}, u32[]{:S(2)}, u32[]{:S(2)}) async-start(s32[32,1,1]{2,1,0:T(1,128)} %copy.69), calls=%async_computation | async-start | bytes 32768 | tf_op jit(solution)/shard_map/all_to_all | solution.py:116
  34.4 34.6 %all-to-all-start.2 = ((bf16[32,1,128,256]{3,2,1,0:T(8,128)(2,1)}), bf16[32,1,128,256]{3,2,1,0:T(8,128)(2,1)S(1)}, u32[]{:S(2)}, u32[]{:S(2)}) async-start(bf16[32,1,128,256]{3,2,1,0:T(8,128)(2,1)} %get-tuple-element.27), calls=%async_computation.2 | async-start | bytes 4194304 | tf_op jit(solution)/shard_map/all_to_all | solution.py:126
  69.0 5.2 %copy-start.3 = (bf16[32,1,128,256]{3,2,1,0:T(8,128)(2,1)}, bf16[32,1,128,256]{3,2,1,0:T(8,128)(2,1)S(1)}, u32[]{:S(2)}) copy-start(bf16[32,1,128,256]{3,2,1,0:T(8,128)(2,1)S(1)} %all-to-all-done.2) | copy-start | bytes 6291460
  69.0 34.1 %all-to-all-start.3 = ((bf16[32,1,128,256]{3,2,1,0:T(8,128)(2,1)}), bf16[32,1,128,256]{3,2,1,0:T(8,128)(2,1)}, u32[]{:S(2)}, u32[]{:S(2)}) async-start(bf16[32,1,128,256]{3,2,1,0:T(8,128)(2,1)} %get-tuple-element.26), calls=%async_computation.3 | async-start | bytes 4194304 | tf_op jit(solution)/shard_map/all_to_all | solution.py:127
  75.3 2.4 copy-start.15
  77.9 27.5 %copy-start.5 = (bf16[1024,128]{1,0:T(8,128)(2,1)}, bf16[1024,128]{1,0:T(8,128)(2,1)S(1)}, u32[]{:S(2)}) copy-start(bf16[1024,128]{1,0:T(8,128)(2,1)S(1)} %reshape.624) | copy-start | bytes 786436
  105.3 1.2 copy-start.10
  105.4 4.8 %copy-start.18 = (bf16[2048,128]{1,0:T(8,128)(2,1)}, bf16[2048,128]{1,0:T(8,128)(2,1)S(1)}, u32[]{:S(2)}) copy-start(bf16[2048,128]{1,0:T(8,128)(2,1)S(1)} %get-tuple-element.13) | copy-start | bytes 1572868
  105.4 19.8 %copy-start.16 = (bf16[2048,128]{1,0:T(8,128)(2,1)}, bf16[2048,128]{1,0:T(8,128)(2,1)S(1)}, u32[]{:S(2)}) copy-start(bf16[2048,128]{1,0:T(8,128)(2,1)S(1)} %get-tuple-element.12) | copy-start | bytes 1572868
  108.9 1.3 copy-start.21
  108.9 1.3 copy-start.25
  117.3 4.9 %copy-start.7 = (bf16[1024,128]{1,0:T(8,128)(2,1)S(1)}, bf16[1024,128]{1,0:T(8,128)(2,1)}, u32[]{:S(2)}) copy-start(bf16[1024,128]{1,0:T(8,128)(2,1)} %reshape.621) | copy-start | bytes 786436
  117.3 4.8 %copy-start.8 = (bf16[2048,128]{1,0:T(8,128)(2,1)S(1)}, bf16[2048,128]{1,0:T(8,128)(2,1)}, u32[]{:S(2)}) copy-start(bf16[2048,128]{1,0:T(8,128)(2,1)} %get-tuple-element.14) | copy-start | bytes 1572868
  117.4 4.8 %copy-start.22 = (bf16[128,128]{1,0:T(8,128)(2,1)S(1)}, bf16[128,128]{1,0:T(8,128)(2,1)}, u32[]{:S(2)}) copy-start(bf16[128,128]{1,0:T(8,128)(2,1)} %get-tuple-element.22) | copy-start | bytes 98308
  123.9 1.3 copy-start.20
  123.9 1.3 copy-start.24
  131.5 2.0 copy-start.4
  133.6 1.6 copy-start.12
  143.7 4.4 %copy-start.6 = (bf16[1024,128]{1,0:T(8,128)(2,1)S(1)}, bf16[1024,128]{1,0:T(8,128)(2,1)}, u32[]{:S(2)}) copy-start(bf16[1024,128]{1,0:T(8,128)(2,1)} %copy-done.5) | copy-start | bytes 786436
  143.7 8.2 %slice-start = ((s8[4456448]{0:T(1024)(128)(4,1)}), s8[262144]{0:T(1024)(128)(4,1)S(1)}, s32[]{:S(2)}) async-start(s8[4456448]{0:T(1024)(128)(4,1)} %bitcast.91), calls=%async_computation.6 | async-start | bytes 524288
  143.7 33.0 %all-to-all-start.5 = ((bf16[32,1,128,256]{3,2,1,0:T(8,128)(2,1)}), bf16[32,1,128,256]{3,2,1,0:T(8,128)(2,1)S(1)}, u32[]{:S(2)}, u32[]{:S(2)}) async-start(bf16[32,1,128,256]{3,2,1,0:T(8,128)(2,1)} %copy.85), calls=%async_computation.5 | async-start | bytes 4194304 | tf_op jit(solution)/shard_map/all_to_all | solution.py:155
  148.0 3.9 %slice-start.1 = ((s8[4456448]{0:T(1024)(128)(4,1)}), s8[4194304]{0:T(1024)(128)(4,1)S(1)}, s32[]{:S(2)}) async-start(s8[4456448]{0:T(1024)(128)(4,1)} %bitcast.91), calls=%async_computation.7 | async-start | bytes 8388608
  166.8 14.8 %copy-start.26 = (s32[32]{0:T(128)S(1)}, s32[32]{0:T(128)}, u32[]{:S(2)}) copy-start(s32[32]{0:T(128)} %get-tuple-element.4) | copy-start | bytes 388
  166.8 14.8 %copy-start.19 = (bf16[2048,128]{1,0:T(8,128)(2,1)S(1)}, bf16[2048,128]{1,0:T(8,128)(2,1)}, u32[]{:S(2)}) copy-start(bf16[2048,128]{1,0:T(8,128)(2,1)} %copy-done.18) | copy-start | bytes 1572868
  176.7 33.7 %all-to-all-start.4 = ((bf16[32,1,128,256]{3,2,1,0:T(8,128)(2,1)}), bf16[32,1,128,256]{3,2,1,0:T(8,128)(2,1)}, u32[]{:S(2)}, u32[]{:S(2)}) async-start(bf16[32,1,128,256]{3,2,1,0:T(8,128)(2,1)} %copy.81), calls=%async_computation.4 | async-start | bytes 4194304 | tf_op jit(solution)/shard_map/all_to_all | solution.py:148
  181.5 4.6 %copy-start.17 = (bf16[2048,128]{1,0:T(8,128)(2,1)S(1)}, bf16[2048,128]{1,0:T(8,128)(2,1)}, u32[]{:S(2)}) copy-start(bf16[2048,128]{1,0:T(8,128)(2,1)} %copy-done.16) | copy-start | bytes 1572868
  186.1 4.5 %copy-start.11 = (bf16[2048,128]{1,0:T(8,128)(2,1)S(1)}, bf16[2048,128]{1,0:T(8,128)(2,1)}, u32[]{:S(2)}) copy-start(bf16[2048,128]{1,0:T(8,128)(2,1)} %get-tuple-element.15) | copy-start | bytes 1572868
  186.1 4.5 %copy-start.23 = (bf16[128,128]{1,0:T(8,128)(2,1)S(1)}, bf16[128,128]{1,0:T(8,128)(2,1)}, u32[]{:S(2)}) copy-start(bf16[128,128]{1,0:T(8,128)(2,1)} %get-tuple-element.23) | copy-start | bytes 98308
  190.6 3.8 %copy-start.9 = (bf16[2048,128]{1,0:T(8,128)(2,1)S(1)}, bf16[2048,128]{1,0:T(8,128)(2,1)}, u32[]{:S(2)}) copy-start(bf16[2048,128]{1,0:T(8,128)(2,1)} %get-tuple-element.14) | copy-start | bytes 1572868
  223.0 1.3 copy-start.2
  231.0 2.5 copy-start.13
  231.0 2.5 copy-start.14
  299.4 4.8 %copy-start.1 = (bf16[16,128,256]{2,1,0:T(8,128)(2,1)S(1)}, bf16[16,128,256]{2,1,0:T(8,128)(2,1)}, u32[]{:S(2)}) copy-start(bf16[16,128,256]{2,1,0:T(8,128)(2,1)} %param.13) | copy-start | bytes 3145732
where the time goes:
time: 310 us; the launch traced here: 305 us
  waiting for transfers between devices  73.2 us (24%)
  blocking collectives  64.3 us (21%)
  other arithmetic  49.1 us (16%)
  local copies, waits for them, and re-layouts  41.2 us (13%)
  matrix products  40.3 us (13%)
  starting transfers between devices  32.3 us (10%)
  between operations  4.18 us (1%)
    psum x1, blocking collectives, local(): total = lax.psum(squares, ('wide', 'mp'))  64.3 us
    all_to_all x1, waiting for transfers between devices, local(): lax.all_to_all(fetch_keys, 'wide', split_axis=0, concat_axis=0, tiled=True)  28.2 us
    all_to_all x1, waiting for transfers between devices, local(): lax.all_to_all(fetch_values, 'wide', split_axis=0, concat_axis=0, tiled=T...  14.7 us
    scatter-add x2, other arithmetic, local(): jnp.zeros((blk_dev, block_tok, width), jnp.float32).at[flat_rows]  12.8 us
    all_to_all x1, waiting for transfers between devices, local(): lax.all_to_all(send_keys.reshape(wide_count, per_owner, block_tok, width)...  12.1 us
    all_to_all x1, waiting for transfers between devices, local(): lax.all_to_all(send_values.reshape(wide_count, per_owner, block_tok, widt...  9.96 us
    convert_element_type x2, other arithmetic, attend_head(): dscore = (prob * (dprob - delta)).astype(jnp.bfloat16)  9.54 us
    all_to_all x1, starting transfers between devices, local(): lax.all_to_all(ask_rows, 'wide', split_axis=0, concat_axis=0, tiled=True)  8.42 us
  transfers between devices with their start and end apart: 6, of which 6 were waited for; matrix products, arithmetic and copies ran while one was open for 18% of the time, Pallas kernels for 0%

commit v1 on v0

v1 whole, which is shorter than its diff:
```python
import functools
import math

import jax
import jax.numpy as jnp
from jax import lax
from jax.experimental import pallas as pl
from jax.experimental.pallas import tpu as pltpu
from jax.sharding import PartitionSpec as P

HD = 128
SLICE = 16
HEADS = 2
KINDS = 2
MIB = 1024 * 1024


def nt(a, b):
    return lax.dot_general(a, b, (((1,), (1,)), ((), ())), preferred_element_type=jnp.float32)


def nn(a, b):
    return jnp.dot(a, b, preferred_element_type=jnp.float32)


def split_kernel(keys_ref, values_ref, tag_ref, out_ref, sems):
    blocks = keys_ref.shape[0]
    copies = []
    for m in range(out_ref.shape[0]):
        t, h, kind = m // 4, (m // 2) % 2, m % 2
        src = (keys_ref, values_ref)[kind]
        copies.append(
            pltpu.make_async_copy(
                src.at[:, pl.ds(t * SLICE, SLICE), pl.ds(h * HD, HD)],
                out_ref.at[m, pl.ds(0, blocks)],
                sems.at[2 * m],
            )
        )
        copies.append(
            pltpu.make_async_copy(tag_ref, out_ref.at[m, pl.ds(blocks, 1)], sems.at[2 * m + 1])
        )
    for copy in copies:
        copy.start()
    for copy in copies:
        copy.wait()


def split(cart_keys, cart_values, tag, count):
    blocks = cart_keys.shape[0]
    return pl.pallas_call(
        split_kernel,
        out_shape=jax.ShapeDtypeStruct((count, blocks + 1, SLICE, HD), jnp.bfloat16),
        in_specs=[pl.BlockSpec(memory_space=pl.ANY)] * 3,
        out_specs=pl.BlockSpec(memory_space=pl.ANY),
        scratch_shapes=[pltpu.SemaphoreType.DMA((2 * count,))],
        name="split_blocks",
    )(cart_keys, cart_values, tag)


def pick_kernel(index_ref, held_ref, out_ref):
    def step(n, carry):
        for u in range(8):
            out_ref[n * 8 + u] = held_ref[index_ref[n * 8 + u]]
        return carry

    lax.fori_loop(0, out_ref.shape[0] // 8, step, 0)


def pick(index, held):
    return pl.pallas_call(
        pick_kernel,
        out_shape=jax.ShapeDtypeStruct((index.shape[0],) + held.shape[1:], jnp.bfloat16),
        in_specs=[
            pl.BlockSpec(memory_space=pltpu.SMEM),
            pl.BlockSpec(memory_space=pltpu.VMEM),
        ],
        out_specs=pl.BlockSpec(memory_space=pltpu.VMEM),
        compiler_params=pltpu.CompilerParams(vmem_limit_bytes=16 * MIB),
        name="pick_requested",
    )(index, held)


def attend_kernel(
    length_ref,
    kv_ref,
    q_ref,
    qt_ref,
    gt_ref,
    own_k_ref,
    own_v_ref,
    out_ref,
    grad_q_ref,
    send_ref,
    score,
    expo,
    acc,
):
    used = length_ref[0]
    chunks = kv_ref.shape[0] // (HEADS * KINDS)
    chunk = kv_ref.shape[1]
    rows = q_ref.shape[1]
    queries = out_ref.shape[0]
    repeat = rows // queries
    own = own_k_ref.shape[0]
    scale = 1.0 / math.sqrt(HD)
    log2e = scale * math.log2(math.e)
    position = lax.rem(lax.broadcasted_iota(jnp.int32, (1, rows), 1), queries)
    row_used = position < used
    own_at = lax.broadcasted_iota(jnp.int32, (own, rows), 0)
    seen = (own_at <= position) & (own_at < used)
    for head in range(HEADS):
        lanes = slice(head * HD, (head + 1) * HD)
        own_k = own_k_ref[:, lanes]
        own_v = own_v_ref[:, lanes]
        qt = qt_ref[head]
        gt = gt_ref[head]
        at = lambda c, kind: (c * HEADS + head) * KINDS + kind
        own_s = jnp.where(seen, nn(own_k, qt), -1e30)
        top = jnp.max(own_s.reshape(own // 8, 8, rows), axis=0)
        for c in range(chunks):
            s = nn(kv_ref[at(c, 0)], qt)
            score[c] = s
            top = jnp.maximum(top, jnp.max(s.reshape(chunk // 8, 8, rows), axis=0))
        top = jnp.max(top, axis=0, keepdims=True) * log2e
        e = jnp.exp2(own_s * log2e - top)
        total = jnp.sum(e.reshape(own // 8, 8, rows), axis=0)
        own_e = e.astype(jnp.bfloat16)
        acc[...] = nn(own_v.T, own_e)
        for c in range(chunks):
            e = jnp.exp2(score[c] * log2e - top)
            total = total + jnp.sum(e.reshape(chunk // 8, 8, rows), axis=0)
            low = e.astype(jnp.bfloat16)
            expo[c] = low
            acc[...] += nn(kv_ref[at(c, 1)].T, low)
        inv = 1.0 / jnp.sum(total, axis=0, keepdims=True)
        gt32 = jnp.where(row_used, gt.astype(jnp.float32), 0.0)
        out = jnp.where(row_used, acc[...] * inv, 0.0)
        for r in range(repeat):
            cols = slice((head * repeat + r) * HD, (head * repeat + r + 1) * HD)
            out_ref[:, cols] = out[:, r * queries : (r + 1) * queries].T.astype(jnp.bfloat16)
        delta = jnp.sum(gt32 * out, axis=0, keepdims=True) * inv
        gs = (gt32 * inv).astype(jnp.bfloat16)
        ds = (own_e.astype(jnp.float32) * (nn(own_v, gs) - delta)).astype(jnp.bfloat16)
        acc[...] = nn(own_k.T, ds)
        for c in range(chunks):
            low = expo[c]
            send_ref[at(c, 1)] = nt(low, gs).astype(jnp.bfloat16)
            dp = nn(kv_ref[at(c, 1)], gs)
            ds = (low.astype(jnp.float32) * (dp - delta)).astype(jnp.bfloat16)
            send_ref[at(c, 0)] = (nn(ds, q_ref[head]) * scale).astype(jnp.bfloat16)
            acc[...] += nn(kv_ref[at(c, 0)].T, ds)
        grad = acc[...] * scale
        for r in range(repeat):
            cols = slice((head * repeat + r) * HD, (head * repeat + r + 1) * HD)
            grad_q_ref[:, cols] = grad[:, r * queries : (r + 1) * queries].T.astype(jnp.bfloat16)


def attend(length, kv, q, qt, gt, own_k, own_v, queries, width):
    count, chunk, _ = kv.shape
    rows = q.shape[1]
    chunks = count // (HEADS * KINDS)
    vmem = pl.BlockSpec(memory_space=pltpu.VMEM)
    return pl.pallas_call(
        attend_kernel,
        out_shape=(
            jax.ShapeDtypeStruct((queries, width), jnp.bfloat16),
            jax.ShapeDtypeStruct((queries, width), jnp.bfloat16),
            jax.ShapeDtypeStruct(kv.shape, jnp.bfloat16),
        ),
        in_specs=[pl.BlockSpec(memory_space=pltpu.SMEM)] + [vmem] * 6,
        out_specs=(vmem, vmem, vmem),
        scratch_shapes=[
            pltpu.VMEM((chunks, chunk, rows), jnp.float32),
            pltpu.VMEM((chunks, chunk, rows), jnp.bfloat16),
            pltpu.VMEM((HD, rows), jnp.float32),
        ],
        compiler_params=pltpu.CompilerParams(vmem_limit_bytes=48 * MIB),
        cost_estimate=pl.CostEstimate(
            flops=12 * 2 * HD * rows * (chunks * chunk + queries),
            bytes_accessed=8 * MIB,
            transcendentals=HEADS * rows * chunks * chunk,
        ),
        name="attend_forward_backward",
    )(length, kv, q, qt, gt, own_k, own_v)


def add_kernel(index_ref, got_ref, out_ref, square_ref, table):
    table[...] = jnp.zeros_like(table)

    def step(n, carry):
        for u in range(4):
            at = index_ref[n * 4 + u]
            table[at] += got_ref[n * 4 + u].astype(jnp.float32)
        return carry

    lax.fori_loop(0, got_ref.shape[0] // 4, step, 0)

    def finish(n, squares):
        rows = table[pl.ds(n * 8, 8)]
        out_ref[pl.ds(n * 8, 8)] = rows.astype(jnp.bfloat16)
        return squares + jnp.sum((rows * rows).reshape(8 * SLICE // 8, 8, HD), axis=0)

    square_ref[...] = lax.fori_loop(
        0, table.shape[0] // 8, finish, jnp.zeros(square_ref.shape, jnp.float32)
    )


def add_up(index, got, blocks):
    vmem = pl.BlockSpec(memory_space=pltpu.VMEM)
    return pl.pallas_call(
        add_kernel,
        out_shape=(
            jax.ShapeDtypeStruct((blocks, SLICE, HD), jnp.bfloat16),
            jax.ShapeDtypeStruct((8, HD), jnp.float32),
        ),
        in_specs=[pl.BlockSpec(memory_space=pltpu.SMEM), vmem],
        out_specs=(vmem, vmem),
        scratch_shapes=[pltpu.VMEM((blocks, SLICE, HD), jnp.float32)],
        compiler_params=pltpu.CompilerParams(vmem_limit_bytes=24 * MIB),
        name="add_over_readers",
    )(index, got)


def finish_kernel(count, square_ref, got_ref, key_ref, value_ref):
    total = jnp.sum(square_ref[...], axis=(0, 1), keepdims=True)
    inv = 1.0 / jnp.sqrt(total / count + 1e-6)
    for m in range(got_ref.shape[0]):
        t, h, kind = m // 4, (m // 2) % 2, m % 2
        dst = (key_ref, value_ref)[kind]
        part = got_ref[m].astype(jnp.float32) * inv.reshape(1, 1, 1)
        dst[:, t * SLICE : (t + 1) * SLICE, h * HD : (h + 1) * HD] = part


def finish(squares, got, block_tok, width, count):
    slices, blocks, _, _ = got.shape
    step = 4
    shape = jax.ShapeDtypeStruct((blocks, block_tok, width), jnp.float32)
    spec = pl.BlockSpec((step, block_tok, width), lambda n: (n, 0, 0))
    return pl.pallas_call(
        functools.partial(finish_kernel, count),
        out_shape=(shape, shape),
        grid=(blocks // step,),
        in_specs=[
            pl.BlockSpec((8, HD), lambda n: (0, 0)),
            pl.BlockSpec((slices, step, SLICE, HD), lambda n: (0, n, 0, 0)),
        ],
        out_specs=(spec, spec),
        compiler_params=pltpu.CompilerParams(vmem_limit_bytes=24 * MIB),
        name="normalize_updates",
    )(squares, got)


def wide_pairs(dy, dz, dc):
    pairs = []
    for y in range(4):
        for z in range(4):
            for c in range(2):
                to = (((y + dy) % 4) * 4 + (z + dz) % 4) * 2 + (c ^ dc)
                pairs.append(((y * 4 + z) * 2 + c, to))
    return pairs


def total_over_mesh(a):
    a = a + lax.ppermute(a, "wide", wide_pairs(0, 0, 1))
    a = a + sum(lax.ppermute(a, "mp", [(i, (i + d) % 4) for i in range(4)]) for d in (1, 2, 3))
    a = a + sum(lax.ppermute(a, "wide", wide_pairs(0, d, 0)) for d in (1, 2, 3))
    a = a + sum(lax.ppermute(a, "wide", wide_pairs(d, 0, 0)) for d in (1, 2, 3))
    return a


def swap(a):
    return lax.all_to_all(a, "wide", split_axis=0, concat_axis=0, tiled=True)


def heads_first(a, rows):
    length = a.shape[0]
    return a.reshape(length, HEADS, rows // length, HD).transpose(1, 2, 0, 3).reshape(HEADS, rows, HD)


def local(
    queries,
    own_keys,
    own_values,
    cart_keys,
    cart_values,
    block_ids,
    block_home,
    query_len,
    grad_out,
):
    wide_count = lax.axis_size("wide")
    blk_dev, block_tok, width = cart_keys.shape
    selected = block_ids.shape[1]
    all_blocks = block_home.shape[0]
    length = queries.shape[1]
    rows = length * queries.shape[2] // width
    lookup = block_ids[0][:, None] == jnp.arange(all_blocks, dtype=jnp.int32)
    storage = jnp.sum(jnp.where(lookup, block_home[None, :], 0), axis=-1)
    tag = jnp.stack([storage // blk_dev, storage % blk_dev]).astype(jnp.bfloat16)
    tag = jnp.pad(tag, ((0, SLICE - 2), (0, HD - selected)))[None]
    held = swap(split(cart_keys, cart_values, tag, wide_count))
    asked = held[:, blk_dev, :2, :selected].astype(jnp.int32)
    owner, row = asked[:, 0].reshape(-1), asked[:, 1].reshape(-1)
    picked = pick(
        owner * (blk_dev + 1) + row, held.reshape(wide_count * (blk_dev + 1), SLICE, HD)
    )
    kv = swap(picked.reshape(wide_count, selected * SLICE, HD))
    q = heads_first(queries[0], rows)
    qt = q.transpose(0, 2, 1)
    gt = heads_first(grad_out[0], rows).transpose(0, 2, 1)
    attn_out, grad_queries, send = attend(
        query_len, kv, q, qt, gt, own_keys[0], own_values[0], length, queries.shape[2]
    )
    got = swap(send)
    sums, squares = add_up(
        owner * blk_dev + row, got.reshape(wide_count * selected, SLICE, HD), all_blocks
    )
    back = swap(sums.reshape(wide_count, blk_dev, SLICE, HD))
    squares = total_over_mesh(squares)
    count = 2.0 * all_blocks * block_tok * width * lax.axis_size("mp")
    key_update, value_update = finish(squares, back, block_tok, width, count)
    return (attn_out[None], grad_queries[None], key_update, value_update)


def solution(mesh):
    shared = P("wide", None, "mp")
    return jax.shard_map(
        local,
        mesh=mesh,
        in_specs=(shared, shared, shared, shared, shared, P("wide", None), P(), P("wide"), shared),
        out_specs=(shared, shared, shared, shared),
        check_vma=False,
    )
```

time: 310 us -> 246 us (0.79); the launches traced: 305 us -> 245 us
  Pallas kernels: 0 us -> 93.4 us
  other arithmetic: 49.1 us -> 1.63 us
  matrix products: 40.3 us -> 0 us
  local copies, waits for them, and re-layouts: 41.2 us -> 12.7 us
  blocking collectives: 64.3 us -> 38.8 us
  starting transfers between devices: 32.3 us -> 28.1 us
  waiting for transfers between devices: 73.2 us -> 69.2 us
    pallas_call x0 -> x5, Pallas kernels: none -> 93.4 us  [the longest x1 69.2 us: split(): pl.pallas_call(split_kernel, out_shape=jax.ShapeDtypeStruct((count, block...]
    psum x1 -> x0, blocking collectives: 64.3 us -> none  [local(): total = lax.psum(squares, ('wide', 'mp'))]
    dot_general x14 -> x0, matrix products: 40.3 us -> none  [the longest x2 7.41 us: attend_head(): output = jnp.dot(prob_low, values, preferred_element_type=jnp.float32)]
    all_to_all x0 -> x1, blocking collectives: none -> 38.8 us  [swap(): return lax.all_to_all(a, 'wide', split_axis=0, concat_axis=0, tiled=True)]
    all_to_all x6 -> x3, waiting for transfers between devices: 73.2 us -> 49.4 us  [swap(): return lax.all_to_all(a, 'wide', split_axis=0, concat_axis=0, tiled=True)]
    all_to_all x6 -> x3, starting transfers between devices: 32.3 us -> 12.2 us  [swap(): return lax.all_to_all(a, 'wide', split_axis=0, concat_axis=0, tiled=True)]
    ppermute x0 -> x10, waiting for transfers between devices: none -> 19.7 us  [the longest x3 10.6 us: total_over_mesh(): lax.ppermute(a, 'wide', wide_pairs(0, d, 0))]
    ppermute x0 -> x10, starting transfers between devices: none -> 15.9 us  [the longest x3 6.59 us: total_over_mesh(): lax.ppermute(a, 'wide', wide_pairs(d, 0, 0))]
  transfers between devices with their start and end apart: 6 -> 13, of which waited for: 6 -> 8; matrix products, arithmetic and copies ran while one was open for 18% -> 3% of each run, Pallas kernels for 0% -> 0%
where the time goes in v1:
time: 246 us; the launch traced here: 245 us
  Pallas kernels  93.4 us (38%)
  waiting for transfers between devices  69.2 us (28%)
  blocking collectives  38.8 us (16%)
  starting transfers between devices  28.1 us (11%)
  local copies, waits for them, and re-layouts  12.7 us (5%)
    pallas_call x1, Pallas kernels, split(): pl.pallas_call(split_kernel, out_shape=jax.ShapeDtypeStruct((count, block...  69.2 us
    all_to_all x3, waiting for transfers between devices, swap(): return lax.all_to_all(a, 'wide', split_axis=0, concat_axis=0, tiled=True)  49.4 us
    all_to_all x1, blocking collectives, swap(): return lax.all_to_all(a, 'wide', split_axis=0, concat_axis=0, tiled=True)  38.8 us
    pallas_call x1, Pallas kernels, attend(): pl.pallas_call(attend_kernel, out_shape=(jax.ShapeDtypeStruct((queries, w...  16.1 us
    all_to_all x3, starting transfers between devices, swap(): return lax.all_to_all(a, 'wide', split_axis=0, concat_axis=0, tiled=True)  12.2 us
    ppermute x3, waiting for transfers between devices, total_over_mesh(): lax.ppermute(a, 'wide', wide_pairs(0, d, 0))  10.6 us
    unnamed x16, local copies, waits for them, and re-layouts  7.07 us
    ppermute x3, starting transfers between devices, total_over_mesh(): lax.ppermute(a, 'wide', wide_pairs(d, 0, 0))  6.59 us
  transfers between devices with their start and end apart: 13, of which 8 were waited for; matrix products, arithmetic and copies ran while one was open for 3% of the time, Pallas kernels for 0%

profile of v1, /device:TPU:0, one launch (start us, length us, event | category | flops | bytes accessed | tf_op | source)
XLA Modules:
  0.0 245.2 jit_solution(5258128873233231138)
XLA Ops:
  0.6 0.9 select_reduce_fusion
  1.5 0.6 fusion.7.tag_ref
  2.1 69.2 %split_blocks.1 = bf16[32,17,16,128]{3,2,1,0:T(8,128)(2,1)} custom-call(bf16[16,128,256]{2,1,0:T(8,128)(2,1)} %keys_ref.1, bf16[16,128,256]{2,1,0:T(8,128)(2,1)} %values_ref.1, bf16[1,16,128]{2,1,0:T(8,128)(2,1)} %fusion.7.tag_ref), custom_call_target="tpu_custom_call" | custom-call | tf_op jit(solution)/shard_map/split_blocks/pallas_call | solution.py:50
  71.3 38.8 %all_to_all.20 = bf16[32,17,16,128]{3,2,1,0:T(8,128)(2,1)S(1)} all-to-all(bf16[32,17,16,128]{3,2,1,0:T(8,128)(2,1)} %split_blocks.1), channel_id=1, replica_groups=mesh['wide'=32,'mp'=4] {'wide'}, dimensions={0} | all-to-all | bytes 4456448 | tf_op jit(solution)/shard_map/all_to_all | solution.py:272
  110.1 0.1 add_reduce_fusion
  110.2 0.1 add.65.index_ref
  110.3 1.4 pick_requested.1
  111.7 0.0 copy-start
  111.7 1.3 copy-done
  113.1 0.0 copy-start.6
  113.1 4.1 %all-to-all-start.1 = ((bf16[32,256,128]{2,1,0:T(8,128)(2,1)}), bf16[32,256,128]{2,1,0:T(8,128)(2,1)S(1)}, u32[]{:S(2)}, u32[]{:S(2)}) async-start(bf16[32,256,128]{2,1,0:T(8,128)(2,1)} %bitcast.54), calls=%async_computation.1 | async-start | bytes 4194304 | tf_op jit(solution)/shard_map/all_to_all | solution.py:272
  117.9 0.0 copy-done.6
  117.9 0.1 copy.22
  118.0 0.6 copy.19
  118.6 0.2 reshape.110
  118.8 0.0 copy-start.4
  118.8 0.0 copy-start.5
  118.8 0.3 copy.21.q_ref
  119.1 2.0 copy.23
  121.1 2.4 copy.20
  123.4 2.1 reshape.111
  125.5 20.6 %all-to-all-done.1.kv_ref = bf16[32,256,128]{2,1,0:T(8,128)(2,1)S(1)} async-done(((bf16[32,256,128]{2,1,0:T(8,128)(2,1)}), bf16[32,256,128]{2,1,0:T(8,128)(2,1)S(1)}, u32[]{:S(2)}, u32[]{:S(2)}) %all-to-all-start.1) | async-done | bytes 2097184 | tf_op jit(solution)/shard_map/all_to_all | solution.py:272
  146.1 0.0 copy-done.4
  146.1 0.0 copy-done.5
  146.1 0.0 copy-start.3
  146.1 1.0 copy-done.3
  147.2 16.1 %attend_forward_backward.1 = (bf16[128,2048]{1,0:T(8,128)(2,1)}, bf16[128,2048]{1,0:T(8,128)(2,1)}, bf16[32,256,128]{2,1,0:T(8,128)(2,1)S(1)}) custom-call(s32[1]{0:T(128)S(6)} %copy.24.length_ref, bf16[32,256,128]{2,1,0:T(8,128)(2,1)S(1)} %all-to-all-done.1.kv_ref, bf16[2,1024,128]{2,1,0:T(8,128)(2,1)S(1)} %copy.21.q_ref, ...), custom_call_target="tpu_custom_call" | custom-call | flops 6845104128 | bytes 8388608 | tf_op jit(solution)/shard_map/attend_forward_backward/pallas_call | solution.py:163
  163.3 0.0 copy-start.2
  163.3 1.3 copy-done.2
  164.6 4.0 %all-to-all-start.2 = ((bf16[32,256,128]{2,1,0:T(8,128)(2,1)}), bf16[32,256,128]{2,1,0:T(8,128)(2,1)S(1)}, u32[]{:S(2)}, u32[]{:S(2)}) async-start(bf16[32,256,128]{2,1,0:T(8,128)(2,1)} %copy-done.2), calls=%async_computation.2 | async-start | bytes 4194304 | tf_op jit(solution)/shard_map/all_to_all | solution.py:272
  168.6 0.1 add.67.index_ref
  168.7 28.8 %all-to-all-done.2 = bf16[32,256,128]{2,1,0:T(8,128)(2,1)S(1)} async-done(((bf16[32,256,128]{2,1,0:T(8,128)(2,1)}), bf16[32,256,128]{2,1,0:T(8,128)(2,1)S(1)}, u32[]{:S(2)}, u32[]{:S(2)}) %all-to-all-start.2) | async-done | bytes 2097184 | tf_op jit(solution)/shard_map/all_to_all | solution.py:272
  197.5 3.9 %add_over_readers.1 = (bf16[512,16,128]{2,1,0:T(8,128)(2,1)S(1)}, f32[8,128]{1,0:T(8,128)S(1)}) custom-call(s32[512]{0:T(512)S(1)} %add.67.index_ref, bf16[512,16,128]{2,1,0:T(8,128)(2,1)S(1)} %bitcast.55), custom_call_target="tpu_custom_call" | custom-call | tf_op jit(solution)/shard_map/add_over_readers/pallas_call | solution.py:210
  201.4 0.0 copy-start.1
  201.4 1.3 copy-done.1
  202.7 4.0 %all-to-all-start.3 = ((bf16[32,16,16,128]{3,2,1,0:T(8,128)(2,1)}), bf16[32,16,16,128]{3,2,1,0:T(8,128)(2,1)S(1)}, u32[]{:S(2)}, u32[]{:S(2)}) async-start(bf16[32,16,16,128]{3,2,1,0:T(8,128)(2,1)} %bitcast.56), calls=%async_computation.3 | async-start | bytes 4194304 | tf_op jit(solution)/shard_map/all_to_all | solution.py:272
  206.7 0.2 collective-permute-start
  207.0 1.0 collective-permute-done
  208.0 2.8 %collective-permute-start.3 = (f32[8,128]{1,0:T(8,128)S(1)}, f32[8,128]{1,0:T(8,128)S(1)}, u32[]{:S(2)}, u32[]{:S(2)}) collective-permute-start(f32[8,128]{1,0:T(8,128)S(1)} %add.68), channel_id=1, source_target_pairs={{0,3},{1,0},{2,1},{3,2},{4,7},{5,4},{6,5},{7,6},{8,11},{9,8},{10,9... | collective-permute-start | bytes 12296 | tf_op jit(solution)/shard_map/ppermute | solution.py:265
  210.7 0.8 collective-permute-start.2
  211.5 0.9 collective-permute-start.1
  212.4 0.0 collective-permute-done.3
  212.4 3.4 %collective-permute-done.2 = f32[8,128]{1,0:T(8,128)S(1)} collective-permute-done((f32[8,128]{1,0:T(8,128)S(1)}, f32[8,128]{1,0:T(8,128)S(1)}, u32[]{:S(2)}, u32[]{:S(2)}) %collective-permute-start.2) | collective-permute-done | bytes 4128 | tf_op jit(solution)/shard_map/ppermute | solution.py:265
  215.8 0.5 collective-permute-done.1
  216.3 2.9 %collective-permute-start.6 = (f32[8,128]{1,0:T(8,128)S(1)}, f32[8,128]{1,0:T(8,128)S(1)}, u32[]{:S(2)}, u32[]{:S(2)}) collective-permute-start(f32[8,128]{1,0:T(8,128)S(1)} %add_add_fusion.2), channel_id=1, source_target_pairs={{0,24},{4,28},{8,0},{12,4},{16,8},{20,12},{24,16},{28,20},{32,56},... | collective-permute-start | bytes 12296 | tf_op jit(solution)/shard_map/ppermute | solution.py:266
  219.3 0.8 collective-permute-start.5
  220.1 0.9 collective-permute-start.4
  221.0 10.6 %collective-permute-done.6 = f32[8,128]{1,0:T(8,128)S(1)} collective-permute-done((f32[8,128]{1,0:T(8,128)S(1)}, f32[8,128]{1,0:T(8,128)S(1)}, u32[]{:S(2)}, u32[]{:S(2)}) %collective-permute-start.6) | collective-permute-done | bytes 4128 | tf_op jit(solution)/shard_map/ppermute | solution.py:266
  231.6 0.0 collective-permute-done.5
  231.6 0.0 collective-permute-done.4
  231.6 5.1 %collective-permute-start.9 = (f32[8,128]{1,0:T(8,128)S(1)}, f32[8,128]{1,0:T(8,128)S(1)}, u32[]{:S(2)}, u32[]{:S(2)}) collective-permute-start(f32[8,128]{1,0:T(8,128)S(1)} %add_add_fusion.1), channel_id=1, source_target_pairs={{0,96},{4,100},{8,104},{12,108},{16,112},{20,116},{24,120},{28,124... | collective-permute-start | bytes 12296 | tf_op jit(solution)/shard_map/ppermute | solution.py:267
  236.7 0.9 collective-permute-start.8
  237.6 0.6 collective-permute-start.7
  238.2 0.0 collective-permute-done.9
  238.2 3.6 %collective-permute-done.8 = f32[8,128]{1,0:T(8,128)S(1)} collective-permute-done((f32[8,128]{1,0:T(8,128)S(1)}, f32[8,128]{1,0:T(8,128)S(1)}, u32[]{:S(2)}, u32[]{:S(2)}) %collective-permute-start.8) | collective-permute-done | bytes 4128 | tf_op jit(solution)/shard_map/ppermute | solution.py:267
  241.8 0.6 collective-permute-done.7
  242.4 0.0 all-to-all-done.3.got_ref
  242.4 2.8 %normalize_updates.1 = (f32[16,128,256]{2,1,0:T(8,128)}, f32[16,128,256]{2,1,0:T(8,128)}) custom-call(f32[8,128]{1,0:T(8,128)S(1)} %add_add_fusion.square_ref, bf16[32,16,16,128]{3,2,1,0:T(8,128)(2,1)S(1)} %all-to-all-done.3.got_ref), custom_call_target="tpu_custom_call" | custom-call | tf_op jit(solution)/shard_map/normalize_updates/pallas_call | solution.py:239
  (6 shorter events, 0.0 us)
Async XLA Ops:
  111.7 1.3 copy-start
  113.1 4.8 %copy-start.6 = (bf16[1,128,2048]{2,1,0:T(8,128)(2,1)S(1)}, bf16[1,128,2048]{2,1,0:T(8,128)(2,1)}, u32[]{:S(2)}) copy-start(bf16[1,128,2048]{2,1,0:T(8,128)(2,1)} %param.9) | copy-start | bytes 1572868
  113.1 33.0 %all-to-all-start.1 = ((bf16[32,256,128]{2,1,0:T(8,128)(2,1)}), bf16[32,256,128]{2,1,0:T(8,128)(2,1)S(1)}, u32[]{:S(2)}, u32[]{:S(2)}) async-start(bf16[32,256,128]{2,1,0:T(8,128)(2,1)} %bitcast.54), calls=%async_computation.1 | async-start | bytes 4194304 | tf_op jit(solution)/shard_map/all_to_all | solution.py:272
  118.8 27.3 %copy-start.4 = (bf16[1,128,256]{2,1,0:T(8,128)(2,1)S(1)}, bf16[1,128,256]{2,1,0:T(8,128)(2,1)}, u32[]{:S(2)}) copy-start(bf16[1,128,256]{2,1,0:T(8,128)(2,1)} %param.10) | copy-start | bytes 196612
  118.8 27.3 %copy-start.5 = (bf16[1,128,256]{2,1,0:T(8,128)(2,1)S(1)}, bf16[1,128,256]{2,1,0:T(8,128)(2,1)}, u32[]{:S(2)}) copy-start(bf16[1,128,256]{2,1,0:T(8,128)(2,1)} %param.11) | copy-start | bytes 196612
  146.1 1.0 copy-start.3
  163.3 1.3 copy-start.2
  164.6 32.9 %all-to-all-start.2 = ((bf16[32,256,128]{2,1,0:T(8,128)(2,1)}), bf16[32,256,128]{2,1,0:T(8,128)(2,1)S(1)}, u32[]{:S(2)}, u32[]{:S(2)}) async-start(bf16[32,256,128]{2,1,0:T(8,128)(2,1)} %copy-done.2), calls=%async_computation.2 | async-start | bytes 4194304 | tf_op jit(solution)/shard_map/all_to_all | solution.py:272
  201.4 1.3 copy-start.1
  202.7 39.7 %all-to-all-start.3 = ((bf16[32,16,16,128]{3,2,1,0:T(8,128)(2,1)}), bf16[32,16,16,128]{3,2,1,0:T(8,128)(2,1)S(1)}, u32[]{:S(2)}, u32[]{:S(2)}) async-start(bf16[32,16,16,128]{3,2,1,0:T(8,128)(2,1)} %bitcast.56), calls=%async_computation.3 | async-start | bytes 4194304 | tf_op jit(solution)/shard_map/all_to_all | solution.py:272
  206.7 1.2 collective-permute-start
  208.0 4.5 %collective-permute-start.3 = (f32[8,128]{1,0:T(8,128)S(1)}, f32[8,128]{1,0:T(8,128)S(1)}, u32[]{:S(2)}, u32[]{:S(2)}) collective-permute-start(f32[8,128]{1,0:T(8,128)S(1)} %add.68), channel_id=1, source_target_pairs={{0,3},{1,0},{2,1},{3,2},{4,7},{5,4},{6,5},{7,6},{8,11},{9,8},{10,9... | collective-permute-start | bytes 12296 | tf_op jit(solution)/shard_map/ppermute | solution.py:265
  210.7 5.1 %collective-permute-start.2 = (f32[8,128]{1,0:T(8,128)S(1)}, f32[8,128]{1,0:T(8,128)S(1)}, u32[]{:S(2)}, u32[]{:S(2)}) collective-permute-start(f32[8,128]{1,0:T(8,128)S(1)} %add.68), channel_id=1, source_target_pairs={{0,2},{1,3},{2,0},{3,1},{4,6},{5,7},{6,4},{7,5},{8,10},{9,11},{10,... | collective-permute-start | bytes 12296 | tf_op jit(solution)/shard_map/ppermute | solution.py:265
  211.5 4.8 %collective-permute-start.1 = (f32[8,128]{1,0:T(8,128)S(1)}, f32[8,128]{1,0:T(8,128)S(1)}, u32[]{:S(2)}, u32[]{:S(2)}) collective-permute-start(f32[8,128]{1,0:T(8,128)S(1)} %add.68), channel_id=1, source_target_pairs={{0,1},{1,2},{2,3},{3,0},{4,5},{5,6},{6,7},{7,4},{8,9},{9,10},{10,1... | collective-permute-start | bytes 12296 | tf_op jit(solution)/shard_map/ppermute | solution.py:265
  216.3 15.2 %collective-permute-start.6 = (f32[8,128]{1,0:T(8,128)S(1)}, f32[8,128]{1,0:T(8,128)S(1)}, u32[]{:S(2)}, u32[]{:S(2)}) collective-permute-start(f32[8,128]{1,0:T(8,128)S(1)} %add_add_fusion.2), channel_id=1, source_target_pairs={{0,24},{4,28},{8,0},{12,4},{16,8},{20,12},{24,16},{28,20},{32,56},... | collective-permute-start | bytes 12296 | tf_op jit(solution)/shard_map/ppermute | solution.py:266
  219.3 12.3 %collective-permute-start.5 = (f32[8,128]{1,0:T(8,128)S(1)}, f32[8,128]{1,0:T(8,128)S(1)}, u32[]{:S(2)}, u32[]{:S(2)}) collective-permute-start(f32[8,128]{1,0:T(8,128)S(1)} %add_add_fusion.2), channel_id=1, source_target_pairs={{0,16},{4,20},{8,24},{12,28},{16,0},{20,4},{24,8},{28,12},{32,48},... | collective-permute-start | bytes 12296 | tf_op jit(solution)/shard_map/ppermute | solution.py:266
  220.1 11.5 %collective-permute-start.4 = (f32[8,128]{1,0:T(8,128)S(1)}, f32[8,128]{1,0:T(8,128)S(1)}, u32[]{:S(2)}, u32[]{:S(2)}) collective-permute-start(f32[8,128]{1,0:T(8,128)S(1)} %add_add_fusion.2), channel_id=1, source_target_pairs={{0,8},{4,12},{8,16},{12,20},{16,24},{20,28},{24,0},{28,4},{32,40},... | collective-permute-start | bytes 12296 | tf_op jit(solution)/shard_map/ppermute | solution.py:266
  231.6 6.6 %collective-permute-start.9 = (f32[8,128]{1,0:T(8,128)S(1)}, f32[8,128]{1,0:T(8,128)S(1)}, u32[]{:S(2)}, u32[]{:S(2)}) collective-permute-start(f32[8,128]{1,0:T(8,128)S(1)} %add_add_fusion.1), channel_id=1, source_target_pairs={{0,96},{4,100},{8,104},{12,108},{16,112},{20,116},{24,120},{28,124... | collective-permute-start | bytes 12296 | tf_op jit(solution)/shard_map/ppermute | solution.py:267
  236.7 5.1 %collective-permute-start.8 = (f32[8,128]{1,0:T(8,128)S(1)}, f32[8,128]{1,0:T(8,128)S(1)}, u32[]{:S(2)}, u32[]{:S(2)}) collective-permute-start(f32[8,128]{1,0:T(8,128)S(1)} %add_add_fusion.1), channel_id=1, source_target_pairs={{0,64},{4,68},{8,72},{12,76},{16,80},{20,84},{24,88},{28,92},{32,9... | collective-permute-start | bytes 12296 | tf_op jit(solution)/shard_map/ppermute | solution.py:267
  237.6 4.8 %collective-permute-start.7 = (f32[8,128]{1,0:T(8,128)S(1)}, f32[8,128]{1,0:T(8,128)S(1)}, u32[]{:S(2)}, u32[]{:S(2)}) collective-permute-start(f32[8,128]{1,0:T(8,128)S(1)} %add_add_fusion.1), channel_id=1, source_target_pairs={{0,32},{4,36},{8,40},{12,44},{16,48},{20,52},{24,56},{28,60},{32,6... | collective-permute-start | bytes 12296 | tf_op jit(solution)/shard_map/ppermute | solution.py:267

commit v2 on v1

--- a/solution.py
+++ b/solution.py
@@ -23,58 +23,94 @@
     return jnp.dot(a, b, preferred_element_type=jnp.float32)
 
 
-def split_kernel(keys_ref, values_ref, tag_ref, out_ref, sems):
-    blocks = keys_ref.shape[0]
-    copies = []
-    for m in range(out_ref.shape[0]):
-        t, h, kind = m // 4, (m // 2) % 2, m % 2
-        src = (keys_ref, values_ref)[kind]
-        copies.append(
-            pltpu.make_async_copy(
-                src.at[:, pl.ds(t * SLICE, SLICE), pl.ds(h * HD, HD)],
-                out_ref.at[m, pl.ds(0, blocks)],
-                sems.at[2 * m],
+def split_kernel(ids_ref, home_ref, keys_ref, values_ref, out_ref, inside, parts, in_sems, out_sems):
+    blocks, tokens, width = keys_ref.shape
+    groups = tokens // SLICE
+    arrive = []
+    for t in range(groups):
+        for kind, src in enumerate((keys_ref, values_ref)):
+            copy = pltpu.make_async_copy(
+                src.at[:, pl.ds(t * SLICE, SLICE)], inside.at[t, kind], in_sems.at[t, kind]
             )
-        )
-        copies.append(
-            pltpu.make_async_copy(tag_ref, out_ref.at[m, pl.ds(blocks, 1)], sems.at[2 * m + 1])
-        )
-    for copy in copies:
-        copy.start()
-    for copy in copies:
+            copy.start()
+            arrive.append(copy)
+    line = lax.broadcasted_iota(jnp.int32, (SLICE, HD), 0)
+    lane = lax.broadcasted_iota(jnp.int32, (SLICE, HD), 1)
+    tag = jnp.zeros((SLICE, HD), jnp.int32)
+    for k in range(ids_ref.shape[1]):
+        storage = home_ref[ids_ref[0, k]]
+        owner = lax.div(storage, blocks)
+        tag = jnp.where((line == 0) & (lane == k), owner, tag)
+        tag = jnp.where((line == 1) & (lane == k), storage - owner * blocks, tag)
+    tag = tag.astype(jnp.float32).astype(jnp.bfloat16)
+    leave = []
+    for t in range(groups):
+        for kind in range(KINDS):
+            arrive[t * KINDS + kind].wait()
+        for part in range(HEADS * KINDS):
+            m = t * HEADS * KINDS + part
+            h, kind = part // KINDS, part % KINDS
+            parts[m, pl.ds(0, blocks)] = inside[t, kind, :, :, h * HD : (h + 1) * HD]
+            parts[m, blocks] = tag
+            copy = pltpu.make_async_copy(parts.at[m], out_ref.at[m], out_sems.at[m])
+            copy.start()
+            leave.append(copy)
+    for copy in leave:
         copy.wait()
 
 
-def split(cart_keys, cart_values, tag, count):
-    blocks = cart_keys.shape[0]
+def split(block_ids, block_home, cart_keys, cart_values, count):
+    blocks, tokens, width = cart_keys.shape
+    groups = tokens // SLICE
+    smem = pl.BlockSpec(memory_space=pltpu.SMEM)
+    hbm = pl.BlockSpec(memory_space=pltpu.HBM)
     return pl.pallas_call(
         split_kernel,
         out_shape=jax.ShapeDtypeStruct((count, blocks + 1, SLICE, HD), jnp.bfloat16),
-        in_specs=[pl.BlockSpec(memory_space=pl.ANY)] * 3,
-        out_specs=pl.BlockSpec(memory_space=pl.ANY),
-        scratch_shapes=[pltpu.SemaphoreType.DMA((2 * count,))],
+        in_specs=[smem, smem, hbm, hbm],
+        out_specs=hbm,
+        scratch_shapes=[
+            pltpu.VMEM((groups, KINDS, blocks, SLICE, width), jnp.bfloat16),
+            pltpu.VMEM((count, blocks + 1, SLICE, HD), jnp.bfloat16),
+            pltpu.SemaphoreType.DMA((groups, KINDS)),
+            pltpu.SemaphoreType.DMA((count,)),
+        ],
+        compiler_params=pltpu.CompilerParams(vmem_limit_bytes=16 * MIB),
         name="split_blocks",
-    )(cart_keys, cart_values, tag)
-
-
-def pick_kernel(index_ref, held_ref, out_ref):
-    def step(n, carry):
-        for u in range(8):
-            out_ref[n * 8 + u] = held_ref[index_ref[n * 8 + u]]
-        return carry
-
-    lax.fori_loop(0, out_ref.shape[0] // 8, step, 0)
+    )(block_ids, block_home, cart_keys, cart_values)
+
+
+def pick_kernel(index_ref, held_ref, out_ref, buffer, sems):
+    parts = sems.shape[0]
+    size = out_ref.shape[0] // parts
+    copies = []
+    for part in range(parts):
+
+        def step(n, carry):
+            for u in range(16):
+                at = part * size + n * 16 + u
+                buffer[at] = held_ref[index_ref[at]]
+            return carry
+
+        lax.fori_loop(0, size // 16, step, 0)
+        at = pl.ds(part * size, size)
+        copies.append(pltpu.make_async_copy(buffer.at[at], out_ref.at[at], sems.at[part]))
+        copies[-1].start()
+    for copy in copies:
+        copy.wait()
 
 
 def pick(index, held):
+    shape = (index.shape[0],) + held.shape[1:]
     return pl.pallas_call(
         pick_kernel,
-        out_shape=jax.ShapeDtypeStruct((index.shape[0],) + held.shape[1:], jnp.bfloat16),
+        out_shape=jax.ShapeDtypeStruct(shape, jnp.bfloat16),
         in_specs=[
             pl.BlockSpec(memory_space=pltpu.SMEM),
             pl.BlockSpec(memory_space=pltpu.VMEM),
         ],
-        out_specs=pl.BlockSpec(memory_space=pltpu.VMEM),
+        out_specs=pl.BlockSpec(memory_space=pltpu.HBM),
+        scratch_shapes=[pltpu.VMEM(shape, jnp.bfloat16), pltpu.SemaphoreType.DMA((4,))],
         compiler_params=pltpu.CompilerParams(vmem_limit_bytes=16 * MIB),
         name="pick_requested",
     )(index, held)
@@ -94,7 +130,22 @@
     score,
     expo,
     acc,
+    gt_in,
+    out_buf,
+    grad_buf,
+    send_buf,
+    gt_sem,
+    out_sems,
+    send_sems,
 ):
+    load_gt = pltpu.make_async_copy(gt_ref, gt_in, gt_sem)
+    load_gt.start()
+    copies = []
+
+    def leave(src, dst, sem):
+        copies.append(pltpu.make_async_copy(src, dst, sem))
+        copies[-1].start()
+
     used = length_ref[0]
     chunks = kv_ref.shape[0] // (HEADS * KINDS)
     chunk = kv_ref.shape[1]
@@ -113,7 +164,6 @@
         own_k = own_k_ref[:, lanes]
         own_v = own_v_ref[:, lanes]
         qt = qt_ref[head]
-        gt = gt_ref[head]
         at = lambda c, kind: (c * HEADS + head) * KINDS + kind
         own_s = jnp.where(seen, nn(own_k, qt), -1e30)
         top = jnp.max(own_s.reshape(own // 8, 8, rows), axis=0)
@@ -133,26 +183,35 @@
             expo[c] = low
             acc[...] += nn(kv_ref[at(c, 1)].T, low)
         inv = 1.0 / jnp.sum(total, axis=0, keepdims=True)
-        gt32 = jnp.where(row_used, gt.astype(jnp.float32), 0.0)
+        if head == 0:
+            load_gt.wait()
+        gt32 = jnp.where(row_used, gt_in[head].astype(jnp.float32), 0.0)
         out = jnp.where(row_used, acc[...] * inv, 0.0)
         for r in range(repeat):
             cols = slice((head * repeat + r) * HD, (head * repeat + r + 1) * HD)
-            out_ref[:, cols] = out[:, r * queries : (r + 1) * queries].T.astype(jnp.bfloat16)
+            out_buf[:, cols] = out[:, r * queries : (r + 1) * queries].T.astype(jnp.bfloat16)
+        half = pl.ds(head * repeat * HD, repeat * HD)
+        leave(out_buf.at[:, half], out_ref.at[:, half], out_sems.at[0, head])
         delta = jnp.sum(gt32 * out, axis=0, keepdims=True) * inv
         gs = (gt32 * inv).astype(jnp.bfloat16)
         ds = (own_e.astype(jnp.float32) * (nn(own_v, gs) - delta)).astype(jnp.bfloat16)
         acc[...] = nn(own_k.T, ds)
         for c in range(chunks):
             low = expo[c]
-            send_ref[at(c, 1)] = nt(low, gs).astype(jnp.bfloat16)
+            send_buf[at(c, 1)] = nt(low, gs).astype(jnp.bfloat16)
             dp = nn(kv_ref[at(c, 1)], gs)
             ds = (low.astype(jnp.float32) * (dp - delta)).astype(jnp.bfloat16)
-            send_ref[at(c, 0)] = (nn(ds, q_ref[head]) * scale).astype(jnp.bfloat16)
+            send_buf[at(c, 0)] = (nn(ds, q_ref[head]) * scale).astype(jnp.bfloat16)
+            pair = pl.ds(at(c, 0), KINDS)
+            leave(send_buf.at[pair], send_ref.at[pair], send_sems.at[c * HEADS + head])
             acc[...] += nn(kv_ref[at(c, 0)].T, ds)
         grad = acc[...] * scale
         for r in range(repeat):
             cols = slice((head * repeat + r) * HD, (head * repeat + r + 1) * HD)
-            grad_q_ref[:, cols] = grad[:, r * queries : (r + 1) * queries].T.astype(jnp.bfloat16)
+            grad_buf[:, cols] = grad[:, r * queries : (r + 1) * queries].T.astype(jnp.bfloat16)
+        leave(grad_buf.at[:, half], grad_q_ref.at[:, half], out_sems.at[1, head])
+    for copy in copies:
+        copy.wait()
 
 
 def attend(length, kv, q, qt, gt, own_k, own_v, queries, width):
@@ -160,6 +219,7 @@
     rows = q.shape[1]
     chunks = count // (HEADS * KINDS)
     vmem = pl.BlockSpec(memory_space=pltpu.VMEM)
+    hbm = pl.BlockSpec(memory_space=pltpu.HBM)
     return pl.pallas_call(
         attend_kernel,
         out_shape=(
@@ -167,12 +227,19 @@
             jax.ShapeDtypeStruct((queries, width), jnp.bfloat16),
             jax.ShapeDtypeStruct(kv.shape, jnp.bfloat16),
         ),
-        in_specs=[pl.BlockSpec(memory_space=pltpu.SMEM)] + [vmem] * 6,
-        out_specs=(vmem, vmem, vmem),
+        in_specs=[pl.BlockSpec(memory_space=pltpu.SMEM), vmem, vmem, vmem, hbm, vmem, vmem],
+        out_specs=(hbm, hbm, hbm),
         scratch_shapes=[
             pltpu.VMEM((chunks, chunk, rows), jnp.float32),
             pltpu.VMEM((chunks, chunk, rows), jnp.bfloat16),
             pltpu.VMEM((HD, rows), jnp.float32),
+            pltpu.VMEM(gt.shape, jnp.bfloat16),
+            pltpu.VMEM((queries, width), jnp.bfloat16),
+            pltpu.VMEM((queries, width), jnp.bfloat16),
+            pltpu.VMEM(kv.shape, jnp.bfloat16),
+            pltpu.SemaphoreType.DMA,
+            pltpu.SemaphoreType.DMA((2, HEADS)),
+            pltpu.SemaphoreType.DMA((chunks * HEADS,)),
         ],
         compiler_params=pltpu.CompilerParams(vmem_limit_bytes=48 * MIB),
         cost_estimate=pl.CostEstimate(
@@ -184,25 +251,37 @@
     )(length, kv, q, qt, gt, own_k, own_v)
 
 
-def add_kernel(index_ref, got_ref, out_ref, square_ref, table):
+def add_kernel(index_ref, got_ref, out_ref, square_ref, table, buffer, sems):
+    selected = index_ref.shape[1]
+    parts = sems.shape[0]
+    size = out_ref.shape[0] // parts
     table[...] = jnp.zeros_like(table)
 
     def step(n, carry):
-        for u in range(4):
-            at = index_ref[n * 4 + u]
-            table[at] += got_ref[n * 4 + u].astype(jnp.float32)
+        at = [index_ref[n, k] for k in range(selected)]
+        sums = [table[at[k]] + got_ref[n, k].astype(jnp.float32) for k in range(selected)]
+        for k in range(selected):
+            table[at[k]] = sums[k]
         return carry
 
-    lax.fori_loop(0, got_ref.shape[0] // 4, step, 0)
-
-    def finish(n, squares):
-        rows = table[pl.ds(n * 8, 8)]
-        out_ref[pl.ds(n * 8, 8)] = rows.astype(jnp.bfloat16)
-        return squares + jnp.sum((rows * rows).reshape(8 * SLICE // 8, 8, HD), axis=0)
-
-    square_ref[...] = lax.fori_loop(
-        0, table.shape[0] // 8, finish, jnp.zeros(square_ref.shape, jnp.float32)
-    )
+    lax.fori_loop(0, got_ref.shape[0], step, 0)
+    squares = jnp.zeros(square_ref.shape, jnp.float32)
+    copies = []
+    for part in range(parts):
+
+        def finish(n, squares):
+            at = pl.ds(part * size + n * 8, 8)
+            rows = table[at]
+            buffer[at] = rows.astype(jnp.bfloat16)
+            return squares + jnp.sum((rows * rows).reshape(SLICE, 8, HD), axis=0)
+
+        squares = lax.fori_loop(0, size // 8, finish, squares)
+        at = pl.ds(part * size, size)
+        copies.append(pltpu.make_async_copy(buffer.at[at], out_ref.at[at], sems.at[part]))
+        copies[-1].start()
+    square_ref[...] = squares
+    for copy in copies:
+        copy.wait()
 
 
 def add_up(index, got, blocks):
@@ -214,8 +293,12 @@
             jax.ShapeDtypeStruct((8, HD), jnp.float32),
         ),
         in_specs=[pl.BlockSpec(memory_space=pltpu.SMEM), vmem],
-        out_specs=(vmem, vmem),
-        scratch_shapes=[pltpu.VMEM((blocks, SLICE, HD), jnp.float32)],
+        out_specs=(pl.BlockSpec(memory_space=pltpu.HBM), vmem),
+        scratch_shapes=[
+            pltpu.VMEM((blocks, SLICE, HD), jnp.float32),
+            pltpu.VMEM((blocks, SLICE, HD), jnp.bfloat16),
+            pltpu.SemaphoreType.DMA((4,)),
+        ],
         compiler_params=pltpu.CompilerParams(vmem_limit_bytes=24 * MIB),
         name="add_over_readers",
     )(index, got)
@@ -263,9 +346,8 @@
 def total_over_mesh(a):
     a = a + lax.ppermute(a, "wide", wide_pairs(0, 0, 1))
     a = a + sum(lax.ppermute(a, "mp", [(i, (i + d) % 4) for i in range(4)]) for d in (1, 2, 3))
-    a = a + sum(lax.ppermute(a, "wide", wide_pairs(0, d, 0)) for d in (1, 2, 3))
-    a = a + sum(lax.ppermute(a, "wide", wide_pairs(d, 0, 0)) for d in (1, 2, 3))
-    return a
+    shifts = [(dy, dz) for dy in range(4) for dz in range(4) if (dy, dz) != (0, 0)]
+    return a + sum(lax.ppermute(a, "wide", wide_pairs(dy, dz, 0)) for dy, dz in shifts)
 
 
 def swap(a):
@@ -294,15 +376,12 @@
     all_blocks = block_home.shape[0]
     length = queries.shape[1]
     rows = length * queries.shape[2] // width
-    lookup = block_ids[0][:, None] == jnp.arange(all_blocks, dtype=jnp.int32)
-    storage = jnp.sum(jnp.where(lookup, block_home[None, :], 0), axis=-1)
-    tag = jnp.stack([storage // blk_dev, storage % blk_dev]).astype(jnp.bfloat16)
-    tag = jnp.pad(tag, ((0, SLICE - 2), (0, HD - selected)))[None]
-    held = swap(split(cart_keys, cart_values, tag, wide_count))
+    held = swap(split(block_ids, block_home, cart_keys, cart_values, wide_count))
     asked = held[:, blk_dev, :2, :selected].astype(jnp.int32)
-    owner, row = asked[:, 0].reshape(-1), asked[:, 1].reshape(-1)
+    owner, row = asked[:, 0], asked[:, 1]
     picked = pick(
-        owner * (blk_dev + 1) + row, held.reshape(wide_count * (blk_dev + 1), SLICE, HD)
+        (owner * (blk_dev + 1) + row).reshape(-1),
+        held.reshape(wide_count * (blk_dev + 1), SLICE, HD),
     )
     kv = swap(picked.reshape(wide_count, selected * SLICE, HD))
     q = heads_first(queries[0], rows)
@@ -313,7 +392,7 @@
     )
     got = swap(send)
     sums, squares = add_up(
-        owner * blk_dev + row, got.reshape(wide_count * selected, SLICE, HD), all_blocks
+        owner * blk_dev + row, got.reshape(wide_count, selected, SLICE, HD), all_blocks
     )
     back = swap(sums.reshape(wide_count, blk_dev, SLICE, HD))
     squares = total_over_mesh(squares)

time: 246 us -> 202 us (0.82)
  Pallas kernels: 93.4 us -> 35.1 us
  waiting for transfers between devices: 69.2 us -> 35.2 us
  blocking collectives: 38.8 us -> 69.6 us
  starting transfers between devices: 28.1 us -> 44.9 us
    pallas_call x1, Pallas kernels: 69.2 us -> 4.65 us  [split(): pl.pallas_call(split_kernel, out_shape=jax.ShapeDtypeStruct((count, block...]
    all_to_all x1 -> x2, blocking collectives: 38.8 us -> 69.6 us  [swap(): return lax.all_to_all(a, 'wide', split_axis=0, concat_axis=0, tiled=True)]
    all_to_all x3 -> x2, waiting for transfers between devices: 49.4 us -> 20.6 us  [swap(): return lax.all_to_all(a, 'wide', split_axis=0, concat_axis=0, tiled=True)]
    ppermute x6 -> x15, starting transfers between devices: 11.2 us -> 31.9 us  [total_over_mesh(): lax.ppermute(a, 'wide', wide_pairs(dy, dz, 0))]
    pallas_call x1, Pallas kernels: 16.1 us -> 22.7 us  [attend(): pl.pallas_call(attend_kernel, out_shape=(jax.ShapeDtypeStruct((queries, w...]
    ppermute x6 -> x15, waiting for transfers between devices: 14.8 us -> 9.79 us  [total_over_mesh(): lax.ppermute(a, 'wide', wide_pairs(dy, dz, 0))]
    all_to_all x3 -> x2, starting transfers between devices: 12.2 us -> 8.19 us  [swap(): return lax.all_to_all(a, 'wide', split_axis=0, concat_axis=0, tiled=True)]
    unnamed x16 -> x22, local copies, waits for them, and re-layouts: 7.07 us -> 9.53 us
  transfers between devices with their start and end apart: 13 -> 21, of which waited for: 8 -> 8; matrix products, arithmetic and copies ran while one was open for 3% -> 4% of each run, Pallas kernels for 0% -> 0%
where the time goes in v2:
time: 202 us; the launch traced here: 201 us
  blocking collectives  69.6 us (34%)
  starting transfers between devices  44.9 us (22%)
  waiting for transfers between devices  35.2 us (17%)
  Pallas kernels  35.1 us (17%)
  local copies, waits for them, and re-layouts  15.1 us (7%)
    all_to_all x2, blocking collectives, swap(): return lax.all_to_all(a, 'wide', split_axis=0, concat_axis=0, tiled=True)  69.6 us
    ppermute x15, starting transfers between devices, total_over_mesh(): lax.ppermute(a, 'wide', wide_pairs(dy, dz, 0))  31.9 us
    pallas_call x1, Pallas kernels, attend(): pl.pallas_call(attend_kernel, out_shape=(jax.ShapeDtypeStruct((queries, w...  22.7 us
    all_to_all x2, waiting for transfers between devices, swap(): return lax.all_to_all(a, 'wide', split_axis=0, concat_axis=0, tiled=True)  20.6 us
    ppermute x15, waiting for transfers between devices, total_over_mesh(): lax.ppermute(a, 'wide', wide_pairs(dy, dz, 0))  9.79 us
    unnamed x22, local copies, waits for them, and re-layouts  9.53 us
    all_to_all x2, starting transfers between devices, swap(): return lax.all_to_all(a, 'wide', split_axis=0, concat_axis=0, tiled=True)  8.19 us
    pallas_call x1, Pallas kernels, split(): pl.pallas_call(split_kernel, out_shape=jax.ShapeDtypeStruct((count, block...  4.65 us
  transfers between devices with their start and end apart: 21, of which 8 were waited for; matrix products, arithmetic and copies ran while one was open for 4% of the time, Pallas kernels for 0%

profile of v2, /device:TPU:0, one launch (start us, length us, event | category | flops | bytes accessed | tf_op | source)
XLA Modules:
  0.0 201.4 jit_solution(16878378893236060096)
XLA Ops:
  0.6 1.2 copy-done.2
  1.9 1.2 copy-done.3
  3.1 0.7 copy-done.5
  3.8 0.7 copy-done.6
  4.4 4.6 %split_blocks.1 = bf16[32,17,16,128]{3,2,1,0:T(8,128)(2,1)S(1)} custom-call(s32[1,16]{1,0:T(1,128)S(1)} %copy-done.6, s32[512]{0:T(512)S(1)} %copy-done.5, bf16[16,128,256]{2,1,0:T(8,128)(2,1)S(1)} %copy-done.2, bf16[16,128,256]{2,1,0:T(8,128)(2,1)S(1)} %copy-done.3), custom_call_target="tpu_custom_call" | custom-call | tf_op jit(solution)/shard_map/split_blocks/pallas_call | solution.py:67
  9.1 38.5 %all_to_all.20 = bf16[32,17,16,128]{3,2,1,0:T(8,128)(2,1)S(1)} all-to-all(bf16[32,17,16,128]{3,2,1,0:T(8,128)(2,1)S(1)} %split_blocks.1), channel_id=1, replica_groups=mesh['wide'=32,'mp'=4] {'wide'}, dimensions={0} | all-to-all | bytes 4456448 | tf_op jit(solution)/shard_map/all_to_all | solution.py:354
  47.7 0.1 add.70.index_ref
  47.8 1.5 pick_requested.1
  49.2 0.0 copy-start
  49.3 1.3 copy-done
  50.6 4.1 %all-to-all-start.1 = ((bf16[32,256,128]{2,1,0:T(8,128)(2,1)}), bf16[32,256,128]{2,1,0:T(8,128)(2,1)S(1)}, u32[]{:S(2)}, u32[]{:S(2)}) async-start(bf16[32,256,128]{2,1,0:T(8,128)(2,1)} %bitcast.38), calls=%async_computation.1 | async-start | bytes 4194304 | tf_op jit(solution)/shard_map/all_to_all | solution.py:354
  55.4 0.1 copy.27
  55.5 0.6 copy.23
  56.1 0.2 reshape.39
  56.3 0.0 copy-start.7
  56.3 0.0 copy-start.8
  56.4 0.3 copy.25.q_ref
  56.6 2.0 copy.28
  58.6 2.4 %copy.24 = bf16[128,2,8,128]{0,2,3,1:T(8,128)(2,1)} copy(bf16[128,2,8,128]{3,2,1,0:T(8,128)(2,1)} %bitcast.48) | data formatting | bytes 1048576 | tf_op jit(solution)/shard_map/reshape;squeeze | solution.py:359
  60.9 2.1 %reshape.40 = bf16[2,1024,128]{1,2,0:T(8,128)(2,1)} reshape(bf16[2,8,128,128]{2,1,3,0:T(8,128)(2,1)} %bitcast.46) | data formatting | bytes 1048576 | tf_op jit(solution)/shard_map/reshape | solution.py:359
  63.0 20.6 %all-to-all-done.1.kv_ref = bf16[32,256,128]{2,1,0:T(8,128)(2,1)S(1)} async-done(((bf16[32,256,128]{2,1,0:T(8,128)(2,1)}), bf16[32,256,128]{2,1,0:T(8,128)(2,1)S(1)}, u32[]{:S(2)}, u32[]{:S(2)}) %all-to-all-start.1) | async-done | bytes 2097184 | tf_op jit(solution)/shard_map/all_to_all | solution.py:354
  83.6 1.0 copy-done.4
  84.7 22.7 %attend_forward_backward.1 = (bf16[128,2048]{1,0:T(8,128)(2,1)}, bf16[128,2048]{1,0:T(8,128)(2,1)}, bf16[32,256,128]{2,1,0:T(8,128)(2,1)S(1)}) custom-call(s32[1]{0:T(128)S(6)} %copy.32.length_ref, bf16[32,256,128]{2,1,0:T(8,128)(2,1)S(1)} %all-to-all-done.1.kv_ref, bf16[2,1024,128]{2,1,0:T(8,128)(2,1)S(1)} %copy.25.q_ref, ...), custom_call_target="tpu_custom_call" | custom-call | flops 6845104128 | bytes 8388608 | tf_op jit(solution)/shard_map/attend_forward_backward/pallas_call | solution.py:223
  107.3 31.1 %all_to_all.21 = bf16[32,256,128]{2,1,0:T(8,128)(2,1)S(1)} all-to-all(bf16[32,256,128]{2,1,0:T(8,128)(2,1)S(1)} %get-tuple-element.13), channel_id=1, replica_groups=mesh['wide'=32,'mp'=4] {'wide'}, dimensions={0} | all-to-all | bytes 4194304 | tf_op jit(solution)/shard_map/all_to_all | solution.py:354
  138.4 3.4 %add_over_readers.1 = (bf16[512,16,128]{2,1,0:T(8,128)(2,1)S(1)}, f32[8,128]{1,0:T(8,128)S(1)}) custom-call(s32[32,16]{1,0:T(8,128)S(1)} %get-tuple-element.18.index_ref, bf16[32,16,16,128]{3,2,1,0:T(8,128)(2,1)S(1)} %bitcast.39), custom_call_target="tpu_custom_call" | custom-call | tf_op jit(solution)/shard_map/add_over_readers/pallas_call | solution.py:289
  141.9 0.0 copy-start.1
  141.9 1.3 copy-done.1
  143.2 4.0 %all-to-all-start.3 = ((bf16[32,16,16,128]{3,2,1,0:T(8,128)(2,1)}), bf16[32,16,16,128]{3,2,1,0:T(8,128)(2,1)S(1)}, u32[]{:S(2)}, u32[]{:S(2)}) async-start(bf16[32,16,16,128]{3,2,1,0:T(8,128)(2,1)} %bitcast.40), calls=%async_computation.3 | async-start | bytes 4194304 | tf_op jit(solution)/shard_map/all_to_all | solution.py:354
  147.2 0.4 collective-permute-start
  147.6 0.9 collective-permute-done
  148.5 2.8 %collective-permute-start.3 = (f32[8,128]{1,0:T(8,128)S(1)}, f32[8,128]{1,0:T(8,128)S(1)}, u32[]{:S(2)}, u32[]{:S(2)}) collective-permute-start(f32[8,128]{1,0:T(8,128)S(1)} %add.73), channel_id=1, source_target_pairs={{0,3},{1,0},{2,1},{3,2},{4,7},{5,4},{6,5},{7,6},{8,11},{9,8},{10,9... | collective-permute-start | bytes 12296 | tf_op jit(solution)/shard_map/ppermute | solution.py:348
  151.2 0.8 collective-permute-start.2
  152.0 0.9 collective-permute-start.1
  152.9 0.0 collective-permute-done.3
  152.9 3.4 %collective-permute-done.2 = f32[8,128]{1,0:T(8,128)S(1)} collective-permute-done((f32[8,128]{1,0:T(8,128)S(1)}, f32[8,128]{1,0:T(8,128)S(1)}, u32[]{:S(2)}, u32[]{:S(2)}) %collective-permute-start.2) | collective-permute-done | bytes 4128 | tf_op jit(solution)/shard_map/ppermute | solution.py:348
  156.3 0.5 collective-permute-done.1
  156.9 5.2 %collective-permute-start.18 = (f32[8,128]{1,0:T(8,128)S(1)}, f32[8,128]{1,0:T(8,128)S(1)}, u32[]{:S(2)}, u32[]{:S(2)}) collective-permute-start(f32[8,128]{1,0:T(8,128)S(1)} %add_add_fusion.1), channel_id=1, source_target_pairs={{0,120},{4,124},{8,96},{12,100},{16,104},{20,108},{24,112},{28,116... | collective-permute-start | bytes 12296 | tf_op jit(solution)/shard_map/ppermute | solution.py:350
  162.1 1.1 collective-permute-start.17
  163.1 0.9 collective-permute-start.16
  164.0 0.6 collective-permute-start.15
  164.6 4.8 %collective-permute-start.14 = (f32[8,128]{1,0:T(8,128)S(1)}, f32[8,128]{1,0:T(8,128)S(1)}, u32[]{:S(2)}, u32[]{:S(2)}) collective-permute-start(f32[8,128]{1,0:T(8,128)S(1)} %add_add_fusion.1), channel_id=1, source_target_pairs={{0,88},{4,92},{8,64},{12,68},{16,72},{20,76},{24,80},{28,84},{32,1... | collective-permute-start | bytes 12296 | tf_op jit(solution)/shard_map/ppermute | solution.py:350
  169.3 4.4 %collective-permute-done.18 = f32[8,128]{1,0:T(8,128)S(1)} collective-permute-done((f32[8,128]{1,0:T(8,128)S(1)}, f32[8,128]{1,0:T(8,128)S(1)}, u32[]{:S(2)}, u32[]{:S(2)}) %collective-permute-start.18) | collective-permute-done | bytes 4128 | tf_op jit(solution)/shard_map/ppermute | solution.py:350
  173.8 5.2 %collective-permute-start.13 = (f32[8,128]{1,0:T(8,128)S(1)}, f32[8,128]{1,0:T(8,128)S(1)}, u32[]{:S(2)}, u32[]{:S(2)}) collective-permute-start(f32[8,128]{1,0:T(8,128)S(1)} %add_add_fusion.1), channel_id=1, source_target_pairs={{0,80},{4,84},{8,88},{12,92},{16,64},{20,68},{24,72},{28,76},{32,1... | collective-permute-start | bytes 12296 | tf_op jit(solution)/shard_map/ppermute | solution.py:350
  179.0 0.0 collective-permute-done.17
  179.0 0.1 collective-permute-start.12
  179.1 0.0 collective-permute-done.16
  179.1 2.7 %collective-permute-start.11 = (f32[8,128]{1,0:T(8,128)S(1)}, f32[8,128]{1,0:T(8,128)S(1)}, u32[]{:S(2)}, u32[]{:S(2)}) collective-permute-start(f32[8,128]{1,0:T(8,128)S(1)} %add_add_fusion.1), channel_id=1, source_target_pairs={{0,64},{4,68},{8,72},{12,76},{16,80},{20,84},{24,88},{28,92},{32,9... | collective-permute-start | bytes 12296 | tf_op jit(solution)/shard_map/ppermute | solution.py:350
  181.8 0.0 collective-permute-done.15
  181.8 1.5 collective-permute-start.10
  183.3 0.0 collective-permute-done.14
  183.3 0.8 collective-permute-start.9
  184.1 0.0 collective-permute-done.13
  184.1 1.6 collective-permute-start.8
  185.7 0.5 collective-permute-done.12
  186.2 2.8 %collective-permute-start.7 = (f32[8,128]{1,0:T(8,128)S(1)}, f32[8,128]{1,0:T(8,128)S(1)}, u32[]{:S(2)}, u32[]{:S(2)}) collective-permute-start(f32[8,128]{1,0:T(8,128)S(1)} %add_add_fusion.1), channel_id=1, source_target_pairs={{0,32},{4,36},{8,40},{12,44},{16,48},{20,52},{24,56},{28,60},{32,6... | collective-permute-start | bytes 12296 | tf_op jit(solution)/shard_map/ppermute | solution.py:350
  189.0 0.0 collective-permute-done.11
  189.0 1.7 collective-permute-start.6
  190.7 3.1 %collective-permute-start.5 = (f32[8,128]{1,0:T(8,128)S(1)}, f32[8,128]{1,0:T(8,128)S(1)}, u32[]{:S(2)}, u32[]{:S(2)}) collective-permute-start(f32[8,128]{1,0:T(8,128)S(1)} %add_add_fusion.1), channel_id=1, source_target_pairs={{0,16},{4,20},{8,24},{12,28},{16,0},{20,4},{24,8},{28,12},{32,48},... | collective-permute-start | bytes 12296 | tf_op jit(solution)/shard_map/ppermute | solution.py:350
  193.8 0.0 collective-permute-done.9
  193.8 0.0 collective-permute-done.7
  193.8 2.0 %collective-permute-done.5 = f32[8,128]{1,0:T(8,128)S(1)} collective-permute-done((f32[8,128]{1,0:T(8,128)S(1)}, f32[8,128]{1,0:T(8,128)S(1)}, u32[]{:S(2)}, u32[]{:S(2)}) %collective-permute-start.5) | collective-permute-done | bytes 4128 | tf_op jit(solution)/shard_map/ppermute | solution.py:350
  195.8 2.8 %collective-permute-done.4 = f32[8,128]{1,0:T(8,128)S(1)} collective-permute-done((f32[8,128]{1,0:T(8,128)S(1)}, f32[8,128]{1,0:T(8,128)S(1)}, u32[]{:S(2)}, u32[]{:S(2)}) %collective-permute-start.4) | collective-permute-done | bytes 4128 | tf_op jit(solution)/shard_map/ppermute | solution.py:350
  198.6 0.0 all-to-all-done.3.got_ref
  198.6 2.8 %normalize_updates.1 = (f32[16,128,256]{2,1,0:T(8,128)}, f32[16,128,256]{2,1,0:T(8,128)}) custom-call(f32[8,128]{1,0:T(8,128)S(1)} %add_add_fusion.square_ref, bf16[32,16,16,128]{3,2,1,0:T(8,128)(2,1)S(1)} %all-to-all-done.3.got_ref), custom_call_target="tpu_custom_call" | custom-call | tf_op jit(solution)/shard_map/normalize_updates/pallas_call | solution.py:322
  (19 shorter events, 0.1 us)
Async XLA Ops:
  0.6 1.2 copy-start.2
  1.9 1.2 copy-start.3
  3.1 0.7 copy-start.5
  3.8 0.7 copy-start.6
  49.2 1.3 copy-start
  50.6 4.8 %copy-start.9 = (bf16[1,128,2048]{2,1,0:T(8,128)(2,1)S(1)}, bf16[1,128,2048]{2,1,0:T(8,128)(2,1)}, u32[]{:S(2)}) copy-start(bf16[1,128,2048]{2,1,0:T(8,128)(2,1)} %param.9) | copy-start | bytes 1572868
  50.6 33.0 %all-to-all-start.1 = ((bf16[32,256,128]{2,1,0:T(8,128)(2,1)}), bf16[32,256,128]{2,1,0:T(8,128)(2,1)S(1)}, u32[]{:S(2)}, u32[]{:S(2)}) async-start(bf16[32,256,128]{2,1,0:T(8,128)(2,1)} %bitcast.38), calls=%async_computation.1 | async-start | bytes 4194304 | tf_op jit(solution)/shard_map/all_to_all | solution.py:354
  56.3 27.3 %copy-start.7 = (bf16[1,128,256]{2,1,0:T(8,128)(2,1)S(1)}, bf16[1,128,256]{2,1,0:T(8,128)(2,1)}, u32[]{:S(2)}) copy-start(bf16[1,128,256]{2,1,0:T(8,128)(2,1)} %param.10) | copy-start | bytes 196612
  56.3 27.3 %copy-start.8 = (bf16[1,128,256]{2,1,0:T(8,128)(2,1)S(1)}, bf16[1,128,256]{2,1,0:T(8,128)(2,1)}, u32[]{:S(2)}) copy-start(bf16[1,128,256]{2,1,0:T(8,128)(2,1)} %param.11) | copy-start | bytes 196612
  83.6 1.0 copy-start.4
  141.9 1.3 copy-start.1
  143.2 55.4 %all-to-all-start.3 = ((bf16[32,16,16,128]{3,2,1,0:T(8,128)(2,1)}), bf16[32,16,16,128]{3,2,1,0:T(8,128)(2,1)S(1)}, u32[]{:S(2)}, u32[]{:S(2)}) async-start(bf16[32,16,16,128]{3,2,1,0:T(8,128)(2,1)} %bitcast.40), calls=%async_computation.3 | async-start | bytes 4194304 | tf_op jit(solution)/shard_map/all_to_all | solution.py:354
  147.2 1.2 collective-permute-start
  148.5 4.5 %collective-permute-start.3 = (f32[8,128]{1,0:T(8,128)S(1)}, f32[8,128]{1,0:T(8,128)S(1)}, u32[]{:S(2)}, u32[]{:S(2)}) collective-permute-start(f32[8,128]{1,0:T(8,128)S(1)} %add.73), channel_id=1, source_target_pairs={{0,3},{1,0},{2,1},{3,2},{4,7},{5,4},{6,5},{7,6},{8,11},{9,8},{10,9... | collective-permute-start | bytes 12296 | tf_op jit(solution)/shard_map/ppermute | solution.py:348
  151.2 5.1 %collective-permute-start.2 = (f32[8,128]{1,0:T(8,128)S(1)}, f32[8,128]{1,0:T(8,128)S(1)}, u32[]{:S(2)}, u32[]{:S(2)}) collective-permute-start(f32[8,128]{1,0:T(8,128)S(1)} %add.73), channel_id=1, source_target_pairs={{0,2},{1,3},{2,0},{3,1},{4,6},{5,7},{6,4},{7,5},{8,10},{9,11},{10,... | collective-permute-start | bytes 12296 | tf_op jit(solution)/shard_map/ppermute | solution.py:348
  152.0 4.8 %collective-permute-start.1 = (f32[8,128]{1,0:T(8,128)S(1)}, f32[8,128]{1,0:T(8,128)S(1)}, u32[]{:S(2)}, u32[]{:S(2)}) collective-permute-start(f32[8,128]{1,0:T(8,128)S(1)} %add.73), channel_id=1, source_target_pairs={{0,1},{1,2},{2,3},{3,0},{4,5},{5,6},{6,7},{7,4},{8,9},{9,10},{10,1... | collective-permute-start | bytes 12296 | tf_op jit(solution)/shard_map/ppermute | solution.py:348
  156.9 16.9 %collective-permute-start.18 = (f32[8,128]{1,0:T(8,128)S(1)}, f32[8,128]{1,0:T(8,128)S(1)}, u32[]{:S(2)}, u32[]{:S(2)}) collective-permute-start(f32[8,128]{1,0:T(8,128)S(1)} %add_add_fusion.1), channel_id=1, source_target_pairs={{0,120},{4,124},{8,96},{12,100},{16,104},{20,108},{24,112},{28,116... | collective-permute-start | bytes 12296 | tf_op jit(solution)/shard_map/ppermute | solution.py:350
  162.1 17.0 %collective-permute-start.17 = (f32[8,128]{1,0:T(8,128)S(1)}, f32[8,128]{1,0:T(8,128)S(1)}, u32[]{:S(2)}, u32[]{:S(2)}) collective-permute-start(f32[8,128]{1,0:T(8,128)S(1)} %add_add_fusion.1), channel_id=1, source_target_pairs={{0,112},{4,116},{8,120},{12,124},{16,96},{20,100},{24,104},{28,108... | collective-permute-start | bytes 12296 | tf_op jit(solution)/shard_map/ppermute | solution.py:350
  163.1 16.0 %collective-permute-start.16 = (f32[8,128]{1,0:T(8,128)S(1)}, f32[8,128]{1,0:T(8,128)S(1)}, u32[]{:S(2)}, u32[]{:S(2)}) collective-permute-start(f32[8,128]{1,0:T(8,128)S(1)} %add_add_fusion.1), channel_id=1, source_target_pairs={{0,104},{4,108},{8,112},{12,116},{16,120},{20,124},{24,96},{28,100... | collective-permute-start | bytes 12296 | tf_op jit(solution)/shard_map/ppermute | solution.py:350
  164.0 17.8 %collective-permute-start.15 = (f32[8,128]{1,0:T(8,128)S(1)}, f32[8,128]{1,0:T(8,128)S(1)}, u32[]{:S(2)}, u32[]{:S(2)}) collective-permute-start(f32[8,128]{1,0:T(8,128)S(1)} %add_add_fusion.1), channel_id=1, source_target_pairs={{0,96},{4,100},{8,104},{12,108},{16,112},{20,116},{24,120},{28,124... | collective-permute-start | bytes 12296 | tf_op jit(solution)/shard_map/ppermute | solution.py:350
  164.6 18.7 %collective-permute-start.14 = (f32[8,128]{1,0:T(8,128)S(1)}, f32[8,128]{1,0:T(8,128)S(1)}, u32[]{:S(2)}, u32[]{:S(2)}) collective-permute-start(f32[8,128]{1,0:T(8,128)S(1)} %add_add_fusion.1), channel_id=1, source_target_pairs={{0,88},{4,92},{8,64},{12,68},{16,72},{20,76},{24,80},{28,84},{32,1... | collective-permute-start | bytes 12296 | tf_op jit(solution)/shard_map/ppermute | solution.py:350
  173.8 10.3 %collective-permute-start.13 = (f32[8,128]{1,0:T(8,128)S(1)}, f32[8,128]{1,0:T(8,128)S(1)}, u32[]{:S(2)}, u32[]{:S(2)}) collective-permute-start(f32[8,128]{1,0:T(8,128)S(1)} %add_add_fusion.1), channel_id=1, source_target_pairs={{0,80},{4,84},{8,88},{12,92},{16,64},{20,68},{24,72},{28,76},{32,1... | collective-permute-start | bytes 12296 | tf_op jit(solution)/shard_map/ppermute | solution.py:350
  179.0 7.2 %collective-permute-start.12 = (f32[8,128]{1,0:T(8,128)S(1)}, f32[8,128]{1,0:T(8,128)S(1)}, u32[]{:S(2)}, u32[]{:S(2)}) collective-permute-start(f32[8,128]{1,0:T(8,128)S(1)} %add_add_fusion.1), channel_id=1, source_target_pairs={{0,72},{4,76},{8,80},{12,84},{16,88},{20,92},{24,64},{28,68},{32,1... | collective-permute-start | bytes 12296 | tf_op jit(solution)/shard_map/ppermute | solution.py:350
  179.1 9.9 %collective-permute-start.11 = (f32[8,128]{1,0:T(8,128)S(1)}, f32[8,128]{1,0:T(8,128)S(1)}, u32[]{:S(2)}, u32[]{:S(2)}) collective-permute-start(f32[8,128]{1,0:T(8,128)S(1)} %add_add_fusion.1), channel_id=1, source_target_pairs={{0,64},{4,68},{8,72},{12,76},{16,80},{20,84},{24,88},{28,92},{32,9... | collective-permute-start | bytes 12296 | tf_op jit(solution)/shard_map/ppermute | solution.py:350
  181.8 8.9 %collective-permute-start.10 = (f32[8,128]{1,0:T(8,128)S(1)}, f32[8,128]{1,0:T(8,128)S(1)}, u32[]{:S(2)}, u32[]{:S(2)}) collective-permute-start(f32[8,128]{1,0:T(8,128)S(1)} %add_add_fusion.1), channel_id=1, source_target_pairs={{0,56},{4,60},{8,32},{12,36},{16,40},{20,44},{24,48},{28,52},{32,8... | collective-permute-start | bytes 12296 | tf_op jit(solution)/shard_map/ppermute | solution.py:350
  183.3 10.5 %collective-permute-start.9 = (f32[8,128]{1,0:T(8,128)S(1)}, f32[8,128]{1,0:T(8,128)S(1)}, u32[]{:S(2)}, u32[]{:S(2)}) collective-permute-start(f32[8,128]{1,0:T(8,128)S(1)} %add_add_fusion.1), channel_id=1, source_target_pairs={{0,48},{4,52},{8,56},{12,60},{16,32},{20,36},{24,40},{28,44},{32,8... | collective-permute-start | bytes 12296 | tf_op jit(solution)/shard_map/ppermute | solution.py:350
  184.1 9.7 %collective-permute-start.8 = (f32[8,128]{1,0:T(8,128)S(1)}, f32[8,128]{1,0:T(8,128)S(1)}, u32[]{:S(2)}, u32[]{:S(2)}) collective-permute-start(f32[8,128]{1,0:T(8,128)S(1)} %add_add_fusion.1), channel_id=1, source_target_pairs={{0,40},{4,44},{8,48},{12,52},{16,56},{20,60},{24,32},{28,36},{32,7... | collective-permute-start | bytes 12296 | tf_op jit(solution)/shard_map/ppermute | solution.py:350
  186.2 7.5 %collective-permute-start.7 = (f32[8,128]{1,0:T(8,128)S(1)}, f32[8,128]{1,0:T(8,128)S(1)}, u32[]{:S(2)}, u32[]{:S(2)}) collective-permute-start(f32[8,128]{1,0:T(8,128)S(1)} %add_add_fusion.1), channel_id=1, source_target_pairs={{0,32},{4,36},{8,40},{12,44},{16,48},{20,52},{24,56},{28,60},{32,6... | collective-permute-start | bytes 12296 | tf_op jit(solution)/shard_map/ppermute | solution.py:350
  189.0 4.8 %collective-permute-start.6 = (f32[8,128]{1,0:T(8,128)S(1)}, f32[8,128]{1,0:T(8,128)S(1)}, u32[]{:S(2)}, u32[]{:S(2)}) collective-permute-start(f32[8,128]{1,0:T(8,128)S(1)} %add_add_fusion.1), channel_id=1, source_target_pairs={{0,24},{4,28},{8,0},{12,4},{16,8},{20,12},{24,16},{28,20},{32,56},... | collective-permute-start | bytes 12296 | tf_op jit(solution)/shard_map/ppermute | solution.py:350
  190.7 5.1 %collective-permute-start.5 = (f32[8,128]{1,0:T(8,128)S(1)}, f32[8,128]{1,0:T(8,128)S(1)}, u32[]{:S(2)}, u32[]{:S(2)}) collective-permute-start(f32[8,128]{1,0:T(8,128)S(1)} %add_add_fusion.1), channel_id=1, source_target_pairs={{0,16},{4,20},{8,24},{12,28},{16,0},{20,4},{24,8},{28,12},{32,48},... | collective-permute-start | bytes 12296 | tf_op jit(solution)/shard_map/ppermute | solution.py:350
  193.8 4.8 %collective-permute-start.4 = (f32[8,128]{1,0:T(8,128)S(1)}, f32[8,128]{1,0:T(8,128)S(1)}, u32[]{:S(2)}, u32[]{:S(2)}) collective-permute-start(f32[8,128]{1,0:T(8,128)S(1)} %add_add_fusion.1), channel_id=1, source_target_pairs={{0,8},{4,12},{8,16},{12,20},{16,24},{20,28},{24,0},{28,4},{32,40},... | collective-permute-start | bytes 12296 | tf_op jit(solution)/shard_map/ppermute | solution.py:350

commit v3 on v2

v3 whole, which is shorter than its diff:
```python
import functools
import math

import jax
import jax.numpy as jnp
from jax import lax
from jax.experimental import pallas as pl
from jax.experimental.pallas import tpu as pltpu
from jax.sharding import PartitionSpec as P

HD = 128
SLICE = 16
HEADS = 2
KINDS = 2
MIB = 1024 * 1024


def nt(a, b):
    return lax.dot_general(a, b, (((1,), (1,)), ((), ())), preferred_element_type=jnp.float32)


def nn(a, b):
    return jnp.dot(a, b, preferred_element_type=jnp.float32)


def split_kernel(ids_ref, home_ref, keys_ref, values_ref, out_ref, inside, parts, in_sems, out_sems):
    blocks, tokens, width = keys_ref.shape
    groups = tokens // SLICE
    arrive = []
    for t in range(groups):
        for kind, src in enumerate((keys_ref, values_ref)):
            copy = pltpu.make_async_copy(
                src.at[:, pl.ds(t * SLICE, SLICE)], inside.at[t, kind], in_sems.at[t, kind]
            )
            copy.start()
            arrive.append(copy)
    line = lax.broadcasted_iota(jnp.int32, (SLICE, HD), 0)
    lane = lax.broadcasted_iota(jnp.int32, (SLICE, HD), 1)
    tag = jnp.zeros((SLICE, HD), jnp.int32)
    for k in range(ids_ref.shape[1]):
        storage = home_ref[ids_ref[0, k]]
        owner = lax.div(storage, blocks)
        tag = jnp.where((line == 0) & (lane == k), owner, tag)
        tag = jnp.where((line == 1) & (lane == k), storage - owner * blocks, tag)
    tag = tag.astype(jnp.float32).astype(jnp.bfloat16)
    leave = []
    for t in range(groups):
        for kind in range(KINDS):
            arrive[t * KINDS + kind].wait()
        for part in range(HEADS * KINDS):
            m = t * HEADS * KINDS + part
            h, kind = part // KINDS, part % KINDS
            parts[m, pl.ds(0, blocks)] = inside[t, kind, :, :, h * HD : (h + 1) * HD]
            parts[m, blocks] = tag
            copy = pltpu.make_async_copy(parts.at[m], out_ref.at[m], out_sems.at[m])
            copy.start()
            leave.append(copy)
    for copy in leave:
        copy.wait()


def split(block_ids, block_home, cart_keys, cart_values, count):
    blocks, tokens, width = cart_keys.shape
    groups = tokens // SLICE
    smem = pl.BlockSpec(memory_space=pltpu.SMEM)
    hbm = pl.BlockSpec(memory_space=pltpu.HBM)
    return pl.pallas_call(
        split_kernel,
        out_shape=jax.ShapeDtypeStruct((count, blocks + 1, SLICE, HD), jnp.bfloat16),
        in_specs=[smem, smem, hbm, hbm],
        out_specs=hbm,
        scratch_shapes=[
            pltpu.VMEM((groups, KINDS, blocks, SLICE, width), jnp.bfloat16),
            pltpu.VMEM((count, blocks + 1, SLICE, HD), jnp.bfloat16),
            pltpu.SemaphoreType.DMA((groups, KINDS)),
            pltpu.SemaphoreType.DMA((count,)),
        ],
        name="split_blocks",
    )(block_ids, block_home, cart_keys, cart_values)


def pick_kernel(index_ref, held_ref, out_ref):
    def step(n, carry):
        for u in range(16):
            out_ref[n * 16 + u] = held_ref[index_ref[n * 16 + u]]
        return carry

    lax.fori_loop(0, out_ref.shape[0] // 16, step, 0)


def pick(index, held):
    vmem = pl.BlockSpec(memory_space=pltpu.VMEM)
    return pl.pallas_call(
        pick_kernel,
        out_shape=jax.ShapeDtypeStruct((index.shape[0],) + held.shape[1:], jnp.bfloat16),
        in_specs=[pl.BlockSpec(memory_space=pltpu.SMEM), vmem],
        out_specs=vmem,
        compiler_params=pltpu.CompilerParams(vmem_limit_bytes=16 * MIB),
        name="pick_requested",
    )(index, held)


def attend_kernel(
    length_ref,
    kv_ref,
    q_ref,
    g_ref,
    own_k_ref,
    own_v_ref,
    out_ref,
    grad_q_ref,
    send_ref,
    score,
    expo,
    acc,
    q_rows,
    g_cols,
):
    used = length_ref[0]
    chunks = kv_ref.shape[0] // (HEADS * KINDS)
    chunk = kv_ref.shape[1]
    rows = q_rows.shape[0]
    queries = q_ref.shape[0]
    repeat = rows // queries
    own = own_k_ref.shape[0]
    scale = 1.0 / math.sqrt(HD)
    log2e = scale * math.log2(math.e)
    position = lax.rem(lax.broadcasted_iota(jnp.int32, (1, rows), 1), queries)
    row_used = position < used
    own_at = lax.broadcasted_iota(jnp.int32, (own, rows), 0)
    seen = (own_at <= position) & (own_at < used)
    for head in range(HEADS):
        lanes = slice(head * HD, (head + 1) * HD)
        own_k = own_k_ref[:, lanes]
        own_v = own_v_ref[:, lanes]
        at = lambda c, kind: (c * HEADS + head) * KINDS + kind
        for r in range(repeat):
            cols = slice((head * repeat + r) * HD, (head * repeat + r + 1) * HD)
            q_rows[r * queries : (r + 1) * queries] = q_ref[:, cols]
            g_cols[:, r * queries : (r + 1) * queries] = g_ref[:, cols].T
        own_s = jnp.where(seen, nt(own_k, q_rows[...]), -1e30)
        top = jnp.max(own_s.reshape(own // 8, 8, rows), axis=0)
        for c in range(chunks):
            s = nt(kv_ref[at(c, 0)], q_rows[...])
            score[c] = s
            top = jnp.maximum(top, jnp.max(s.reshape(chunk // 8, 8, rows), axis=0))
        top = jnp.max(top, axis=0, keepdims=True) * log2e
        e = jnp.exp2(own_s * log2e - top)
        total = jnp.sum(e.reshape(own // 8, 8, rows), axis=0)
        own_e = e.astype(jnp.bfloat16)
        acc[...] = nn(own_v.T, own_e)
        for c in range(chunks):
            e = jnp.exp2(score[c] * log2e - top)
            total = total + jnp.sum(e.reshape(chunk // 8, 8, rows), axis=0)
            low = e.astype(jnp.bfloat16)
            expo[c] = low
            acc[...] += nn(kv_ref[at(c, 1)].T, low)
        inv = 1.0 / jnp.sum(total, axis=0, keepdims=True)
        g = jnp.where(row_used, g_cols[...].astype(jnp.float32), 0.0)
        out = jnp.where(row_used, acc[...] * inv, 0.0)
        for r in range(repeat):
            cols = slice((head * repeat + r) * HD, (head * repeat + r + 1) * HD)
            out_ref[:, cols] = out[:, r * queries : (r + 1) * queries].T.astype(jnp.bfloat16)
        delta = jnp.sum(g * out, axis=0, keepdims=True) * inv
        gs = (g * inv).astype(jnp.bfloat16)
        ds = (own_e.astype(jnp.float32) * (nn(own_v, gs) - delta)).astype(jnp.bfloat16)
        acc[...] = nn(own_k.T, ds)
        for c in range(chunks):
            low = expo[c]
            send_ref[at(c, 1)] = nt(low, gs).astype(jnp.bfloat16)
            dp = nn(kv_ref[at(c, 1)], gs)
            ds = (low.astype(jnp.float32) * (dp - delta)).astype(jnp.bfloat16)
            send_ref[at(c, 0)] = (nn(ds, q_rows[...]) * scale).astype(jnp.bfloat16)
            acc[...] += nn(kv_ref[at(c, 0)].T, ds)
        grad = acc[...] * scale
        for r in range(repeat):
            cols = slice((head * repeat + r) * HD, (head * repeat + r + 1) * HD)
            grad_q_ref[:, cols] = grad[:, r * queries : (r + 1) * queries].T.astype(jnp.bfloat16)


def attend(length, kv, q, g, own_k, own_v):
    count, chunk, _ = kv.shape
    queries, width = q.shape
    rows = queries * width // (HEADS * HD)
    chunks = count // (HEADS * KINDS)
    vmem = pl.BlockSpec(memory_space=pltpu.VMEM)
    return pl.pallas_call(
        attend_kernel,
        out_shape=(
            jax.ShapeDtypeStruct(q.shape, jnp.bfloat16),
            jax.ShapeDtypeStruct(q.shape, jnp.bfloat16),
            jax.ShapeDtypeStruct(kv.shape, jnp.bfloat16),
        ),
        in_specs=[pl.BlockSpec(memory_space=pltpu.SMEM)] + [vmem] * 5,
        out_specs=(vmem, vmem, vmem),
        scratch_shapes=[
            pltpu.VMEM((chunks, chunk, rows), jnp.float32),
            pltpu.VMEM((chunks, chunk, rows), jnp.bfloat16),
            pltpu.VMEM((HD, rows), jnp.float32),
            pltpu.VMEM((rows, HD), jnp.bfloat16),
            pltpu.VMEM((HD, rows), jnp.bfloat16),
        ],
        compiler_params=pltpu.CompilerParams(vmem_limit_bytes=48 * MIB),
        cost_estimate=pl.CostEstimate(
            flops=12 * 2 * HD * rows * (chunks * chunk + queries),
            bytes_accessed=8 * MIB,
            transcendentals=HEADS * rows * chunks * chunk,
        ),
        name="attend_forward_backward",
    )(length, kv, q, g, own_k, own_v)


def add_kernel(index_ref, got_ref, out_ref, table):
    selected = index_ref.shape[1]
    owners, blocks = out_ref.shape[0], out_ref.shape[1] - 1
    table[...] = jnp.zeros_like(table)

    def step(n, carry):
        at = [index_ref[n, k] for k in range(selected)]
        sums = [table[at[k]] + got_ref[n, k].astype(jnp.float32) for k in range(selected)]
        for k in range(selected):
            table[at[k]] = sums[k]
        return carry

    lax.fori_loop(0, got_ref.shape[0], step, 0)

    def finish(n, squares):
        rows = table[pl.ds(n * blocks, blocks)]
        out_ref[n, pl.ds(0, blocks)] = rows.astype(jnp.bfloat16)
        return squares + jnp.sum((rows * rows).reshape(blocks * SLICE // 8, 8, HD), axis=0)

    squares = lax.fori_loop(0, owners, finish, jnp.zeros((8, HD), jnp.float32))
    high = squares.astype(jnp.bfloat16).astype(jnp.float32)
    tag = jnp.concatenate([high, squares - high], axis=0).astype(jnp.bfloat16)
    for n in range(owners):
        out_ref[n, blocks] = tag


def add_up(index, got, blk_dev):
    count = got.shape[0]
    vmem = pl.BlockSpec(memory_space=pltpu.VMEM)
    return pl.pallas_call(
        add_kernel,
        out_shape=jax.ShapeDtypeStruct((count, blk_dev + 1, SLICE, HD), jnp.bfloat16),
        in_specs=[pl.BlockSpec(memory_space=pltpu.SMEM), vmem],
        out_specs=vmem,
        scratch_shapes=[pltpu.VMEM((count * blk_dev, SLICE, HD), jnp.float32)],
        compiler_params=pltpu.CompilerParams(vmem_limit_bytes=24 * MIB),
        name="add_over_readers",
    )(index, got)


def finish_kernel(count, step, *refs):
    squares, (got_ref, key_ref, value_ref) = refs[:-3], refs[-3:]
    total = sum(jnp.sum(ref[...], axis=(0, 1), keepdims=True) for ref in squares)
    inv = 1.0 / jnp.sqrt(total / count + 1e-6)
    for m in range(got_ref.shape[0]):
        t, h, kind = m // 4, (m // 2) % 2, m % 2
        dst = (key_ref, value_ref)[kind]
        part = got_ref[m].astype(jnp.float32) * inv.reshape(1, 1, 1)
        dst[:, t * SLICE : (t + 1) * SLICE, h * HD : (h + 1) * HD] = part


def finish(squares, got, block_tok, width, count):
    slices, blocks = got.shape[0], got.shape[1] - 1
    step = 4
    shape = jax.ShapeDtypeStruct((blocks, block_tok, width), jnp.float32)
    spec = pl.BlockSpec((step, block_tok, width), lambda n: (n, 0, 0))
    return pl.pallas_call(
        functools.partial(finish_kernel, count, step),
        out_shape=(shape, shape),
        grid=(blocks // step,),
        in_specs=[pl.BlockSpec((8, HD), lambda n: (0, 0))] * len(squares)
        + [pl.BlockSpec((slices, step, SLICE, HD), lambda n: (0, n, 0, 0))],
        out_specs=(spec, spec),
        compiler_params=pltpu.CompilerParams(vmem_limit_bytes=24 * MIB),
        name="normalize_updates",
    )(*squares, got)


def swap(a):
    return lax.all_to_all(a, "wide", split_axis=0, concat_axis=0, tiled=True)


def local(
    queries,
    own_keys,
    own_values,
    cart_keys,
    cart_values,
    block_ids,
    block_home,
    query_len,
    grad_out,
):
    wide_count = lax.axis_size("wide")
    blk_dev, block_tok, width = cart_keys.shape
    selected = block_ids.shape[1]
    all_blocks = block_home.shape[0]
    held = swap(split(block_ids, block_home, cart_keys, cart_values, wide_count))
    asked = held[:, blk_dev, :2, :selected].astype(jnp.int32)
    owner, row = asked[:, 0], asked[:, 1]
    picked = pick(
        (owner * (blk_dev + 1) + row).reshape(-1),
        held.reshape(wide_count * (blk_dev + 1), SLICE, HD),
    )
    kv = swap(picked.reshape(wide_count, selected * SLICE, HD))
    attn_out, grad_queries, send = attend(
        query_len, kv, queries[0], grad_out[0], own_keys[0], own_values[0]
    )
    got = swap(send).reshape(wide_count, selected, SLICE, HD)
    back = swap(add_up(owner * blk_dev + row, got, blk_dev))
    squares = jnp.sum(
        back[:, blk_dev].astype(jnp.float32).reshape(2 * wide_count, SLICE // 2, HD), axis=0
    )
    mp = lax.axis_size("mp")
    shifts = [[(i, (i + d) % mp) for i in range(mp)] for d in range(1, mp)]
    squares = [squares] + [lax.ppermute(squares, "mp", pairs) for pairs in shifts]
    count = 2.0 * all_blocks * block_tok * width * mp
    key_update, value_update = finish(squares, back, block_tok, width, count)
    return (attn_out[None], grad_queries[None], key_update, value_update)


def solution(mesh):
    shared = P("wide", None, "mp")
    return jax.shard_map(
        local,
        mesh=mesh,
        in_specs=(shared, shared, shared, shared, shared, P("wide", None), P(), P("wide"), shared),
        out_specs=(shared, shared, shared, shared),
        check_vma=False,
    )
```

time: 202 us -> 175 us (0.87)
  starting transfers between devices: 44.9 us -> 8.65 us
  blocking collectives: 69.6 us -> 104 us
  local copies, waits for them, and re-layouts: 15.1 us -> 1.43 us
  Pallas kernels: 35.1 us -> 27.1 us
  waiting for transfers between devices: 35.2 us -> 32.2 us
    all_to_all x2 -> x3, blocking collectives: 69.6 us -> 104 us  [swap(): return lax.all_to_all(a, 'wide', split_axis=0, concat_axis=0, tiled=True)]
    ppermute x19 -> x3, starting transfers between devices: 36.7 us -> 4.49 us  [local(): lax.ppermute(squares, 'mp', pairs)]
    ppermute x19 -> x3, waiting for transfers between devices: 14.6 us -> 3.94 us  [local(): lax.ppermute(squares, 'mp', pairs)]
    unnamed x22 -> x10, local copies, waits for them, and re-layouts: 9.53 us -> 1.33 us
    all_to_all x2 -> x1, waiting for transfers between devices: 20.6 us -> 28.2 us  [swap(): return lax.all_to_all(a, 'wide', split_axis=0, concat_axis=0, tiled=True)]
    pallas_call x4, Pallas kernels: 30.4 us -> 23.6 us  [the longest x1 16.1 us: attend(): pl.pallas_call(attend_kernel, out_shape=(jax.ShapeDtypeStruct(q.shape, jn...]
    all_to_all x2 -> x1, starting transfers between devices: 8.19 us -> 4.16 us  [swap(): return lax.all_to_all(a, 'wide', split_axis=0, concat_axis=0, tiled=True)]
    another operation x2 -> x0, local copies, waits for them, and re-layouts: 2.95 us -> none  [heads_first(): a.reshape(length, HEADS, rows // length, HD).transpose(1, 2, 0, 3)]
  transfers between devices with their start and end apart: 21 -> 4, of which waited for: 8 -> 3; matrix products, arithmetic and copies ran while one was open for 4% -> 0% of each run, Pallas kernels for 0% -> 0%
where the time goes in v3:
time: 175 us
  blocking collectives  104 us (59%)
  waiting for transfers between devices  32.2 us (18%)
  Pallas kernels  27.1 us (15%)
  starting transfers between devices  8.65 us (5%)
    all_to_all x3, blocking collectives, swap(): return lax.all_to_all(a, 'wide', split_axis=0, concat_axis=0, tiled=True)  104 us
    all_to_all x1, waiting for transfers between devices, swap(): return lax.all_to_all(a, 'wide', split_axis=0, concat_axis=0, tiled=True)  28.2 us
    pallas_call x1, Pallas kernels, attend(): pl.pallas_call(attend_kernel, out_shape=(jax.ShapeDtypeStruct(q.shape, jn...  16.1 us
    ppermute x3, starting transfers between devices, local(): lax.ppermute(squares, 'mp', pairs)  4.49 us
    all_to_all x1, starting transfers between devices, swap(): return lax.all_to_all(a, 'wide', split_axis=0, concat_axis=0, tiled=True)  4.16 us
    ppermute x3, waiting for transfers between devices, local(): lax.ppermute(squares, 'mp', pairs)  3.94 us
    pallas_call x1, Pallas kernels, split(): pl.pallas_call(split_kernel, out_shape=jax.ShapeDtypeStruct((count, block...  3.56 us
  transfers between devices with their start and end apart: 4, of which 3 were waited for; matrix products, arithmetic and copies ran while one was open for 0% of the time, Pallas kernels for 0%

profile of v3, /device:TPU:0, one launch (start us, length us, event | category | flops | bytes accessed | tf_op | source)
XLA Modules:
  0.0 174.8 jit_solution(15087902263067460233)
XLA Ops:
  0.6 3.6 %split_blocks.1 = bf16[32,17,16,128]{3,2,1,0:T(8,128)(2,1)} custom-call(s32[1,16]{1,0:T(1,128)} %ids_ref.1, s32[512]{0:T(512)} %home_ref.1, bf16[16,128,256]{2,1,0:T(8,128)(2,1)} %keys_ref.1, bf16[16,128,256]{2,1,0:T(8,128)(2,1)} %values_ref.1), custom_call_target="tpu_custom_call" | custom-call | tf_op jit(solution)/shard_map/split_blocks/pallas_call | solution.py:67
  4.2 38.8 %all_to_all.20 = bf16[32,17,16,128]{3,2,1,0:T(8,128)(2,1)S(1)} all-to-all(bf16[32,17,16,128]{3,2,1,0:T(8,128)(2,1)} %split_blocks.1), channel_id=1, replica_groups=mesh['wide'=32,'mp'=4] {'wide'}, dimensions={0} | all-to-all | bytes 4456448 | tf_op jit(solution)/shard_map/all_to_all | solution.py:282
  43.0 0.1 add.13.index_ref
  43.1 1.3 pick_requested.1
  44.4 0.0 copy-start
  44.4 1.3 copy-done
  45.7 0.0 copy-start.1
  45.7 0.0 copy-start.2
  45.7 0.0 copy-start.3
  45.7 0.0 copy-start.4
  45.7 4.2 %all-to-all-start.1 = ((bf16[32,256,128]{2,1,0:T(8,128)(2,1)}), bf16[32,256,128]{2,1,0:T(8,128)(2,1)S(1)}, u32[]{:S(2)}, u32[]{:S(2)}) async-start(bf16[32,256,128]{2,1,0:T(8,128)(2,1)} %bitcast.21), calls=%async_computation.1 | async-start | bytes 4194304 | tf_op jit(solution)/shard_map/all_to_all | solution.py:282
  50.5 28.2 %all-to-all-done.1.kv_ref = bf16[32,256,128]{2,1,0:T(8,128)(2,1)S(1)} async-done(((bf16[32,256,128]{2,1,0:T(8,128)(2,1)}), bf16[32,256,128]{2,1,0:T(8,128)(2,1)S(1)}, u32[]{:S(2)}, u32[]{:S(2)}) %all-to-all-start.1) | async-done | bytes 2097184 | tf_op jit(solution)/shard_map/all_to_all | solution.py:282
  78.7 0.0 copy-done.1
  78.7 0.0 copy-done.2
  78.7 0.0 copy-done.3
  78.8 0.0 copy-done.4
  78.8 16.1 %attend_forward_backward.1 = (bf16[128,2048]{1,0:T(8,128)(2,1)}, bf16[128,2048]{1,0:T(8,128)(2,1)}, bf16[32,256,128]{2,1,0:T(8,128)(2,1)S(1)}) custom-call(s32[1]{0:T(128)S(6)} %copy.21.length_ref, bf16[32,256,128]{2,1,0:T(8,128)(2,1)S(1)} %all-to-all-done.1.kv_ref, bf16[128,2048]{1,0:T(8,128)(2,1)S(1)} %bitcast.23, bf16[128,2048]{1,0:T(8,128)(2,1)S(1)} %bitcast.24, ...), custom_call_target="tpu_custom_call" | custom-call | flops 6845104128 | bytes 8388608 | tf_op jit(solution)/shard_map/attend_forward_backward/pallas_call | solution.py:187
  94.9 31.1 %all_to_all.21 = bf16[32,256,128]{2,1,0:T(8,128)(2,1)S(1)} all-to-all(bf16[32,256,128]{2,1,0:T(8,128)(2,1)S(1)} %get-tuple-element.11), channel_id=1, replica_groups=mesh['wide'=32,'mp'=4] {'wide'}, dimensions={0} | all-to-all | bytes 4194304 | tf_op jit(solution)/shard_map/all_to_all | solution.py:282
  126.0 3.2 %add_over_readers.1 = bf16[32,17,16,128]{3,2,1,0:T(8,128)(2,1)S(1)} custom-call(s32[32,16]{1,0:T(8,128)S(1)} %get-tuple-element.14.index_ref, bf16[32,16,16,128]{3,2,1,0:T(8,128)(2,1)S(1)} %bitcast.22), custom_call_target="tpu_custom_call" | custom-call | tf_op jit(solution)/shard_map/add_over_readers/pallas_call | solution.py:242
  129.1 34.2 %all_to_all.22.refs_4_ = bf16[32,17,16,128]{3,2,1,0:T(8,128)(2,1)S(1)} all-to-all(bf16[32,17,16,128]{3,2,1,0:T(8,128)(2,1)S(1)} %add_over_readers.1), channel_id=1, replica_groups=mesh['wide'=32,'mp'=4] {'wide'}, dimensions={0} | all-to-all | bytes 4456448 | tf_op jit(solution)/shard_map/all_to_all | solution.py:282
  163.3 0.1 convert_reduce_fusion.refs_0_
  163.4 2.8 %collective-permute-start.2 = (f32[8,128]{1,0:T(8,128)S(1)}, f32[8,128]{1,0:T(8,128)S(1)}, u32[]{:S(2)}, u32[]{:S(2)}) collective-permute-start(f32[8,128]{1,0:T(8,128)S(1)} %convert_reduce_fusion.refs_0_), channel_id=1, source_target_pairs={{0,3},{1,0},{2,1},{3,2},{4,7},{5,4},{6,5},{7,6},{8,11},{9,8},{10,9... | collective-permute-start | bytes 12296 | tf_op jit(solution)/shard_map/ppermute | solution.py:318
  166.2 0.8 collective-permute-start.1
  167.0 0.9 collective-permute-start
  167.9 0.0 collective-permute-done.2.refs_3_
  167.9 3.4 %collective-permute-done.1.refs_2_ = f32[8,128]{1,0:T(8,128)S(1)} collective-permute-done((f32[8,128]{1,0:T(8,128)S(1)}, f32[8,128]{1,0:T(8,128)S(1)}, u32[]{:S(2)}, u32[]{:S(2)}) %collective-permute-start.1) | collective-permute-done | bytes 4128 | tf_op jit(solution)/shard_map/ppermute | solution.py:318
  171.3 0.5 collective-permute-done.refs_1_
  171.8 3.0 %normalize_updates.1 = (f32[16,128,256]{2,1,0:T(8,128)}, f32[16,128,256]{2,1,0:T(8,128)}) custom-call(f32[8,128]{1,0:T(8,128)S(1)} %convert_reduce_fusion.refs_0_, f32[8,128]{1,0:T(8,128)S(1)} %collective-permute-done.refs_1_, f32[8,128]{1,0:T(8,128)S(1)} %collective-permute-done.1.refs_2_, f32[8,128]{1,0:T(8,128)S(1)} %collective-permute-done.2.refs_3_, ...), custom_call_target="tpu_custom_call" | custom-call | tf_op jit(solution)/shard_map/normalize_updates/pallas_call | solution.py:269
  (4 shorter events, 0.0 us)
Async XLA Ops:
  44.4 1.3 copy-start
  45.7 33.1 %copy-start.1 = (bf16[1,128,2048]{2,1,0:T(8,128)(2,1)S(1)}, bf16[1,128,2048]{2,1,0:T(8,128)(2,1)}, u32[]{:S(2)}) copy-start(bf16[1,128,2048]{2,1,0:T(8,128)(2,1)} %param.9) | copy-start | bytes 1572868
  45.7 33.1 %copy-start.2 = (bf16[1,128,2048]{2,1,0:T(8,128)(2,1)S(1)}, bf16[1,128,2048]{2,1,0:T(8,128)(2,1)}, u32[]{:S(2)}) copy-start(bf16[1,128,2048]{2,1,0:T(8,128)(2,1)} %param.17) | copy-start | bytes 1572868
  45.7 33.1 %copy-start.3 = (bf16[1,128,256]{2,1,0:T(8,128)(2,1)S(1)}, bf16[1,128,256]{2,1,0:T(8,128)(2,1)}, u32[]{:S(2)}) copy-start(bf16[1,128,256]{2,1,0:T(8,128)(2,1)} %param.10) | copy-start | bytes 196612
  45.7 33.1 %copy-start.4 = (bf16[1,128,256]{2,1,0:T(8,128)(2,1)S(1)}, bf16[1,128,256]{2,1,0:T(8,128)(2,1)}, u32[]{:S(2)}) copy-start(bf16[1,128,256]{2,1,0:T(8,128)(2,1)} %param.11) | copy-start | bytes 196612
  45.7 33.1 %all-to-all-start.1 = ((bf16[32,256,128]{2,1,0:T(8,128)(2,1)}), bf16[32,256,128]{2,1,0:T(8,128)(2,1)S(1)}, u32[]{:S(2)}, u32[]{:S(2)}) async-start(bf16[32,256,128]{2,1,0:T(8,128)(2,1)} %bitcast.21), calls=%async_computation.1 | async-start | bytes 4194304 | tf_op jit(solution)/shard_map/all_to_all | solution.py:282
  163.4 4.5 %collective-permute-start.2 = (f32[8,128]{1,0:T(8,128)S(1)}, f32[8,128]{1,0:T(8,128)S(1)}, u32[]{:S(2)}, u32[]{:S(2)}) collective-permute-start(f32[8,128]{1,0:T(8,128)S(1)} %convert_reduce_fusion.refs_0_), channel_id=1, source_target_pairs={{0,3},{1,0},{2,1},{3,2},{4,7},{5,4},{6,5},{7,6},{8,11},{9,8},{10,9... | collective-permute-start | bytes 12296 | tf_op jit(solution)/shard_map/ppermute | solution.py:318
  166.2 5.1 %collective-permute-start.1 = (f32[8,128]{1,0:T(8,128)S(1)}, f32[8,128]{1,0:T(8,128)S(1)}, u32[]{:S(2)}, u32[]{:S(2)}) collective-permute-start(f32[8,128]{1,0:T(8,128)S(1)} %convert_reduce_fusion.refs_0_), channel_id=1, source_target_pairs={{0,2},{1,3},{2,0},{3,1},{4,6},{5,7},{6,4},{7,5},{8,10},{9,11},{10,... | collective-permute-start | bytes 12296 | tf_op jit(solution)/shard_map/ppermute | solution.py:318
  167.0 4.8 %collective-permute-start = (f32[8,128]{1,0:T(8,128)S(1)}, f32[8,128]{1,0:T(8,128)S(1)}, u32[]{:S(2)}, u32[]{:S(2)}) collective-permute-start(f32[8,128]{1,0:T(8,128)S(1)} %convert_reduce_fusion.refs_0_), channel_id=1, source_target_pairs={{0,1},{1,2},{2,3},{3,0},{4,5},{5,6},{6,7},{7,4},{8,9},{9,10},{10,1... | collective-permute-start | bytes 12296 | tf_op jit(solution)/shard_map/ppermute | solution.py:318

commit v4 on v3

v4 whole, which is shorter than its diff:
```python
import functools
import math

import jax
import jax.numpy as jnp
from jax import lax
from jax.experimental import pallas as pl
from jax.experimental.pallas import tpu as pltpu
from jax.sharding import PartitionSpec as P

HD = 128
HEADS = 2
KINDS = 2
MIB = 1024 * 1024

def nt(a, b):
    return lax.dot_general(a, b, (((1,), (1,)), ((), ())), preferred_element_type=jnp.float32)


def nn(a, b):
    return jnp.dot(a, b, preferred_element_type=jnp.float32)


def pack_kernel(asked_ref, keys_ref, values_ref, out_ref):
    def step(reader, carry):
        row = jnp.maximum(asked_ref[reader, 0, 0] - 1, 0)
        out_ref[reader, 0] = keys_ref[row]
        out_ref[reader, 1] = values_ref[row]
        return carry

    lax.fori_loop(0, out_ref.shape[0], step, 0)


def pack(asked, keys, values):
    vmem = pl.BlockSpec(memory_space=pltpu.VMEM)
    return pl.pallas_call(
        pack_kernel,
        out_shape=jax.ShapeDtypeStruct((asked.shape[0], KINDS) + keys.shape[1:], jnp.bfloat16),
        in_specs=[pl.BlockSpec(memory_space=pltpu.SMEM), vmem, vmem],
        out_specs=vmem,
        compiler_params=pltpu.CompilerParams(vmem_limit_bytes=16 * MIB),
        name="pack_slots",
    )(asked, keys, values)


def attend_kernel(
    length_ref,
    slot_ref,
    kv_ref,
    q_ref,
    g_ref,
    own_k_ref,
    own_v_ref,
    out_ref,
    grad_q_ref,
    send_ref,
    score,
    expo,
    acc,
    q_rows,
    g_cols,
):
    used = length_ref[0]
    chunks, chunk, _ = score.shape
    tokens = kv_ref.shape[2]
    pair = chunk // tokens
    rows = q_rows.shape[0]
    queries = q_ref.shape[0]
    repeat = rows // queries
    own = own_k_ref.shape[0]
    scale = 1.0 / math.sqrt(HD)
    log2e = scale * math.log2(math.e)
    position = lax.rem(lax.broadcasted_iota(jnp.int32, (1, rows), 1), queries)
    row_used = position < used
    own_at = lax.broadcasted_iota(jnp.int32, (own, rows), 0)
    seen = (own_at <= position) & (own_at < used)
    for head in range(HEADS):
        lanes = slice(head * HD, (head + 1) * HD)
        own_k = own_k_ref[:, lanes]
        own_v = own_v_ref[:, lanes]

        def read(c, kind):
            parts = [kv_ref[slot_ref[c * pair + n], kind, :, lanes] for n in range(pair)]
            return jnp.concatenate(parts, axis=0)

        def write(c, kind, value):
            for n in range(pair):
                part = value[n * tokens : (n + 1) * tokens].astype(jnp.bfloat16)
                send_ref[slot_ref[c * pair + n], kind, :, lanes] = part

        for r in range(repeat):
            cols = slice((head * repeat + r) * HD, (head * repeat + r + 1) * HD)
            q_rows[r * queries : (r + 1) * queries] = q_ref[:, cols]
            g_cols[:, r * queries : (r + 1) * queries] = g_ref[:, cols].T
        own_s = jnp.where(seen, nt(own_k, q_rows[...]), -1e30)
        top = jnp.max(own_s.reshape(own // 8, 8, rows), axis=0)
        for c in range(chunks):
            s = nt(read(c, 0), q_rows[...])
            score[c] = s
            top = jnp.maximum(top, jnp.max(s.reshape(chunk // 8, 8, rows), axis=0))
        top = jnp.max(top, axis=0, keepdims=True) * log2e
        e = jnp.exp2(own_s * log2e - top)
        total = jnp.sum(e.reshape(own // 8, 8, rows), axis=0)
        own_e = e.astype(jnp.bfloat16)
        acc[...] = nn(own_v.T, own_e)
        for c in range(chunks):
            e = jnp.exp2(score[c] * log2e - top)
            total = total + jnp.sum(e.reshape(chunk // 8, 8, rows), axis=0)
            low = e.astype(jnp.bfloat16)
            expo[c] = low
            acc[...] += nn(read(c, 1).T, low)
        inv = 1.0 / jnp.sum(total, axis=0, keepdims=True)
        g = jnp.where(row_used, g_cols[...].astype(jnp.float32), 0.0)
        out = jnp.where(row_used, acc[...] * inv, 0.0)
        for r in range(repeat):
            cols = slice((head * repeat + r) * HD, (head * repeat + r + 1) * HD)
            out_ref[:, cols] = out[:, r * queries : (r + 1) * queries].T.astype(jnp.bfloat16)
        delta = jnp.sum(g * out, axis=0, keepdims=True) * inv
        gs = (g * inv).astype(jnp.bfloat16)
        ds = (own_e.astype(jnp.float32) * (nn(own_v, gs) - delta)).astype(jnp.bfloat16)
        acc[...] = nn(own_k.T, ds)
        for c in range(chunks):
            low = expo[c]
            write(c, 1, nt(low, gs))
            dp = nn(read(c, 1), gs)
            ds = (low.astype(jnp.float32) * (dp - delta)).astype(jnp.bfloat16)
            write(c, 0, nn(ds, q_rows[...]) * scale)
            acc[...] += nn(read(c, 0).T, ds)
        grad = acc[...] * scale
        for r in range(repeat):
            cols = slice((head * repeat + r) * HD, (head * repeat + r + 1) * HD)
            grad_q_ref[:, cols] = grad[:, r * queries : (r + 1) * queries].T.astype(jnp.bfloat16)


def attend(length, slots, kv, q, g, own_k, own_v):
    chunk = 2 * kv.shape[2]
    queries, width = q.shape
    rows = queries * width // (HEADS * HD)
    chunks = slots.shape[0] * kv.shape[2] // chunk
    vmem = pl.BlockSpec(memory_space=pltpu.VMEM)
    return pl.pallas_call(
        attend_kernel,
        out_shape=(
            jax.ShapeDtypeStruct(q.shape, jnp.bfloat16),
            jax.ShapeDtypeStruct(q.shape, jnp.bfloat16),
            jax.ShapeDtypeStruct(kv.shape, jnp.bfloat16),
        ),
        in_specs=[pl.BlockSpec(memory_space=pltpu.SMEM)] * 2 + [vmem] * 5,
        out_specs=(vmem, vmem, vmem),
        scratch_shapes=[
            pltpu.VMEM((chunks, chunk, rows), jnp.float32),
            pltpu.VMEM((chunks, chunk, rows), jnp.bfloat16),
            pltpu.VMEM((HD, rows), jnp.float32),
            pltpu.VMEM((rows, HD), jnp.bfloat16),
            pltpu.VMEM((HD, rows), jnp.bfloat16),
        ],
        compiler_params=pltpu.CompilerParams(vmem_limit_bytes=44 * MIB),
        cost_estimate=pl.CostEstimate(
            flops=12 * 2 * HD * rows * (chunks * chunk + queries),
            bytes_accessed=8 * MIB,
            transcendentals=HEADS * rows * chunks * chunk,
        ),
        name="attend_forward_backward",
    )(length, slots, kv, q, g, own_k, own_v)


def add_kernel(asked_ref, got_ref, keys_ref, values_ref, squares_ref):
    sums = (keys_ref, values_ref)
    for ref in sums:
        ref[...] = jnp.zeros_like(ref)

    def step(reader, carry):
        asked = asked_ref[reader, 0, 0]

        @pl.when(asked > 0)
        def _():
            for kind, ref in enumerate(sums):
                ref[asked - 1] += got_ref[reader, kind].astype(jnp.float32)

        return carry

    lax.fori_loop(0, got_ref.shape[0], step, 0)
    blocks, tokens, width = keys_ref.shape

    def square(block, total):
        for ref in sums:
            rows = ref[block]
            total = total + jnp.sum((rows * rows).reshape(tokens // 8, 8, width), axis=0)
        return total

    total = lax.fori_loop(0, blocks, square, jnp.zeros((8, width), jnp.float32))
    total = jnp.sum(total, axis=0, keepdims=True)
    total = sum(total[:, n * HD : (n + 1) * HD] for n in range(width // HD))
    squares_ref[...] = jnp.broadcast_to(total[None], squares_ref.shape)


def add_up(asked, got, blocks, devices):
    vmem = pl.BlockSpec(memory_space=pltpu.VMEM)
    sums = jax.ShapeDtypeStruct((blocks,) + got.shape[2:], jnp.float32)
    return pl.pallas_call(
        add_kernel,
        out_shape=(sums, sums, jax.ShapeDtypeStruct((devices, 1, HD), jnp.float32)),
        in_specs=[pl.BlockSpec(memory_space=pltpu.SMEM), vmem],
        out_specs=(vmem, vmem, vmem),
        compiler_params=pltpu.CompilerParams(vmem_limit_bytes=24 * MIB),
        name="add_over_readers",
    )(asked, got)


def finish_kernel(count, squares_ref, keys_ref, values_ref, key_ref, value_ref):
    total = jnp.sum(jnp.sum(squares_ref[...], axis=0), axis=1, keepdims=True)
    inv = (1.0 / jnp.sqrt(total / count + 1e-6)).reshape(1, 1, 1)
    step = key_ref.shape[0]
    at = pl.ds(pl.program_id(0) * step, step)
    key_ref[...] = keys_ref[at] * inv
    value_ref[...] = values_ref[at] * inv


def finish(squares, keys, values, count):
    step = 2
    vmem = pl.BlockSpec(memory_space=pltpu.VMEM)
    shape = jax.ShapeDtypeStruct(keys.shape, jnp.float32)
    spec = pl.BlockSpec((step,) + keys.shape[1:], lambda n: (n, 0, 0))
    return pl.pallas_call(
        functools.partial(finish_kernel, count),
        out_shape=(shape, shape),
        grid=(keys.shape[0] // step,),
        in_specs=[vmem, vmem, vmem],
        out_specs=(spec, spec),
        compiler_params=pltpu.CompilerParams(vmem_limit_bytes=24 * MIB),
        name="normalize_updates",
    )(squares, keys, values)


def swap(a, axes="wide"):
    return lax.all_to_all(a, axes, split_axis=0, concat_axis=0, tiled=True)


def local(
    queries,
    own_keys,
    own_values,
    cart_keys,
    cart_values,
    block_ids,
    block_home,
    query_len,
    grad_out,
):
    wide_count, mp = lax.axis_size("wide"), lax.axis_size("mp")
    blk_dev = cart_keys.shape[0]
    lookup = block_ids[0][:, None] == jnp.arange(block_home.shape[0], dtype=jnp.int32)
    storage = jnp.sum(jnp.where(lookup, block_home[None, :], 0), axis=-1)
    slots, row = storage // blk_dev, storage % blk_dev
    mine = slots[None, :] == jnp.arange(wide_count, dtype=jnp.int32)[:, None]
    ask = jnp.sum(jnp.where(mine, row[None, :] + 1, 0), axis=1)
    asked = swap(jnp.broadcast_to(ask[:, None, None], (wide_count, 1, HD)))
    kv = swap(pack(asked, cart_keys, cart_values))
    attn_out, grad_queries, send = attend(
        query_len, slots, kv, queries[0], grad_out[0], own_keys[0], own_values[0]
    )
    keys, values, squares = add_up(asked, swap(send), blk_dev, wide_count * mp)
    squares = swap(squares, ("wide", "mp"))
    count = 2.0 * keys.size * wide_count * mp
    key_update, value_update = finish(squares, keys, values, count)
    return (attn_out[None], grad_queries[None], key_update, value_update)


def solution(mesh):
    shared = P("wide", None, "mp")
    return jax.shard_map(
        local,
        mesh=mesh,
        in_specs=(shared, shared, shared, shared, shared, P("wide", None), P(), P("wide"), shared),
        out_specs=(shared, shared, shared, shared),
        check_vma=False,
    )
```

time: 175 us -> 180 us (1.029)
  waiting for transfers between devices: 32.2 us -> 52 us
  blocking collectives: 104 us -> 88 us
  starting transfers between devices: 8.65 us -> 5.01 us
  local copies, waits for them, and re-layouts: 1.43 us -> 4.54 us
    all_to_all x1, waiting for transfers between devices: 28.2 us -> 52 us  [swap(): return lax.all_to_all(a, axes, split_axis=0, concat_axis=0, tiled=True)]
    all_to_all x3, blocking collectives: 104 us -> 88 us  [swap(): return lax.all_to_all(a, axes, split_axis=0, concat_axis=0, tiled=True)]
    ppermute x3 -> x0, starting transfers between devices: 4.49 us -> none  [local(): lax.ppermute(squares, 'mp', pairs)]
    ppermute x3 -> x0, waiting for transfers between devices: 3.94 us -> none  [local(): lax.ppermute(squares, 'mp', pairs)]
    unnamed x10 -> x14, local copies, waits for them, and re-layouts: 1.33 us -> 4.44 us
    pallas_call x4 -> x3, Pallas kernels: 11 us -> 8.35 us  [the longest x1 4.41 us: finish(): pl.pallas_call(functools.partial(finish_kernel, count), out_shape=(shape,...]
    pallas_call x1, Pallas kernels: 16.1 us -> 18.4 us  [attend(): pl.pallas_call(attend_kernel, out_shape=(jax.ShapeDtypeStruct(q.shape, jn...]
  transfers between devices with their start and end apart: 4 -> 1, of which waited for: 3 -> 1; matrix products, arithmetic and copies ran while one was open for 0% -> 0% of each run, Pallas kernels for 0% -> 0%
where the time goes in v4:
time: 180 us; the launch traced here: 179 us
  blocking collectives  88 us (49%)
  waiting for transfers between devices  52 us (29%)
  Pallas kernels  26.8 us (15%)
  starting transfers between devices  5.01 us (3%)
  local copies, waits for them, and re-layouts  4.54 us (3%)
    all_to_all x3, blocking collectives, swap(): return lax.all_to_all(a, axes, split_axis=0, concat_axis=0, tiled=True)  88 us
    all_to_all x1, waiting for transfers between devices, swap(): return lax.all_to_all(a, axes, split_axis=0, concat_axis=0, tiled=True)  52 us
    pallas_call x1, Pallas kernels, attend(): pl.pallas_call(attend_kernel, out_shape=(jax.ShapeDtypeStruct(q.shape, jn...  18.4 us
    all_to_all x1, starting transfers between devices, swap(): return lax.all_to_all(a, axes, split_axis=0, concat_axis=0, tiled=True)  5.01 us
    unnamed x14, local copies, waits for them, and re-layouts  4.44 us
    pallas_call x1, Pallas kernels, finish(): pl.pallas_call(functools.partial(finish_kernel, count), out_shape=(shape,...  4.41 us
  transfers between devices with their start and end apart: 1, of which 1 were waited for; matrix products, arithmetic and copies ran while one was open for 0% of the time, Pallas kernels for 0%

profile of v4, /device:TPU:0, one launch (start us, length us, event | category | flops | bytes accessed | tf_op | source)
XLA Modules:
  0.0 178.6 jit_solution(13704186412018521315)
XLA Ops:
  0.6 0.9 select_reduce_fusion
  1.5 0.1 select_reduce_fusion.1
  1.6 0.1 broadcast_in_dim.45
  1.7 15.6 %all_to_all.20.asked_ref = s32[32,1,128]{2,1,0:T(1,128)S(1)} all-to-all(s32[32,1,128]{2,1,0:T(1,128)S(1)} %broadcast_in_dim.45), channel_id=1, replica_groups=mesh['wide'=32,'mp'=4] {'wide'}, dimensions={0} | all-to-all | bytes 32768 | tf_op jit(solution)/shard_map/all_to_all | solution.py:236
  17.3 0.0 copy-start.1
  17.3 1.2 copy-done.1
  18.5 0.0 copy-start.2
  18.5 1.2 copy-done.2
  19.7 1.3 pack_slots.1
  21.1 0.0 copy-start
  21.1 2.0 %copy-done = bf16[32,2,128,256]{3,2,1,0:T(8,128)(2,1)} copy-done((bf16[32,2,128,256]{3,2,1,0:T(8,128)(2,1)}, bf16[32,2,128,256]{3,2,1,0:T(8,128)(2,1)S(1)}, u32[]{:S(2)}) %copy-start) | copy-done | bytes 4194328
  23.0 0.0 copy-start.3
  23.0 0.0 copy-start.4
  23.0 0.0 copy-start.5
  23.0 0.0 copy-start.6
  23.1 5.0 %all-to-all-start.1 = ((bf16[32,2,128,256]{3,2,1,0:T(8,128)(2,1)}), bf16[32,2,128,256]{3,2,1,0:T(8,128)(2,1)}, u32[]{:S(2)}, u32[]{:S(2)}) async-start(bf16[32,2,128,256]{3,2,1,0:T(8,128)(2,1)} %copy-done), calls=%async_computation.1 | async-start | bytes 8388608 | tf_op jit(solution)/shard_map/all_to_all | solution.py:236
  28.7 52.0 %all-to-all-done.1.kv_ref = bf16[32,2,128,256]{3,2,1,0:T(8,128)(2,1)} async-done(((bf16[32,2,128,256]{3,2,1,0:T(8,128)(2,1)}), bf16[32,2,128,256]{3,2,1,0:T(8,128)(2,1)}, u32[]{:S(2)}, u32[]{:S(2)}) %all-to-all-start.1) | async-done | bytes 4194336 | tf_op jit(solution)/shard_map/all_to_all | solution.py:236
  80.7 0.0 copy-done.3
  80.7 0.0 copy-done.4
  80.7 0.0 copy-done.5
  80.7 0.0 copy-done.6
  80.7 18.4 %attend_forward_backward.1 = (bf16[128,2048]{1,0:T(8,128)(2,1)}, bf16[128,2048]{1,0:T(8,128)(2,1)}, bf16[32,2,128,256]{3,2,1,0:T(8,128)(2,1)S(1)}) custom-call(s32[1]{0:T(128)S(6)} %copy.13.length_ref, s32[16]{0:T(128)S(1)} %get-tuple-element.21.slot_ref, bf16[32,2,128,256]{3,2,1,0:T(8,128)(2,1)} %all-to-all-done.1.kv_ref, bf16[128,2048]{1,0:T(8,128)(2,1)S(1)} %bitcast.7, ...), custom_call_target="tpu_custom_call" | custom-call | flops 6845104128 | bytes 8388608 | tf_op jit(solution)/shard_map/attend_forward_backward/pallas_call | solution.py:141
  99.2 56.9 %all_to_all.21.got_ref = bf16[32,2,128,256]{3,2,1,0:T(8,128)(2,1)S(1)} all-to-all(bf16[32,2,128,256]{3,2,1,0:T(8,128)(2,1)S(1)} %get-tuple-element.14), channel_id=1, replica_groups=mesh['wide'=32,'mp'=4] {'wide'}, dimensions={0} | all-to-all | bytes 8388608 | tf_op jit(solution)/shard_map/all_to_all | solution.py:236
  156.1 2.6 %add_over_readers.1 = (f32[16,128,256]{2,1,0:T(8,128)S(1)}, f32[16,128,256]{2,1,0:T(8,128)S(1)}, f32[128,1,128]{2,1,0:T(1,128)S(1)}) custom-call(s32[32,1,128]{2,1,0:T(1,128)S(1)} %all_to_all.20.asked_ref, bf16[32,2,128,256]{3,2,1,0:T(8,128)(2,1)S(1)} %all_to_all.21.got_ref), custom_call_target="tpu_custom_call" | custom-call | tf_op jit(solution)/shard_map/add_over_readers/pallas_call | solution.py:200
  158.7 15.5 %all_to_all.22.squares_ref = f32[128,1,128]{2,1,0:T(1,128)S(1)} all-to-all(f32[128,1,128]{2,1,0:T(1,128)S(1)} %get-tuple-element.15), channel_id=1, replica_groups=mesh['wide'=32,'mp'=4] {'wide','mp'}, dimensions={0} | all-to-all | bytes 131072 | tf_op jit(solution)/shard_map/all_to_all | solution.py:236
  174.2 4.4 %normalize_updates.1 = (f32[16,128,256]{2,1,0:T(8,128)}, f32[16,128,256]{2,1,0:T(8,128)}) custom-call(f32[128,1,128]{2,1,0:T(1,128)S(1)} %all_to_all.22.squares_ref, f32[16,128,256]{2,1,0:T(8,128)S(1)} %get-tuple-element.16.keys_ref, f32[16,128,256]{2,1,0:T(8,128)S(1)} %get-tuple-element.17.values_ref), custom_call_target="tpu_custom_call" | custom-call | tf_op jit(solution)/shard_map/normalize_updates/pallas_call | solution.py:224
  (1 shorter events, 0.0 us)
Async XLA Ops:
  17.3 1.2 copy-start.1
  18.5 1.2 copy-start.2
  21.1 2.0 %copy-start = (bf16[32,2,128,256]{3,2,1,0:T(8,128)(2,1)}, bf16[32,2,128,256]{3,2,1,0:T(8,128)(2,1)S(1)}, u32[]{:S(2)}) copy-start(bf16[32,2,128,256]{3,2,1,0:T(8,128)(2,1)S(1)} %pack_slots.1) | copy-start | bytes 12582916
  23.0 57.7 %copy-start.3 = (bf16[1,128,2048]{2,1,0:T(8,128)(2,1)S(1)}, bf16[1,128,2048]{2,1,0:T(8,128)(2,1)}, u32[]{:S(2)}) copy-start(bf16[1,128,2048]{2,1,0:T(8,128)(2,1)} %param.9) | copy-start | bytes 1572868
  23.0 57.7 %copy-start.4 = (bf16[1,128,2048]{2,1,0:T(8,128)(2,1)S(1)}, bf16[1,128,2048]{2,1,0:T(8,128)(2,1)}, u32[]{:S(2)}) copy-start(bf16[1,128,2048]{2,1,0:T(8,128)(2,1)} %param.17) | copy-start | bytes 1572868
  23.0 57.7 %copy-start.5 = (bf16[1,128,256]{2,1,0:T(8,128)(2,1)S(1)}, bf16[1,128,256]{2,1,0:T(8,128)(2,1)}, u32[]{:S(2)}) copy-start(bf16[1,128,256]{2,1,0:T(8,128)(2,1)} %param.10) | copy-start | bytes 196612
  23.0 57.7 %copy-start.6 = (bf16[1,128,256]{2,1,0:T(8,128)(2,1)S(1)}, bf16[1,128,256]{2,1,0:T(8,128)(2,1)}, u32[]{:S(2)}) copy-start(bf16[1,128,256]{2,1,0:T(8,128)(2,1)} %param.11) | copy-start | bytes 196612
  23.1 57.7 %all-to-all-start.1 = ((bf16[32,2,128,256]{3,2,1,0:T(8,128)(2,1)}), bf16[32,2,128,256]{3,2,1,0:T(8,128)(2,1)}, u32[]{:S(2)}, u32[]{:S(2)}) async-start(bf16[32,2,128,256]{3,2,1,0:T(8,128)(2,1)} %copy-done), calls=%async_computation.1 | async-start | bytes 8388608 | tf_op jit(solution)/shard_map/all_to_all | solution.py:236

commit v5 on v3

--- a/solution.py
+++ b/solution.py
@@ -10,6 +10,7 @@
 
 HD = 128
 SLICE = 16
+TAG = 8
 HEADS = 2
 KINDS = 2
 MIB = 1024 * 1024
@@ -23,7 +24,23 @@
     return jnp.dot(a, b, preferred_element_type=jnp.float32)
 
 
-def split_kernel(ids_ref, home_ref, keys_ref, values_ref, out_ref, inside, parts, in_sems, out_sems):
+def split_kernel(
+    ids_ref,
+    home_ref,
+    length_ref,
+    keys_ref,
+    values_ref,
+    out_ref,
+    used_ref,
+    inside,
+    parts,
+    ids,
+    home,
+    length,
+    in_sems,
+    out_sems,
+    list_sems,
+):
     blocks, tokens, width = keys_ref.shape
     groups = tokens // SLICE
     arrive = []
@@ -34,11 +51,20 @@
             )
             copy.start()
             arrive.append(copy)
+    lists = ((ids_ref, ids), (home_ref, home), (length_ref, length))
+    lists = [
+        pltpu.make_async_copy(src, dst, list_sems.at[n]) for n, (src, dst) in enumerate(lists)
+    ]
+    for copy in lists:
+        copy.start()
+    for copy in lists:
+        copy.wait()
+    used_ref[...] = jnp.full(used_ref.shape, length[0], jnp.int32)
     line = lax.broadcasted_iota(jnp.int32, (SLICE, HD), 0)
     lane = lax.broadcasted_iota(jnp.int32, (SLICE, HD), 1)
     tag = jnp.zeros((SLICE, HD), jnp.int32)
-    for k in range(ids_ref.shape[1]):
-        storage = home_ref[ids_ref[0, k]]
+    for k in range(ids.shape[1]):
+        storage = home[ids[0, k]]
         owner = lax.div(storage, blocks)
         tag = jnp.where((line == 0) & (lane == k), owner, tag)
         tag = jnp.where((line == 1) & (lane == k), storage - owner * blocks, tag)
@@ -59,24 +85,30 @@
         copy.wait()
 
 
-def split(block_ids, block_home, cart_keys, cart_values, count):
+def split(block_ids, block_home, length, cart_keys, cart_values, count):
     blocks, tokens, width = cart_keys.shape
     groups = tokens // SLICE
-    smem = pl.BlockSpec(memory_space=pltpu.SMEM)
     hbm = pl.BlockSpec(memory_space=pltpu.HBM)
     return pl.pallas_call(
         split_kernel,
-        out_shape=jax.ShapeDtypeStruct((count, blocks + 1, SLICE, HD), jnp.bfloat16),
-        in_specs=[smem, smem, hbm, hbm],
-        out_specs=hbm,
+        out_shape=(
+            jax.ShapeDtypeStruct((count, blocks + 1, SLICE, HD), jnp.bfloat16),
+            jax.ShapeDtypeStruct((8, HD), jnp.int32),
+        ),
+        in_specs=[hbm] * 5,
+        out_specs=(hbm, pl.BlockSpec(memory_space=pltpu.VMEM)),
         scratch_shapes=[
             pltpu.VMEM((groups, KINDS, blocks, SLICE, width), jnp.bfloat16),
             pltpu.VMEM((count, blocks + 1, SLICE, HD), jnp.bfloat16),
+            pltpu.SMEM(block_ids.shape, jnp.int32),
+            pltpu.SMEM(block_home.shape, jnp.int32),
+            pltpu.SMEM(length.shape, jnp.int32),
             pltpu.SemaphoreType.DMA((groups, KINDS)),
             pltpu.SemaphoreType.DMA((count,)),
+            pltpu.SemaphoreType.DMA((3,)),
         ],
         name="split_blocks",
-    )(block_ids, block_home, cart_keys, cart_values)
+    )(block_ids, block_home, length, cart_keys, cart_values)
 
 
 def pick_kernel(index_ref, held_ref, out_ref):
@@ -116,7 +148,7 @@
     q_rows,
     g_cols,
 ):
-    used = length_ref[0]
+    used = length_ref[0:1, 0:1]
     chunks = kv_ref.shape[0] // (HEADS * KINDS)
     chunk = kv_ref.shape[1]
     rows = q_rows.shape[0]
@@ -191,7 +223,7 @@
             jax.ShapeDtypeStruct(q.shape, jnp.bfloat16),
             jax.ShapeDtypeStruct(kv.shape, jnp.bfloat16),
         ),
-        in_specs=[pl.BlockSpec(memory_space=pltpu.SMEM)] + [vmem] * 5,
+        in_specs=[vmem] * 6,
         out_specs=(vmem, vmem, vmem),
         scratch_shapes=[
             pltpu.VMEM((chunks, chunk, rows), jnp.float32),
@@ -212,7 +244,8 @@
 
 def add_kernel(index_ref, got_ref, out_ref, table):
     selected = index_ref.shape[1]
-    owners, blocks = out_ref.shape[0], out_ref.shape[1] - 1
+    owners, held = out_ref.shape[0], out_ref.shape[1] - TAG
+    blocks = held // SLICE
     table[...] = jnp.zeros_like(table)
 
     def step(n, carry):
@@ -222,18 +255,19 @@
             table[at[k]] = sums[k]
         return carry
 
-    lax.fori_loop(0, got_ref.shape[0], step, 0)
+    lax.fori_loop(0, got_ref.shape[0], step, 0, unroll=4)
 
     def finish(n, squares):
-        rows = table[pl.ds(n * blocks, blocks)]
-        out_ref[n, pl.ds(0, blocks)] = rows.astype(jnp.bfloat16)
-        return squares + jnp.sum((rows * rows).reshape(blocks * SLICE // 8, 8, HD), axis=0)
-
-    squares = lax.fori_loop(0, owners, finish, jnp.zeros((8, HD), jnp.float32))
+        rows = table[pl.ds(n * blocks, blocks)].reshape(held, HD)
+        out_ref[n, pl.ds(0, held)] = rows.astype(jnp.bfloat16)
+        return squares + jnp.sum((rows * rows).reshape(held // 8, 8, HD), axis=0)
+
+    squares = lax.fori_loop(0, owners, finish, jnp.zeros((8, HD), jnp.float32), unroll=4)
+    squares = squares[: TAG // 2] + squares[TAG // 2 :]
     high = squares.astype(jnp.bfloat16).astype(jnp.float32)
     tag = jnp.concatenate([high, squares - high], axis=0).astype(jnp.bfloat16)
     for n in range(owners):
-        out_ref[n, blocks] = tag
+        out_ref[n, pl.ds(held, TAG)] = tag
 
 
 def add_up(index, got, blk_dev):
@@ -241,7 +275,7 @@
     vmem = pl.BlockSpec(memory_space=pltpu.VMEM)
     return pl.pallas_call(
         add_kernel,
-        out_shape=jax.ShapeDtypeStruct((count, blk_dev + 1, SLICE, HD), jnp.bfloat16),
+        out_shape=jax.ShapeDtypeStruct((count, blk_dev * SLICE + TAG, HD), jnp.bfloat16),
         in_specs=[pl.BlockSpec(memory_space=pltpu.SMEM), vmem],
         out_specs=vmem,
         scratch_shapes=[pltpu.VMEM((count * blk_dev, SLICE, HD), jnp.float32)],
@@ -250,29 +284,42 @@
     )(index, got)
 
 
-def finish_kernel(count, step, *refs):
-    squares, (got_ref, key_ref, value_ref) = refs[:-3], refs[-3:]
-    total = sum(jnp.sum(ref[...], axis=(0, 1), keepdims=True) for ref in squares)
+def finish_kernel(count, *refs):
+    squares, (got_ref, key_ref, value_ref, keys, values, sems) = refs[:-6], refs[-6:]
+    total = jnp.sum(sum(ref[...] for ref in squares), axis=(0, 1), keepdims=True)
     inv = 1.0 / jnp.sqrt(total / count + 1e-6)
-    for m in range(got_ref.shape[0]):
-        t, h, kind = m // 4, (m // 2) % 2, m % 2
-        dst = (key_ref, value_ref)[kind]
-        part = got_ref[m].astype(jnp.float32) * inv.reshape(1, 1, 1)
-        dst[:, t * SLICE : (t + 1) * SLICE, h * HD : (h + 1) * HD] = part
+    parts = sems.shape[0]
+    step = keys.shape[0] // parts
+    copies = []
+    for n in range(parts):
+        at = pl.ds(n * step, step)
+        for m in range(got_ref.shape[0]):
+            t, h, kind = m // 4, (m // 2) % 2, m % 2
+            part = got_ref[m, n * step * SLICE : (n + 1) * step * SLICE].astype(jnp.float32) * inv
+            part = part.reshape(step, SLICE, HD)
+            (keys, values)[kind][at, t * SLICE : (t + 1) * SLICE, h * HD : (h + 1) * HD] = part
+        for kind, (src, dst) in enumerate(((keys, key_ref), (values, value_ref))):
+            copies.append(pltpu.make_async_copy(src.at[at], dst.at[at], sems.at[n, kind]))
+            copies[-1].start()
+    for copy in copies:
+        copy.wait()
 
 
 def finish(squares, got, block_tok, width, count):
-    slices, blocks = got.shape[0], got.shape[1] - 1
-    step = 4
-    shape = jax.ShapeDtypeStruct((blocks, block_tok, width), jnp.float32)
-    spec = pl.BlockSpec((step, block_tok, width), lambda n: (n, 0, 0))
-    return pl.pallas_call(
-        functools.partial(finish_kernel, count, step),
-        out_shape=(shape, shape),
-        grid=(blocks // step,),
-        in_specs=[pl.BlockSpec((8, HD), lambda n: (0, 0))] * len(squares)
-        + [pl.BlockSpec((slices, step, SLICE, HD), lambda n: (0, n, 0, 0))],
-        out_specs=(spec, spec),
+    blocks = (got.shape[1] - TAG) // SLICE
+    vmem = pl.BlockSpec(memory_space=pltpu.VMEM)
+    hbm = pl.BlockSpec(memory_space=pltpu.HBM)
+    shape = (blocks, block_tok, width)
+    return pl.pallas_call(
+        functools.partial(finish_kernel, count),
+        out_shape=(jax.ShapeDtypeStruct(shape, jnp.float32),) * 2,
+        in_specs=[vmem] * (len(squares) + 1),
+        out_specs=(hbm, hbm),
+        scratch_shapes=[
+            pltpu.VMEM(shape, jnp.float32),
+            pltpu.VMEM(shape, jnp.float32),
+            pltpu.SemaphoreType.DMA((4, KINDS)),
+        ],
         compiler_params=pltpu.CompilerParams(vmem_limit_bytes=24 * MIB),
         name="normalize_updates",
     )(*squares, got)
@@ -297,7 +344,8 @@
     blk_dev, block_tok, width = cart_keys.shape
     selected = block_ids.shape[1]
     all_blocks = block_home.shape[0]
-    held = swap(split(block_ids, block_home, cart_keys, cart_values, wide_count))
+    parts, used = split(block_ids, block_home, query_len, cart_keys, cart_values, wide_count)
+    held = swap(parts)
     asked = held[:, blk_dev, :2, :selected].astype(jnp.int32)
     owner, row = asked[:, 0], asked[:, 1]
     picked = pick(
@@ -306,13 +354,11 @@
     )
     kv = swap(picked.reshape(wide_count, selected * SLICE, HD))
     attn_out, grad_queries, send = attend(
-        query_len, kv, queries[0], grad_out[0], own_keys[0], own_values[0]
+        used, kv, queries[0], grad_out[0], own_keys[0], own_values[0]
     )
     got = swap(send).reshape(wide_count, selected, SLICE, HD)
     back = swap(add_up(owner * blk_dev + row, got, blk_dev))
-    squares = jnp.sum(
-        back[:, blk_dev].astype(jnp.float32).reshape(2 * wide_count, SLICE // 2, HD), axis=0
-    )
+    squares = jnp.sum(back[:, -TAG:].astype(jnp.float32), axis=0)
     mp = lax.axis_size("mp")
     shifts = [[(i, (i + d) % mp) for i in range(mp)] for d in range(1, mp)]
     squares = [squares] + [lax.ppermute(squares, "mp", pairs) for pairs in shifts]

time: 175 us -> 172 us (0.983)
  blocking collectives: 104 us -> 136 us
  waiting for transfers between devices: 32.2 us -> 3.93 us
  starting transfers between devices: 8.65 us -> 4.51 us
    all_to_all x3 -> x4, blocking collectives: 104 us -> 136 us  [swap(): return lax.all_to_all(a, 'wide', split_axis=0, concat_axis=0, tiled=True)]
    all_to_all x1 -> x0, waiting for transfers between devices: 28.2 us -> none  [swap(): return lax.all_to_all(a, 'wide', split_axis=0, concat_axis=0, tiled=True)]
    all_to_all x1 -> x0, starting transfers between devices: 4.16 us -> none  [swap(): return lax.all_to_all(a, 'wide', split_axis=0, concat_axis=0, tiled=True)]
  transfers between devices with their start and end apart: 4 -> 3, of which waited for: 3 -> 2; matrix products, arithmetic and copies ran while one was open for 0% -> 0% of each run, Pallas kernels for 0% -> 0%
where the time goes in v5:
time: 172 us
  blocking collectives  136 us (79%)
  Pallas kernels  25.5 us (15%)
  starting transfers between devices  4.51 us (3%)
  waiting for transfers between devices  3.93 us (2%)
    all_to_all x4, blocking collectives, swap(): return lax.all_to_all(a, 'wide', split_axis=0, concat_axis=0, tiled=True)  136 us
    pallas_call x1, Pallas kernels, attend(): pl.pallas_call(attend_kernel, out_shape=(jax.ShapeDtypeStruct(q.shape, jn...  16.2 us
    ppermute x3, starting transfers between devices, local(): lax.ppermute(squares, 'mp', pairs)  4.51 us
    ppermute x3, waiting for transfers between devices, local(): lax.ppermute(squares, 'mp', pairs)  3.93 us
    pallas_call x1, Pallas kernels, split(): pl.pallas_call(split_kernel, out_shape=(jax.ShapeDtypeStruct((count, bloc...  3.48 us
  transfers between devices with their start and end apart: 3, of which 2 were waited for; matrix products, arithmetic and copies ran while one was open for 0% of the time, Pallas kernels for 0%

profile of v5, /device:TPU:0, one launch (start us, length us, event | category | flops | bytes accessed | tf_op | source)
XLA Modules:
  0.0 171.5 jit_solution(366323019306665272)
XLA Ops:
  1.3 3.5 %split_blocks.1 = (bf16[32,17,16,128]{3,2,1,0:T(8,128)(2,1)}, s32[8,128]{1,0:T(8,128)}) custom-call(s32[1,16]{1,0:T(1,128)} %ids_ref.1, s32[512]{0:T(512)} %home_ref.1, s32[1]{0:T(128)S(6)} %copy.21.length_ref, bf16[16,128,256]{2,1,0:T(8,128)(2,1)} %keys_ref.1, bf16[16,128,256]{2,1,0:T(8,128)(2,1)} %values_ref.1), custom_call_target="tpu_custom_call" | custom-call | tf_op jit(solution)/shard_map/split_blocks/pallas_call | solution.py:92
  4.8 38.8 %all_to_all.20 = bf16[32,17,16,128]{3,2,1,0:T(8,128)(2,1)S(1)} all-to-all(bf16[32,17,16,128]{3,2,1,0:T(8,128)(2,1)} %get-tuple-element.12), channel_id=1, replica_groups=mesh['wide'=32,'mp'=4] {'wide'}, dimensions={0} | all-to-all | bytes 4456448 | tf_op jit(solution)/shard_map/all_to_all | solution.py:329
  43.6 0.1 add.13.index_ref
  43.7 1.3 pick_requested.1
  44.9 0.0 copy-start
  44.9 0.0 copy-start.1
  44.9 0.0 copy-start.2
  45.0 0.0 copy-start.3
  45.0 0.0 copy-start.4
  45.0 31.6 %all_to_all.21.kv_ref = bf16[32,256,128]{2,1,0:T(8,128)(2,1)S(1)} all-to-all(bf16[32,256,128]{2,1,0:T(8,128)(2,1)S(1)} %bitcast.20), channel_id=1, replica_groups=mesh['wide'=32,'mp'=4] {'wide'}, dimensions={0} | all-to-all | bytes 4194304 | tf_op jit(solution)/shard_map/all_to_all | solution.py:329
  76.6 0.0 copy-done
  76.6 0.0 copy-done.1
  76.6 0.0 copy-done.2
  76.6 0.0 copy-done.3
  76.6 0.0 copy-done.4
  76.6 16.2 %attend_forward_backward.1 = (bf16[128,2048]{1,0:T(8,128)(2,1)}, bf16[128,2048]{1,0:T(8,128)(2,1)}, bf16[32,256,128]{2,1,0:T(8,128)(2,1)S(1)}) custom-call(s32[8,128]{1,0:T(8,128)S(1)} %copy-done.4, bf16[32,256,128]{2,1,0:T(8,128)(2,1)S(1)} %all_to_all.21.kv_ref, bf16[128,2048]{1,0:T(8,128)(2,1)S(1)} %bitcast.21, bf16[128,2048]{1,0:T(8,128)(2,1)S(1)} %bitcast.22, ...), custom_call_target="tpu_custom_call" | custom-call | flops 6845104128 | bytes 8388608 | tf_op jit(solution)/shard_map/attend_forward_backward/pallas_call | solution.py:219
  92.8 31.9 %all_to_all.22 = bf16[32,256,128]{2,1,0:T(8,128)(2,1)S(1)} all-to-all(bf16[32,256,128]{2,1,0:T(8,128)(2,1)S(1)} %get-tuple-element.15), channel_id=1, replica_groups=mesh['wide'=32,'mp'=4] {'wide'}, dimensions={0} | all-to-all | bytes 4194304 | tf_op jit(solution)/shard_map/all_to_all | solution.py:329
  124.7 2.3 %add_over_readers.1 = bf16[32,264,128]{2,1,0:T(8,128)(2,1)S(1)} custom-call(s32[32,16]{1,0:T(8,128)S(1)} %get-tuple-element.18.index_ref, bf16[32,16,16,128]{3,2,1,0:T(8,128)(2,1)S(1)} %bitcast.19), custom_call_target="tpu_custom_call" | custom-call | tf_op jit(solution)/shard_map/add_over_readers/pallas_call | solution.py:276
  127.0 33.7 %all_to_all.23.refs_4_ = bf16[32,264,128]{2,1,0:T(8,128)(2,1)S(1)} all-to-all(bf16[32,264,128]{2,1,0:T(8,128)(2,1)S(1)} %add_over_readers.1), channel_id=1, replica_groups=mesh['wide'=32,'mp'=4] {'wide'}, dimensions={0} | all-to-all | bytes 4325376 | tf_op jit(solution)/shard_map/all_to_all | solution.py:329
  160.7 2.8 %collective-permute-start.2 = (f32[8,128]{1,0:T(8,128)S(1)}, f32[8,128]{1,0:T(8,128)S(1)}, u32[]{:S(2)}, u32[]{:S(2)}) collective-permute-start(f32[8,128]{1,0:T(8,128)S(1)} %convert_reduce_fusion.refs_0_), channel_id=1, source_target_pairs={{0,3},{1,0},{2,1},{3,2},{4,7},{5,4},{6,5},{7,6},{8,11},{9,8},{10,9... | collective-permute-start | bytes 12296 | tf_op jit(solution)/shard_map/ppermute | solution.py:364
  163.5 0.8 collective-permute-start.1
  164.3 0.9 collective-permute-start
  165.2 0.0 collective-permute-done.2.refs_3_
  165.2 3.4 %collective-permute-done.1.refs_2_ = f32[8,128]{1,0:T(8,128)S(1)} collective-permute-done((f32[8,128]{1,0:T(8,128)S(1)}, f32[8,128]{1,0:T(8,128)S(1)}, u32[]{:S(2)}, u32[]{:S(2)}) %collective-permute-start.1) | collective-permute-done | bytes 4128 | tf_op jit(solution)/shard_map/ppermute | solution.py:364
  168.6 0.5 collective-permute-done.refs_1_
  169.1 2.3 %normalize_updates.1 = (f32[16,128,256]{2,1,0:T(8,128)}, f32[16,128,256]{2,1,0:T(8,128)}) custom-call(f32[8,128]{1,0:T(8,128)S(1)} %convert_reduce_fusion.refs_0_, f32[8,128]{1,0:T(8,128)S(1)} %collective-permute-done.refs_1_, f32[8,128]{1,0:T(8,128)S(1)} %collective-permute-done.1.refs_2_, f32[8,128]{1,0:T(8,128)S(1)} %collective-permute-done.2.refs_3_, ...), custom_call_target="tpu_custom_call" | custom-call | tf_op jit(solution)/shard_map/normalize_updates/pallas_call | solution.py:313
  (4 shorter events, 0.1 us)
Async XLA Ops:
  44.9 31.7 %copy-start = (bf16[1,128,2048]{2,1,0:T(8,128)(2,1)S(1)}, bf16[1,128,2048]{2,1,0:T(8,128)(2,1)}, u32[]{:S(2)}) copy-start(bf16[1,128,2048]{2,1,0:T(8,128)(2,1)} %param.9) | copy-start | bytes 1572868
  44.9 31.6 %copy-start.1 = (bf16[1,128,2048]{2,1,0:T(8,128)(2,1)S(1)}, bf16[1,128,2048]{2,1,0:T(8,128)(2,1)}, u32[]{:S(2)}) copy-start(bf16[1,128,2048]{2,1,0:T(8,128)(2,1)} %param.17) | copy-start | bytes 1572868
  44.9 31.6 %copy-start.2 = (bf16[1,128,256]{2,1,0:T(8,128)(2,1)S(1)}, bf16[1,128,256]{2,1,0:T(8,128)(2,1)}, u32[]{:S(2)}) copy-start(bf16[1,128,256]{2,1,0:T(8,128)(2,1)} %param.10) | copy-start | bytes 196612
  45.0 31.6 %copy-start.3 = (bf16[1,128,256]{2,1,0:T(8,128)(2,1)S(1)}, bf16[1,128,256]{2,1,0:T(8,128)(2,1)}, u32[]{:S(2)}) copy-start(bf16[1,128,256]{2,1,0:T(8,128)(2,1)} %param.11) | copy-start | bytes 196612
  45.0 31.6 %copy-start.4 = (s32[8,128]{1,0:T(8,128)S(1)}, s32[8,128]{1,0:T(8,128)}, u32[]{:S(2)}) copy-start(s32[8,128]{1,0:T(8,128)} %get-tuple-element.11.length_ref) | copy-start | bytes 12292
  160.7 4.5 %collective-permute-start.2 = (f32[8,128]{1,0:T(8,128)S(1)}, f32[8,128]{1,0:T(8,128)S(1)}, u32[]{:S(2)}, u32[]{:S(2)}) collective-permute-start(f32[8,128]{1,0:T(8,128)S(1)} %convert_reduce_fusion.refs_0_), channel_id=1, source_target_pairs={{0,3},{1,0},{2,1},{3,2},{4,7},{5,4},{6,5},{7,6},{8,11},{9,8},{10,9... | collective-permute-start | bytes 12296 | tf_op jit(solution)/shard_map/ppermute | solution.py:364
  163.5 5.1 %collective-permute-start.1 = (f32[8,128]{1,0:T(8,128)S(1)}, f32[8,128]{1,0:T(8,128)S(1)}, u32[]{:S(2)}, u32[]{:S(2)}) collective-permute-start(f32[8,128]{1,0:T(8,128)S(1)} %convert_reduce_fusion.refs_0_), channel_id=1, source_target_pairs={{0,2},{1,3},{2,0},{3,1},{4,6},{5,7},{6,4},{7,5},{8,10},{9,11},{10,... | collective-permute-start | bytes 12296 | tf_op jit(solution)/shard_map/ppermute | solution.py:364
  164.3 4.8 %collective-permute-start = (f32[8,128]{1,0:T(8,128)S(1)}, f32[8,128]{1,0:T(8,128)S(1)}, u32[]{:S(2)}, u32[]{:S(2)}) collective-permute-start(f32[8,128]{1,0:T(8,128)S(1)} %convert_reduce_fusion.refs_0_), channel_id=1, source_target_pairs={{0,1},{1,2},{2,3},{3,0},{4,5},{5,6},{6,7},{7,4},{8,9},{9,10},{10,1... | collective-permute-start | bytes 12296 | tf_op jit(solution)/shard_map/ppermute | solution.py:364

commit v6 on v5

--- a/solution.py
+++ b/solution.py
@@ -139,9 +139,10 @@
     g_ref,
     own_k_ref,
     own_v_ref,
+    send_ref,
     out_ref,
-    grad_q_ref,
-    send_ref,
+    slope_ref,
+    own_slope_ref,
     score,
     expo,
     acc,
@@ -190,24 +191,18 @@
         inv = 1.0 / jnp.sum(total, axis=0, keepdims=True)
         g = jnp.where(row_used, g_cols[...].astype(jnp.float32), 0.0)
         out = jnp.where(row_used, acc[...] * inv, 0.0)
-        for r in range(repeat):
-            cols = slice((head * repeat + r) * HD, (head * repeat + r + 1) * HD)
-            out_ref[:, cols] = out[:, r * queries : (r + 1) * queries].T.astype(jnp.bfloat16)
+        out_ref[head] = out
         delta = jnp.sum(g * out, axis=0, keepdims=True) * inv
         gs = (g * inv).astype(jnp.bfloat16)
-        ds = (own_e.astype(jnp.float32) * (nn(own_v, gs) - delta)).astype(jnp.bfloat16)
-        acc[...] = nn(own_k.T, ds)
+        ds = own_e.astype(jnp.float32) * (nn(own_v, gs) - delta)
+        own_slope_ref[head] = ds.astype(jnp.bfloat16)
         for c in range(chunks):
             low = expo[c]
             send_ref[at(c, 1)] = nt(low, gs).astype(jnp.bfloat16)
             dp = nn(kv_ref[at(c, 1)], gs)
             ds = (low.astype(jnp.float32) * (dp - delta)).astype(jnp.bfloat16)
+            slope_ref[head, c] = ds
             send_ref[at(c, 0)] = (nn(ds, q_rows[...]) * scale).astype(jnp.bfloat16)
-            acc[...] += nn(kv_ref[at(c, 0)].T, ds)
-        grad = acc[...] * scale
-        for r in range(repeat):
-            cols = slice((head * repeat + r) * HD, (head * repeat + r + 1) * HD)
-            grad_q_ref[:, cols] = grad[:, r * queries : (r + 1) * queries].T.astype(jnp.bfloat16)
 
 
 def attend(length, kv, q, g, own_k, own_v):
@@ -219,12 +214,13 @@
     return pl.pallas_call(
         attend_kernel,
         out_shape=(
-            jax.ShapeDtypeStruct(q.shape, jnp.bfloat16),
-            jax.ShapeDtypeStruct(q.shape, jnp.bfloat16),
             jax.ShapeDtypeStruct(kv.shape, jnp.bfloat16),
+            jax.ShapeDtypeStruct((HEADS, HD, rows), jnp.float32),
+            jax.ShapeDtypeStruct((HEADS, chunks, chunk, rows), jnp.bfloat16),
+            jax.ShapeDtypeStruct((HEADS, own_k.shape[0], rows), jnp.bfloat16),
         ),
         in_specs=[vmem] * 6,
-        out_specs=(vmem, vmem, vmem),
+        out_specs=(vmem,) * 4,
         scratch_shapes=[
             pltpu.VMEM((chunks, chunk, rows), jnp.float32),
             pltpu.VMEM((chunks, chunk, rows), jnp.bfloat16),
@@ -232,14 +228,52 @@
             pltpu.VMEM((rows, HD), jnp.bfloat16),
             pltpu.VMEM((HD, rows), jnp.bfloat16),
         ],
-        compiler_params=pltpu.CompilerParams(vmem_limit_bytes=48 * MIB),
+        compiler_params=pltpu.CompilerParams(vmem_limit_bytes=36 * MIB),
         cost_estimate=pl.CostEstimate(
-            flops=12 * 2 * HD * rows * (chunks * chunk + queries),
+            flops=10 * 2 * HD * rows * (chunks * chunk + queries),
             bytes_accessed=8 * MIB,
             transcendentals=HEADS * rows * chunks * chunk,
         ),
         name="attend_forward_backward",
     )(length, kv, q, g, own_k, own_v)
+
+
+def rows_kernel(kv_ref, own_k_ref, out_t_ref, slope_ref, own_slope_ref, out_ref, grad_q_ref):
+    chunks = slope_ref.shape[1]
+    rows = out_t_ref.shape[2]
+    queries = out_ref.shape[0]
+    repeat = rows // queries
+    scale = 1.0 / math.sqrt(HD)
+    for head in range(HEADS):
+        own_k = own_k_ref[:, head * HD : (head + 1) * HD]
+        grad = nn(own_k.T, own_slope_ref[head])
+        for c in range(chunks):
+            grad += nn(kv_ref[(c * HEADS + head) * KINDS].T, slope_ref[head, c])
+        grad = grad * scale
+        out = out_t_ref[head]
+        for r in range(repeat):
+            cols = slice((head * repeat + r) * HD, (head * repeat + r + 1) * HD)
+            at = slice(r * queries, (r + 1) * queries)
+            out_ref[:, cols] = out[:, at].T.astype(jnp.bfloat16)
+            grad_q_ref[:, cols] = grad[:, at].T.astype(jnp.bfloat16)
+
+
+def query_rows(kv, own_k, out_t, slope, own_slope, queries, width):
+    vmem = pl.BlockSpec(memory_space=pltpu.VMEM)
+    shape = jax.ShapeDtypeStruct((queries, width), jnp.bfloat16)
+    return pl.pallas_call(
+        rows_kernel,
+        out_shape=(shape, shape),
+        in_specs=[vmem] * 5,
+        out_specs=(vmem, vmem),
+        compiler_params=pltpu.CompilerParams(vmem_limit_bytes=24 * MIB),
+        cost_estimate=pl.CostEstimate(
+            flops=2 * HD * HEADS * out_t.shape[2] * kv.shape[0] * kv.shape[1] // 2,
+            bytes_accessed=12 * MIB,
+            transcendentals=0,
+        ),
+        name="outputs_by_query",
+    )(kv, own_k, out_t, slope, own_slope)
 
 
 def add_kernel(index_ref, got_ref, out_ref, table):
@@ -353,7 +387,7 @@
         held.reshape(wide_count * (blk_dev + 1), SLICE, HD),
     )
     kv = swap(picked.reshape(wide_count, selected * SLICE, HD))
-    attn_out, grad_queries, send = attend(
+    send, out_t, slope, own_slope = attend(
         used, kv, queries[0], grad_out[0], own_keys[0], own_values[0]
     )
     got = swap(send).reshape(wide_count, selected, SLICE, HD)
@@ -362,6 +396,10 @@
     mp = lax.axis_size("mp")
     shifts = [[(i, (i + d) % mp) for i in range(mp)] for d in range(1, mp)]
     squares = [squares] + [lax.ppermute(squares, "mp", pairs) for pairs in shifts]
+    out_t, slope, _ = lax.optimization_barrier((out_t, slope, back))
+    attn_out, grad_queries = query_rows(
+        kv, own_keys[0], out_t, slope, own_slope, queries.shape[1], queries.shape[2]
+    )
     count = 2.0 * all_blocks * block_tok * width * mp
     key_update, value_update = finish(squares, back, block_tok, width, count)
     return (attn_out[None], grad_queries[None], key_update, value_update)

time: 172 us -> 170 us (0.988)
  waiting for transfers between devices: 3.93 us -> 1.42 us
    ppermute x3, waiting for transfers between devices: 3.93 us -> 1.42 us  [local(): lax.ppermute(squares, 'mp', pairs)]
    pallas_call x1 -> x2, Pallas kernels: 16.2 us -> 16.4 us  [the longest x1 13.9 us: attend(): pl.pallas_call(attend_kernel, out_shape=(jax.ShapeDtypeStruct(kv.shape, j...]
  transfers between devices with their start and end apart: 3 -> 3, of which waited for: 2 -> 2; matrix products, arithmetic and copies ran while one was open for 0% -> 0% of each run, Pallas kernels for 0% -> 1%
where the time goes in v6:
time: 170 us; the launch traced here: 169 us
  blocking collectives  136 us (80%)
  Pallas kernels  25.7 us (15%)
  starting transfers between devices  4.5 us (3%)
    all_to_all x4, blocking collectives, swap(): return lax.all_to_all(a, 'wide', split_axis=0, concat_axis=0, tiled=True)  136 us
    pallas_call x1, Pallas kernels, attend(): pl.pallas_call(attend_kernel, out_shape=(jax.ShapeDtypeStruct(kv.shape, j...  13.9 us
    ppermute x3, starting transfers between devices, local(): lax.ppermute(squares, 'mp', pairs)  4.5 us
    pallas_call x1, Pallas kernels, split(): pl.pallas_call(split_kernel, out_shape=(jax.ShapeDtypeStruct((count, bloc...  3.48 us
  transfers between devices with their start and end apart: 3, of which 2 were waited for; matrix products, arithmetic and copies ran while one was open for 0% of the time, Pallas kernels for 1%

profile of v6, /device:TPU:0, one launch (start us, length us, event | category | flops | bytes accessed | tf_op | source)
XLA Modules:
  0.0 169.3 jit_solution(3320707988361840602)
XLA Ops:
  1.3 3.5 %split_blocks.1 = (bf16[32,17,16,128]{3,2,1,0:T(8,128)(2,1)}, s32[8,128]{1,0:T(8,128)}) custom-call(s32[1,16]{1,0:T(1,128)} %ids_ref.1, s32[512]{0:T(512)} %home_ref.1, s32[1]{0:T(128)S(6)} %copy.21.length_ref, bf16[16,128,256]{2,1,0:T(8,128)(2,1)} %keys_ref.1, bf16[16,128,256]{2,1,0:T(8,128)(2,1)} %values_ref.1), custom_call_target="tpu_custom_call" | custom-call | tf_op jit(solution)/shard_map/split_blocks/pallas_call | solution.py:92
  4.8 38.8 %all_to_all.20 = bf16[32,17,16,128]{3,2,1,0:T(8,128)(2,1)S(1)} all-to-all(bf16[32,17,16,128]{3,2,1,0:T(8,128)(2,1)} %get-tuple-element.16), channel_id=1, replica_groups=mesh['wide'=32,'mp'=4] {'wide'}, dimensions={0} | all-to-all | bytes 4456448 | tf_op jit(solution)/shard_map/all_to_all | solution.py:363
  43.6 0.1 add.13.index_ref
  43.7 1.3 pick_requested.1
  44.9 0.0 copy-start
  44.9 0.0 copy-start.1
  44.9 0.0 copy-start.2
  45.0 0.0 copy-start.3
  45.0 0.0 copy-start.4
  45.0 31.6 %all_to_all.21.kv_ref = bf16[32,256,128]{2,1,0:T(8,128)(2,1)S(1)} all-to-all(bf16[32,256,128]{2,1,0:T(8,128)(2,1)S(1)} %bitcast.20), channel_id=1, replica_groups=mesh['wide'=32,'mp'=4] {'wide'}, dimensions={0} | all-to-all | bytes 4194304 | tf_op jit(solution)/shard_map/all_to_all | solution.py:363
  76.6 0.0 copy-done
  76.6 0.0 copy-done.1
  76.6 0.0 copy-done.2
  76.6 0.0 copy-done.3
  76.6 0.0 copy-done.4
  76.6 13.9 %attend_forward_backward.1 = (bf16[32,256,128]{2,1,0:T(8,128)(2,1)S(1)}, f32[2,128,1024]{2,1,0:T(8,128)S(1)}, bf16[2,8,256,1024]{3,2,1,0:T(8,128)(2,1)S(1)}, bf16[2,128,1024]{2,1,0:T(8,128)(2,1)S(1)}) custom-call(s32[8,128]{1,0:T(8,128)S(1)} %copy-done.4, bf16[32,256,128]{2,1,0:T(8,128)(2,1)S(1)} %all_to_all.21.kv_ref, bf16[128,2048]{1,0:T(8,128)(2,1)S(1)} %bitcast.23, ...), custom_call_target="tpu_custom_call" | custom-call | flops 5704253440 | bytes 8388608 | tf_op jit(solution)/shard_map/attend_forward_backward/pallas_call | solution.py:214
  90.5 31.9 %all_to_all.22 = bf16[32,256,128]{2,1,0:T(8,128)(2,1)S(1)} all-to-all(bf16[32,256,128]{2,1,0:T(8,128)(2,1)S(1)} %get-tuple-element.20), channel_id=1, replica_groups=mesh['wide'=32,'mp'=4] {'wide'}, dimensions={0} | all-to-all | bytes 4194304 | tf_op jit(solution)/shard_map/all_to_all | solution.py:363
  122.4 2.3 %add_over_readers.1 = bf16[32,264,128]{2,1,0:T(8,128)(2,1)S(1)} custom-call(s32[32,16]{1,0:T(8,128)S(1)} %get-tuple-element.28.index_ref, bf16[32,16,16,128]{3,2,1,0:T(8,128)(2,1)S(1)} %bitcast.19), custom_call_target="tpu_custom_call" | custom-call | tf_op jit(solution)/shard_map/add_over_readers/pallas_call | solution.py:310
  124.7 33.7 %all_to_all.23.refs_4_ = bf16[32,264,128]{2,1,0:T(8,128)(2,1)S(1)} all-to-all(bf16[32,264,128]{2,1,0:T(8,128)(2,1)S(1)} %add_over_readers.1), channel_id=1, replica_groups=mesh['wide'=32,'mp'=4] {'wide'}, dimensions={0} | all-to-all | bytes 4325376 | tf_op jit(solution)/shard_map/all_to_all | solution.py:363
  158.4 2.8 %collective-permute-start.2 = (f32[8,128]{1,0:T(8,128)S(1)}, f32[8,128]{1,0:T(8,128)S(1)}, u32[]{:S(2)}, u32[]{:S(2)}) collective-permute-start(f32[8,128]{1,0:T(8,128)S(1)} %convert_reduce_fusion.refs_0_), channel_id=1, source_target_pairs={{0,3},{1,0},{2,1},{3,2},{4,7},{5,4},{6,5},{7,6},{8,11},{9,8},{10,9... | collective-permute-start | bytes 12296 | tf_op jit(solution)/shard_map/ppermute | solution.py:398
  161.2 0.8 collective-permute-start.1
  162.0 0.9 collective-permute-start
  162.9 2.5 %outputs_by_query.1 = (bf16[128,2048]{1,0:T(8,128)(2,1)}, bf16[128,2048]{1,0:T(8,128)(2,1)}) custom-call(bf16[32,256,128]{2,1,0:T(8,128)(2,1)S(1)} %all_to_all.21.kv_ref, bf16[128,256]{1,0:T(8,128)(2,1)S(1)} %bitcast.22, f32[2,128,1024]{2,1,0:T(8,128)S(1)} %get-tuple-element.21.out_t_ref, bf16[2,8,256,1024]{3,2,1,0:T(8,128)(2,1)S(1)} %get-tuple-element.22.slope_ref, ...), custom_call_target="tpu_custom_call" | custom-call | flops 2147483648 | bytes 12582912 | tf_op jit(solution)/shard_map/outputs_by_query/pallas_call | solution.py:264
  165.4 0.0 collective-permute-done.2.refs_3_
  165.4 0.9 collective-permute-done.1.refs_2_
  166.3 0.5 collective-permute-done.refs_1_
  166.8 2.3 %normalize_updates.1 = (f32[16,128,256]{2,1,0:T(8,128)}, f32[16,128,256]{2,1,0:T(8,128)}) custom-call(f32[8,128]{1,0:T(8,128)S(1)} %convert_reduce_fusion.refs_0_, f32[8,128]{1,0:T(8,128)S(1)} %collective-permute-done.refs_1_, f32[8,128]{1,0:T(8,128)S(1)} %collective-permute-done.1.refs_2_, f32[8,128]{1,0:T(8,128)S(1)} %collective-permute-done.2.refs_3_, ...), custom_call_target="tpu_custom_call" | custom-call | tf_op jit(solution)/shard_map/normalize_updates/pallas_call | solution.py:347
  (4 shorter events, 0.1 us)
Async XLA Ops:
  44.9 31.7 %copy-start = (bf16[1,128,256]{2,1,0:T(8,128)(2,1)S(1)}, bf16[1,128,256]{2,1,0:T(8,128)(2,1)}, u32[]{:S(2)}) copy-start(bf16[1,128,256]{2,1,0:T(8,128)(2,1)} %param.10) | copy-start | bytes 196612
  44.9 31.6 %copy-start.1 = (bf16[1,128,2048]{2,1,0:T(8,128)(2,1)S(1)}, bf16[1,128,2048]{2,1,0:T(8,128)(2,1)}, u32[]{:S(2)}) copy-start(bf16[1,128,2048]{2,1,0:T(8,128)(2,1)} %param.9) | copy-start | bytes 1572868
  44.9 31.6 %copy-start.2 = (bf16[1,128,2048]{2,1,0:T(8,128)(2,1)S(1)}, bf16[1,128,2048]{2,1,0:T(8,128)(2,1)}, u32[]{:S(2)}) copy-start(bf16[1,128,2048]{2,1,0:T(8,128)(2,1)} %param.17) | copy-start | bytes 1572868
  45.0 31.6 %copy-start.3 = (bf16[1,128,256]{2,1,0:T(8,128)(2,1)S(1)}, bf16[1,128,256]{2,1,0:T(8,128)(2,1)}, u32[]{:S(2)}) copy-start(bf16[1,128,256]{2,1,0:T(8,128)(2,1)} %param.11) | copy-start | bytes 196612
  45.0 31.6 %copy-start.4 = (s32[8,128]{1,0:T(8,128)S(1)}, s32[8,128]{1,0:T(8,128)}, u32[]{:S(2)}) copy-start(s32[8,128]{1,0:T(8,128)} %get-tuple-element.17.length_ref) | copy-start | bytes 12292
  158.4 7.0 %collective-permute-start.2 = (f32[8,128]{1,0:T(8,128)S(1)}, f32[8,128]{1,0:T(8,128)S(1)}, u32[]{:S(2)}, u32[]{:S(2)}) collective-permute-start(f32[8,128]{1,0:T(8,128)S(1)} %convert_reduce_fusion.refs_0_), channel_id=1, source_target_pairs={{0,3},{1,0},{2,1},{3,2},{4,7},{5,4},{6,5},{7,6},{8,11},{9,8},{10,9... | collective-permute-start | bytes 12296 | tf_op jit(solution)/shard_map/ppermute | solution.py:398
  161.2 5.1 %collective-permute-start.1 = (f32[8,128]{1,0:T(8,128)S(1)}, f32[8,128]{1,0:T(8,128)S(1)}, u32[]{:S(2)}, u32[]{:S(2)}) collective-permute-start(f32[8,128]{1,0:T(8,128)S(1)} %convert_reduce_fusion.refs_0_), channel_id=1, source_target_pairs={{0,2},{1,3},{2,0},{3,1},{4,6},{5,7},{6,4},{7,5},{8,10},{9,11},{10,... | collective-permute-start | bytes 12296 | tf_op jit(solution)/shard_map/ppermute | solution.py:398
  162.0 4.8 %collective-permute-start = (f32[8,128]{1,0:T(8,128)S(1)}, f32[8,128]{1,0:T(8,128)S(1)}, u32[]{:S(2)}, u32[]{:S(2)}) collective-permute-start(f32[8,128]{1,0:T(8,128)S(1)} %convert_reduce_fusion.refs_0_), channel_id=1, source_target_pairs={{0,1},{1,2},{2,3},{3,0},{4,5},{5,6},{6,7},{7,4},{8,9},{9,10},{10,1... | collective-permute-start | bytes 12296 | tf_op jit(solution)/shard_map/ppermute | solution.py:398

commit v7 on v6

--- a/solution.py
+++ b/solution.py
@@ -27,16 +27,13 @@
 def split_kernel(
     ids_ref,
     home_ref,
-    length_ref,
     keys_ref,
     values_ref,
     out_ref,
-    used_ref,
     inside,
     parts,
     ids,
     home,
-    length,
     in_sems,
     out_sems,
     list_sems,
@@ -51,7 +48,7 @@
             )
             copy.start()
             arrive.append(copy)
-    lists = ((ids_ref, ids), (home_ref, home), (length_ref, length))
+    lists = ((ids_ref, ids), (home_ref, home))
     lists = [
         pltpu.make_async_copy(src, dst, list_sems.at[n]) for n, (src, dst) in enumerate(lists)
     ]
@@ -59,7 +56,6 @@
         copy.start()
     for copy in lists:
         copy.wait()
-    used_ref[...] = jnp.full(used_ref.shape, length[0], jnp.int32)
     line = lax.broadcasted_iota(jnp.int32, (SLICE, HD), 0)
     lane = lax.broadcasted_iota(jnp.int32, (SLICE, HD), 1)
     tag = jnp.zeros((SLICE, HD), jnp.int32)
@@ -85,33 +81,31 @@
         copy.wait()
 
 
-def split(block_ids, block_home, length, cart_keys, cart_values, count):
+def split(block_ids, block_home, cart_keys, cart_values, count):
     blocks, tokens, width = cart_keys.shape
     groups = tokens // SLICE
     hbm = pl.BlockSpec(memory_space=pltpu.HBM)
     return pl.pallas_call(
         split_kernel,
-        out_shape=(
-            jax.ShapeDtypeStruct((count, blocks + 1, SLICE, HD), jnp.bfloat16),
-            jax.ShapeDtypeStruct((8, HD), jnp.int32),
-        ),
-        in_specs=[hbm] * 5,
-        out_specs=(hbm, pl.BlockSpec(memory_space=pltpu.VMEM)),
+        out_shape=jax.ShapeDtypeStruct((count, blocks + 1, SLICE, HD), jnp.bfloat16),
+        in_specs=[hbm] * 4,
+        out_specs=hbm,
         scratch_shapes=[
             pltpu.VMEM((groups, KINDS, blocks, SLICE, width), jnp.bfloat16),
             pltpu.VMEM((count, blocks + 1, SLICE, HD), jnp.bfloat16),
             pltpu.SMEM(block_ids.shape, jnp.int32),
             pltpu.SMEM(block_home.shape, jnp.int32),
-            pltpu.SMEM(length.shape, jnp.int32),
             pltpu.SemaphoreType.DMA((groups, KINDS)),
             pltpu.SemaphoreType.DMA((count,)),
-            pltpu.SemaphoreType.DMA((3,)),
+            pltpu.SemaphoreType.DMA((2,)),
         ],
         name="split_blocks",
-    )(block_ids, block_home, length, cart_keys, cart_values)
-
-
-def pick_kernel(index_ref, held_ref, out_ref):
+    )(block_ids, block_home, cart_keys, cart_values)
+
+
+def pick_kernel(index_ref, length_ref, held_ref, out_ref, used_ref):
+    used_ref[...] = jnp.full(used_ref.shape, length_ref[0], jnp.int32)
+
     def step(n, carry):
         for u in range(16):
             out_ref[n * 16 + u] = held_ref[index_ref[n * 16 + u]]
@@ -120,16 +114,20 @@
     lax.fori_loop(0, out_ref.shape[0] // 16, step, 0)
 
 
-def pick(index, held):
+def pick(index, length, held):
+    smem = pl.BlockSpec(memory_space=pltpu.SMEM)
     vmem = pl.BlockSpec(memory_space=pltpu.VMEM)
     return pl.pallas_call(
         pick_kernel,
-        out_shape=jax.ShapeDtypeStruct((index.shape[0],) + held.shape[1:], jnp.bfloat16),
-        in_specs=[pl.BlockSpec(memory_space=pltpu.SMEM), vmem],
-        out_specs=vmem,
+        out_shape=(
+            jax.ShapeDtypeStruct((index.shape[0],) + held.shape[1:], jnp.bfloat16),
+            jax.ShapeDtypeStruct((8, HD), jnp.int32),
+        ),
+        in_specs=[smem, smem, vmem],
+        out_specs=(vmem, vmem),
         compiler_params=pltpu.CompilerParams(vmem_limit_bytes=16 * MIB),
         name="pick_requested",
-    )(index, held)
+    )(index, length, held)
 
 
 def attend_kernel(
@@ -378,12 +376,12 @@
     blk_dev, block_tok, width = cart_keys.shape
     selected = block_ids.shape[1]
     all_blocks = block_home.shape[0]
-    parts, used = split(block_ids, block_home, query_len, cart_keys, cart_values, wide_count)
-    held = swap(parts)
+    held = swap(split(block_ids, block_home, cart_keys, cart_values, wide_count))
     asked = held[:, blk_dev, :2, :selected].astype(jnp.int32)
     owner, row = asked[:, 0], asked[:, 1]
-    picked = pick(
+    picked, used = pick(
         (owner * (blk_dev + 1) + row).reshape(-1),
+        query_len,
         held.reshape(wide_count * (blk_dev + 1), SLICE, HD),
     )
     kv = swap(picked.reshape(wide_count, selected * SLICE, HD))

time: 170 us -> 168 us (0.988)
  blocking collectives: 136 us -> 96.7 us
  waiting for transfers between devices: 1.42 us -> 31.1 us
  starting transfers between devices: 4.5 us -> 12.9 us
    all_to_all x4 -> x3, blocking collectives: 136 us -> 96.7 us  [swap(): return lax.all_to_all(a, 'wide', split_axis=0, concat_axis=0, tiled=True)]
    all_to_all x0 -> x1, waiting for transfers between devices: none -> 29.7 us  [swap(): return lax.all_to_all(a, 'wide', split_axis=0, concat_axis=0, tiled=True)]
    all_to_all x0 -> x1, starting transfers between devices: none -> 8.43 us  [swap(): return lax.all_to_all(a, 'wide', split_axis=0, concat_axis=0, tiled=True)]
  transfers between devices with their start and end apart: 3 -> 4, of which waited for: 2 -> 3; matrix products, arithmetic and copies ran while one was open for 0% -> 0% of each run, Pallas kernels for 1% -> 2%
where the time goes in v7:
time: 168 us
  blocking collectives  96.7 us (58%)
  waiting for transfers between devices  31.1 us (19%)
  Pallas kernels  25.2 us (15%)
  starting transfers between devices  12.9 us (8%)
    all_to_all x3, blocking collectives, swap(): return lax.all_to_all(a, 'wide', split_axis=0, concat_axis=0, tiled=True)  96.7 us
    all_to_all x1, waiting for transfers between devices, swap(): return lax.all_to_all(a, 'wide', split_axis=0, concat_axis=0, tiled=True)  29.7 us
    pallas_call x1, Pallas kernels, attend(): pl.pallas_call(attend_kernel, out_shape=(jax.ShapeDtypeStruct(kv.shape, j...  13.9 us
    all_to_all x1, starting transfers between devices, swap(): return lax.all_to_all(a, 'wide', split_axis=0, concat_axis=0, tiled=True)  8.43 us
    ppermute x3, starting transfers between devices, local(): lax.ppermute(squares, 'mp', pairs)  4.51 us
  transfers between devices with their start and end apart: 4, of which 3 were waited for; matrix products, arithmetic and copies ran while one was open for 0% of the time, Pallas kernels for 2%

profile of v7, /device:TPU:0, one launch (start us, length us, event | category | flops | bytes accessed | tf_op | source)
XLA Modules:
  0.0 167.7 jit_solution(750048028662584833)
XLA Ops:
  0.6 2.9 %split_blocks.1 = bf16[32,17,16,128]{3,2,1,0:T(8,128)(2,1)} custom-call(s32[1,16]{1,0:T(1,128)} %ids_ref.1, s32[512]{0:T(512)} %home_ref.1, bf16[16,128,256]{2,1,0:T(8,128)(2,1)} %keys_ref.1, bf16[16,128,256]{2,1,0:T(8,128)(2,1)} %values_ref.1), custom_call_target="tpu_custom_call" | custom-call | tf_op jit(solution)/shard_map/split_blocks/pallas_call | solution.py:88
  3.5 8.4 %all-to-all-start = ((bf16[32,17,16,128]{3,2,1,0:T(8,128)(2,1)}), bf16[32,17,16,128]{3,2,1,0:T(8,128)(2,1)S(1)}, u32[]{:S(2)}, u32[]{:S(2)}) async-start(bf16[32,17,16,128]{3,2,1,0:T(8,128)(2,1)} %split_blocks.1), calls=%async_computation | async-start | bytes 4456448 | tf_op jit(solution)/shard_map/all_to_all | solution.py:361
  12.6 29.7 %all-to-all-done = bf16[32,17,16,128]{3,2,1,0:T(8,128)(2,1)S(1)} async-done(((bf16[32,17,16,128]{3,2,1,0:T(8,128)(2,1)}), bf16[32,17,16,128]{3,2,1,0:T(8,128)(2,1)S(1)}, u32[]{:S(2)}, u32[]{:S(2)}) %all-to-all-start) | async-done | bytes 2228256 | tf_op jit(solution)/shard_map/all_to_all | solution.py:361
  42.4 0.1 add.13.index_ref
  42.5 1.3 pick_requested.1
  43.7 0.0 copy-start
  43.7 0.0 copy-start.1
  43.7 0.0 copy-start.2
  43.8 0.0 copy-start.3
  43.8 31.2 %all_to_all.20.kv_ref = bf16[32,256,128]{2,1,0:T(8,128)(2,1)S(1)} all-to-all(bf16[32,256,128]{2,1,0:T(8,128)(2,1)S(1)} %bitcast.20), channel_id=1, replica_groups=mesh['wide'=32,'mp'=4] {'wide'}, dimensions={0} | all-to-all | bytes 4194304 | tf_op jit(solution)/shard_map/all_to_all | solution.py:361
  74.9 0.0 copy-done
  74.9 0.0 copy-done.1
  75.0 0.0 copy-done.2
  75.0 0.0 copy-done.3
  75.0 13.9 %attend_forward_backward.1 = (bf16[32,256,128]{2,1,0:T(8,128)(2,1)S(1)}, f32[2,128,1024]{2,1,0:T(8,128)S(1)}, bf16[2,8,256,1024]{3,2,1,0:T(8,128)(2,1)S(1)}, bf16[2,128,1024]{2,1,0:T(8,128)(2,1)S(1)}) custom-call(s32[8,128]{1,0:T(8,128)S(1)} %get-tuple-element.17.length_ref, bf16[32,256,128]{2,1,0:T(8,128)(2,1)S(1)} %all_to_all.20.kv_ref, ...), custom_call_target="tpu_custom_call" | custom-call | flops 5704253440 | bytes 8388608 | tf_op jit(solution)/shard_map/attend_forward_backward/pallas_call | solution.py:212
  88.9 31.9 %all_to_all.21 = bf16[32,256,128]{2,1,0:T(8,128)(2,1)S(1)} all-to-all(bf16[32,256,128]{2,1,0:T(8,128)(2,1)S(1)} %get-tuple-element.20), channel_id=1, replica_groups=mesh['wide'=32,'mp'=4] {'wide'}, dimensions={0} | all-to-all | bytes 4194304 | tf_op jit(solution)/shard_map/all_to_all | solution.py:361
  120.8 2.3 %add_over_readers.1 = bf16[32,264,128]{2,1,0:T(8,128)(2,1)S(1)} custom-call(s32[32,16]{1,0:T(8,128)S(1)} %get-tuple-element.28.index_ref, bf16[32,16,16,128]{3,2,1,0:T(8,128)(2,1)S(1)} %bitcast.19), custom_call_target="tpu_custom_call" | custom-call | tf_op jit(solution)/shard_map/add_over_readers/pallas_call | solution.py:308
  123.1 33.7 %all_to_all.22.refs_4_ = bf16[32,264,128]{2,1,0:T(8,128)(2,1)S(1)} all-to-all(bf16[32,264,128]{2,1,0:T(8,128)(2,1)S(1)} %add_over_readers.1), channel_id=1, replica_groups=mesh['wide'=32,'mp'=4] {'wide'}, dimensions={0} | all-to-all | bytes 4325376 | tf_op jit(solution)/shard_map/all_to_all | solution.py:361
  156.8 2.8 %collective-permute-start.2 = (f32[8,128]{1,0:T(8,128)S(1)}, f32[8,128]{1,0:T(8,128)S(1)}, u32[]{:S(2)}, u32[]{:S(2)}) collective-permute-start(f32[8,128]{1,0:T(8,128)S(1)} %convert_reduce_fusion.refs_0_), channel_id=1, source_target_pairs={{0,3},{1,0},{2,1},{3,2},{4,7},{5,4},{6,5},{7,6},{8,11},{9,8},{10,9... | collective-permute-start | bytes 12296 | tf_op jit(solution)/shard_map/ppermute | solution.py:396
  159.6 0.8 collective-permute-start.1
  160.4 0.9 collective-permute-start
  161.3 2.5 %outputs_by_query.1 = (bf16[128,2048]{1,0:T(8,128)(2,1)}, bf16[128,2048]{1,0:T(8,128)(2,1)}) custom-call(bf16[32,256,128]{2,1,0:T(8,128)(2,1)S(1)} %all_to_all.20.kv_ref, bf16[128,256]{1,0:T(8,128)(2,1)S(1)} %bitcast.22, f32[2,128,1024]{2,1,0:T(8,128)S(1)} %get-tuple-element.21.out_t_ref, bf16[2,8,256,1024]{3,2,1,0:T(8,128)(2,1)S(1)} %get-tuple-element.22.slope_ref, ...), custom_call_target="tpu_custom_call" | custom-call | flops 2147483648 | bytes 12582912 | tf_op jit(solution)/shard_map/outputs_by_query/pallas_call | solution.py:262
  163.8 0.0 collective-permute-done.2.refs_3_
  163.8 0.9 collective-permute-done.1.refs_2_
  164.7 0.5 collective-permute-done.refs_1_
  165.2 2.3 %normalize_updates.1 = (f32[16,128,256]{2,1,0:T(8,128)}, f32[16,128,256]{2,1,0:T(8,128)}) custom-call(f32[8,128]{1,0:T(8,128)S(1)} %convert_reduce_fusion.refs_0_, f32[8,128]{1,0:T(8,128)S(1)} %collective-permute-done.refs_1_, f32[8,128]{1,0:T(8,128)S(1)} %collective-permute-done.1.refs_2_, f32[8,128]{1,0:T(8,128)S(1)} %collective-permute-done.2.refs_3_, ...), custom_call_target="tpu_custom_call" | custom-call | tf_op jit(solution)/shard_map/normalize_updates/pallas_call | solution.py:345
  (4 shorter events, 0.1 us)
Async XLA Ops:
  3.5 38.8 %all-to-all-start = ((bf16[32,17,16,128]{3,2,1,0:T(8,128)(2,1)}), bf16[32,17,16,128]{3,2,1,0:T(8,128)(2,1)S(1)}, u32[]{:S(2)}, u32[]{:S(2)}) async-start(bf16[32,17,16,128]{3,2,1,0:T(8,128)(2,1)} %split_blocks.1), calls=%async_computation | async-start | bytes 4456448 | tf_op jit(solution)/shard_map/all_to_all | solution.py:361
  43.7 31.2 %copy-start = (bf16[1,128,256]{2,1,0:T(8,128)(2,1)S(1)}, bf16[1,128,256]{2,1,0:T(8,128)(2,1)}, u32[]{:S(2)}) copy-start(bf16[1,128,256]{2,1,0:T(8,128)(2,1)} %param.10) | copy-start | bytes 196612
  43.7 31.2 %copy-start.1 = (bf16[1,128,2048]{2,1,0:T(8,128)(2,1)S(1)}, bf16[1,128,2048]{2,1,0:T(8,128)(2,1)}, u32[]{:S(2)}) copy-start(bf16[1,128,2048]{2,1,0:T(8,128)(2,1)} %param.9) | copy-start | bytes 1572868
  43.7 31.2 %copy-start.2 = (bf16[1,128,2048]{2,1,0:T(8,128)(2,1)S(1)}, bf16[1,128,2048]{2,1,0:T(8,128)(2,1)}, u32[]{:S(2)}) copy-start(bf16[1,128,2048]{2,1,0:T(8,128)(2,1)} %param.17) | copy-start | bytes 1572868
  43.8 31.2 %copy-start.3 = (bf16[1,128,256]{2,1,0:T(8,128)(2,1)S(1)}, bf16[1,128,256]{2,1,0:T(8,128)(2,1)}, u32[]{:S(2)}) copy-start(bf16[1,128,256]{2,1,0:T(8,128)(2,1)} %param.11) | copy-start | bytes 196612
  156.8 7.0 %collective-permute-start.2 = (f32[8,128]{1,0:T(8,128)S(1)}, f32[8,128]{1,0:T(8,128)S(1)}, u32[]{:S(2)}, u32[]{:S(2)}) collective-permute-start(f32[8,128]{1,0:T(8,128)S(1)} %convert_reduce_fusion.refs_0_), channel_id=1, source_target_pairs={{0,3},{1,0},{2,1},{3,2},{4,7},{5,4},{6,5},{7,6},{8,11},{9,8},{10,9... | collective-permute-start | bytes 12296 | tf_op jit(solution)/shard_map/ppermute | solution.py:396
  159.6 5.1 %collective-permute-start.1 = (f32[8,128]{1,0:T(8,128)S(1)}, f32[8,128]{1,0:T(8,128)S(1)}, u32[]{:S(2)}, u32[]{:S(2)}) collective-permute-start(f32[8,128]{1,0:T(8,128)S(1)} %convert_reduce_fusion.refs_0_), channel_id=1, source_target_pairs={{0,2},{1,3},{2,0},{3,1},{4,6},{5,7},{6,4},{7,5},{8,10},{9,11},{10,... | collective-permute-start | bytes 12296 | tf_op jit(solution)/shard_map/ppermute | solution.py:396
  160.4 4.8 %collective-permute-start = (f32[8,128]{1,0:T(8,128)S(1)}, f32[8,128]{1,0:T(8,128)S(1)}, u32[]{:S(2)}, u32[]{:S(2)}) collective-permute-start(f32[8,128]{1,0:T(8,128)S(1)} %convert_reduce_fusion.refs_0_), channel_id=1, source_target_pairs={{0,1},{1,2},{2,3},{3,0},{4,5},{5,6},{6,7},{7,4},{8,9},{9,10},{10,1... | collective-permute-start | bytes 12296 | tf_op jit(solution)/shard_map/ppermute | solution.py:396

commit v8 on v7

--- a/solution.py
+++ b/solution.py
@@ -10,7 +10,7 @@
 
 HD = 128
 SLICE = 16
-TAG = 8
+TAG = 16
 HEADS = 2
 KINDS = 2
 MIB = 1024 * 1024
@@ -111,7 +111,7 @@
             out_ref[n * 16 + u] = held_ref[index_ref[n * 16 + u]]
         return carry
 
-    lax.fori_loop(0, out_ref.shape[0] // 16, step, 0)
+    lax.fori_loop(0, out_ref.shape[0] // 16, step, 0, unroll=2)
 
 
 def pick(index, length, held):
@@ -295,7 +295,6 @@
         return squares + jnp.sum((rows * rows).reshape(held // 8, 8, HD), axis=0)
 
     squares = lax.fori_loop(0, owners, finish, jnp.zeros((8, HD), jnp.float32), unroll=4)
-    squares = squares[: TAG // 2] + squares[TAG // 2 :]
     high = squares.astype(jnp.bfloat16).astype(jnp.float32)
     tag = jnp.concatenate([high, squares - high], axis=0).astype(jnp.bfloat16)
     for n in range(owners):
@@ -390,7 +389,8 @@
     )
     got = swap(send).reshape(wide_count, selected, SLICE, HD)
     back = swap(add_up(owner * blk_dev + row, got, blk_dev))
-    squares = jnp.sum(back[:, -TAG:].astype(jnp.float32), axis=0)
+    squares = back[:, -TAG:].astype(jnp.float32).reshape(2 * wide_count, TAG // 2, HD)
+    squares = jnp.sum(squares, axis=0)
     mp = lax.axis_size("mp")
     shifts = [[(i, (i + d) % mp) for i in range(mp)] for d in range(1, mp)]
     squares = [squares] + [lax.ppermute(squares, "mp", pairs) for pairs in shifts]

time: 168 us -> 168 us (level)
  transfers between devices with their start and end apart: 4 -> 4, of which waited for: 3 -> 3; matrix products, arithmetic and copies ran while one was open for 0% -> 0% of each run, Pallas kernels for 2% -> 1%
where the time goes in v8:
time: 168 us
  blocking collectives  97.2 us (58%)
  waiting for transfers between devices  31.1 us (19%)
  Pallas kernels  25.1 us (15%)
  starting transfers between devices  12.9 us (8%)
    all_to_all x3, blocking collectives, swap(): return lax.all_to_all(a, 'wide', split_axis=0, concat_axis=0, tiled=True)  97.2 us
    all_to_all x1, waiting for transfers between devices, swap(): return lax.all_to_all(a, 'wide', split_axis=0, concat_axis=0, tiled=True)  29.7 us
    pallas_call x1, Pallas kernels, attend(): pl.pallas_call(attend_kernel, out_shape=(jax.ShapeDtypeStruct(kv.shape, j...  13.9 us
    all_to_all x1, starting transfers between devices, swap(): return lax.all_to_all(a, 'wide', split_axis=0, concat_axis=0, tiled=True)  8.43 us
    ppermute x3, starting transfers between devices, local(): lax.ppermute(squares, 'mp', pairs)  4.51 us
  transfers between devices with their start and end apart: 4, of which 3 were waited for; matrix products, arithmetic and copies ran while one was open for 0% of the time, Pallas kernels for 1%

profile of v8, /device:TPU:0, one launch (start us, length us, event | category | flops | bytes accessed | tf_op | source)
XLA Modules:
  0.0 168.1 jit_solution(6149085490912620974)
XLA Ops:
  0.6 2.9 %split_blocks.1 = bf16[32,17,16,128]{3,2,1,0:T(8,128)(2,1)} custom-call(s32[1,16]{1,0:T(1,128)} %ids_ref.1, s32[512]{0:T(512)} %home_ref.1, bf16[16,128,256]{2,1,0:T(8,128)(2,1)} %keys_ref.1, bf16[16,128,256]{2,1,0:T(8,128)(2,1)} %values_ref.1), custom_call_target="tpu_custom_call" | custom-call | tf_op jit(solution)/shard_map/split_blocks/pallas_call | solution.py:88
  3.5 8.4 %all-to-all-start = ((bf16[32,17,16,128]{3,2,1,0:T(8,128)(2,1)}), bf16[32,17,16,128]{3,2,1,0:T(8,128)(2,1)S(1)}, u32[]{:S(2)}, u32[]{:S(2)}) async-start(bf16[32,17,16,128]{3,2,1,0:T(8,128)(2,1)} %split_blocks.1), calls=%async_computation | async-start | bytes 4456448 | tf_op jit(solution)/shard_map/all_to_all | solution.py:360
  12.6 29.7 %all-to-all-done = bf16[32,17,16,128]{3,2,1,0:T(8,128)(2,1)S(1)} async-done(((bf16[32,17,16,128]{3,2,1,0:T(8,128)(2,1)}), bf16[32,17,16,128]{3,2,1,0:T(8,128)(2,1)S(1)}, u32[]{:S(2)}, u32[]{:S(2)}) %all-to-all-start) | async-done | bytes 2228256 | tf_op jit(solution)/shard_map/all_to_all | solution.py:360
  42.4 0.1 add.13.index_ref
  42.5 1.2 pick_requested.1
  43.6 0.0 copy-start
  43.6 0.0 copy-start.1
  43.6 0.0 copy-start.2
  43.7 0.0 copy-start.3
  43.7 31.2 %all_to_all.20.kv_ref = bf16[32,256,128]{2,1,0:T(8,128)(2,1)S(1)} all-to-all(bf16[32,256,128]{2,1,0:T(8,128)(2,1)S(1)} %bitcast.22), channel_id=1, replica_groups=mesh['wide'=32,'mp'=4] {'wide'}, dimensions={0} | all-to-all | bytes 4194304 | tf_op jit(solution)/shard_map/all_to_all | solution.py:360
  74.9 0.0 copy-done
  74.9 0.0 copy-done.1
  74.9 0.0 copy-done.2
  74.9 0.0 copy-done.3
  74.9 13.9 %attend_forward_backward.1 = (bf16[32,256,128]{2,1,0:T(8,128)(2,1)S(1)}, f32[2,128,1024]{2,1,0:T(8,128)S(1)}, bf16[2,8,256,1024]{3,2,1,0:T(8,128)(2,1)S(1)}, bf16[2,128,1024]{2,1,0:T(8,128)(2,1)S(1)}) custom-call(s32[8,128]{1,0:T(8,128)S(1)} %get-tuple-element.17.length_ref, bf16[32,256,128]{2,1,0:T(8,128)(2,1)S(1)} %all_to_all.20.kv_ref, ...), custom_call_target="tpu_custom_call" | custom-call | flops 5704253440 | bytes 8388608 | tf_op jit(solution)/shard_map/attend_forward_backward/pallas_call | solution.py:212
  88.8 31.9 %all_to_all.21 = bf16[32,256,128]{2,1,0:T(8,128)(2,1)S(1)} all-to-all(bf16[32,256,128]{2,1,0:T(8,128)(2,1)S(1)} %get-tuple-element.20), channel_id=1, replica_groups=mesh['wide'=32,'mp'=4] {'wide'}, dimensions={0} | all-to-all | bytes 4194304 | tf_op jit(solution)/shard_map/all_to_all | solution.py:360
  120.7 2.3 %add_over_readers.1 = bf16[32,272,128]{2,1,0:T(8,128)(2,1)S(1)} custom-call(s32[32,16]{1,0:T(8,128)S(1)} %get-tuple-element.28.index_ref, bf16[32,16,16,128]{3,2,1,0:T(8,128)(2,1)S(1)} %bitcast.21), custom_call_target="tpu_custom_call" | custom-call | tf_op jit(solution)/shard_map/add_over_readers/pallas_call | solution.py:307
  123.0 34.2 %all_to_all.22.refs_4_ = bf16[32,272,128]{2,1,0:T(8,128)(2,1)S(1)} all-to-all(bf16[32,272,128]{2,1,0:T(8,128)(2,1)S(1)} %add_over_readers.1), channel_id=1, replica_groups=mesh['wide'=32,'mp'=4] {'wide'}, dimensions={0} | all-to-all | bytes 4456448 | tf_op jit(solution)/shard_map/all_to_all | solution.py:360
  157.2 0.1 convert_reduce_fusion.refs_0_
  157.3 2.8 %collective-permute-start.2 = (f32[8,128]{1,0:T(8,128)S(1)}, f32[8,128]{1,0:T(8,128)S(1)}, u32[]{:S(2)}, u32[]{:S(2)}) collective-permute-start(f32[8,128]{1,0:T(8,128)S(1)} %convert_reduce_fusion.refs_0_), channel_id=1, source_target_pairs={{0,3},{1,0},{2,1},{3,2},{4,7},{5,4},{6,5},{7,6},{8,11},{9,8},{10,9... | collective-permute-start | bytes 12296 | tf_op jit(solution)/shard_map/ppermute | solution.py:396
  160.1 0.8 collective-permute-start.1
  160.9 0.9 collective-permute-start
  161.8 2.5 %outputs_by_query.1 = (bf16[128,2048]{1,0:T(8,128)(2,1)}, bf16[128,2048]{1,0:T(8,128)(2,1)}) custom-call(bf16[32,256,128]{2,1,0:T(8,128)(2,1)S(1)} %all_to_all.20.kv_ref, bf16[128,256]{1,0:T(8,128)(2,1)S(1)} %bitcast.24, f32[2,128,1024]{2,1,0:T(8,128)S(1)} %get-tuple-element.21.out_t_ref, bf16[2,8,256,1024]{3,2,1,0:T(8,128)(2,1)S(1)} %get-tuple-element.22.slope_ref, ...), custom_call_target="tpu_custom_call" | custom-call | flops 2147483648 | bytes 12582912 | tf_op jit(solution)/shard_map/outputs_by_query/pallas_call | solution.py:262
  164.3 0.0 collective-permute-done.2.refs_3_
  164.3 0.9 collective-permute-done.1.refs_2_
  165.2 0.5 collective-permute-done.refs_1_
  165.7 2.3 %normalize_updates.1 = (f32[16,128,256]{2,1,0:T(8,128)}, f32[16,128,256]{2,1,0:T(8,128)}) custom-call(f32[8,128]{1,0:T(8,128)S(1)} %convert_reduce_fusion.refs_0_, f32[8,128]{1,0:T(8,128)S(1)} %collective-permute-done.refs_1_, f32[8,128]{1,0:T(8,128)S(1)} %collective-permute-done.1.refs_2_, f32[8,128]{1,0:T(8,128)S(1)} %collective-permute-done.2.refs_3_, ...), custom_call_target="tpu_custom_call" | custom-call | tf_op jit(solution)/shard_map/normalize_updates/pallas_call | solution.py:344
  (4 shorter events, 0.0 us)
Async XLA Ops:
  3.5 38.8 %all-to-all-start = ((bf16[32,17,16,128]{3,2,1,0:T(8,128)(2,1)}), bf16[32,17,16,128]{3,2,1,0:T(8,128)(2,1)S(1)}, u32[]{:S(2)}, u32[]{:S(2)}) async-start(bf16[32,17,16,128]{3,2,1,0:T(8,128)(2,1)} %split_blocks.1), calls=%async_computation | async-start | bytes 4456448 | tf_op jit(solution)/shard_map/all_to_all | solution.py:360
  43.6 31.2 %copy-start = (bf16[1,128,256]{2,1,0:T(8,128)(2,1)S(1)}, bf16[1,128,256]{2,1,0:T(8,128)(2,1)}, u32[]{:S(2)}) copy-start(bf16[1,128,256]{2,1,0:T(8,128)(2,1)} %param.10) | copy-start | bytes 196612
  43.6 31.2 %copy-start.1 = (bf16[1,128,2048]{2,1,0:T(8,128)(2,1)S(1)}, bf16[1,128,2048]{2,1,0:T(8,128)(2,1)}, u32[]{:S(2)}) copy-start(bf16[1,128,2048]{2,1,0:T(8,128)(2,1)} %param.9) | copy-start | bytes 1572868
  43.6 31.2 %copy-start.2 = (bf16[1,128,2048]{2,1,0:T(8,128)(2,1)S(1)}, bf16[1,128,2048]{2,1,0:T(8,128)(2,1)}, u32[]{:S(2)}) copy-start(bf16[1,128,2048]{2,1,0:T(8,128)(2,1)} %param.17) | copy-start | bytes 1572868
  43.7 31.2 %copy-start.3 = (bf16[1,128,256]{2,1,0:T(8,128)(2,1)S(1)}, bf16[1,128,256]{2,1,0:T(8,128)(2,1)}, u32[]{:S(2)}) copy-start(bf16[1,128,256]{2,1,0:T(8,128)(2,1)} %param.11) | copy-start | bytes 196612
  157.3 7.0 %collective-permute-start.2 = (f32[8,128]{1,0:T(8,128)S(1)}, f32[8,128]{1,0:T(8,128)S(1)}, u32[]{:S(2)}, u32[]{:S(2)}) collective-permute-start(f32[8,128]{1,0:T(8,128)S(1)} %convert_reduce_fusion.refs_0_), channel_id=1, source_target_pairs={{0,3},{1,0},{2,1},{3,2},{4,7},{5,4},{6,5},{7,6},{8,11},{9,8},{10,9... | collective-permute-start | bytes 12296 | tf_op jit(solution)/shard_map/ppermute | solution.py:396
  160.1 5.1 %collective-permute-start.1 = (f32[8,128]{1,0:T(8,128)S(1)}, f32[8,128]{1,0:T(8,128)S(1)}, u32[]{:S(2)}, u32[]{:S(2)}) collective-permute-start(f32[8,128]{1,0:T(8,128)S(1)} %convert_reduce_fusion.refs_0_), channel_id=1, source_target_pairs={{0,2},{1,3},{2,0},{3,1},{4,6},{5,7},{6,4},{7,5},{8,10},{9,11},{10,... | collective-permute-start | bytes 12296 | tf_op jit(solution)/shard_map/ppermute | solution.py:396
  160.9 4.8 %collective-permute-start = (f32[8,128]{1,0:T(8,128)S(1)}, f32[8,128]{1,0:T(8,128)S(1)}, u32[]{:S(2)}, u32[]{:S(2)}) collective-permute-start(f32[8,128]{1,0:T(8,128)S(1)} %convert_reduce_fusion.refs_0_), channel_id=1, source_target_pairs={{0,1},{1,2},{2,3},{3,0},{4,5},{5,6},{6,7},{7,4},{8,9},{9,10},{10,1... | collective-permute-start | bytes 12296 | tf_op jit(solution)/shard_map/ppermute | solution.py:396

commit v9 on v8

--- a/solution.py
+++ b/solution.py
@@ -160,6 +160,7 @@
     row_used = position < used
     own_at = lax.broadcasted_iota(jnp.int32, (own, rows), 0)
     seen = (own_at <= position) & (own_at < used)
+    ones = jnp.ones((16, chunk), jnp.bfloat16)
     for head in range(HEADS):
         lanes = slice(head * HD, (head + 1) * HD)
         own_k = own_k_ref[:, lanes]
@@ -177,18 +178,16 @@
             top = jnp.maximum(top, jnp.max(s.reshape(chunk // 8, 8, rows), axis=0))
         top = jnp.max(top, axis=0, keepdims=True) * log2e
         e = jnp.exp2(own_s * log2e - top)
-        total = jnp.sum(e.reshape(own // 8, 8, rows), axis=0)
         own_e = e.astype(jnp.bfloat16)
-        acc[...] = nn(own_v.T, own_e)
+        acc[...] = nn(jnp.concatenate([own_v.T, ones[:, :own]], axis=0), own_e)
         for c in range(chunks):
             e = jnp.exp2(score[c] * log2e - top)
-            total = total + jnp.sum(e.reshape(chunk // 8, 8, rows), axis=0)
             low = e.astype(jnp.bfloat16)
             expo[c] = low
-            acc[...] += nn(kv_ref[at(c, 1)].T, low)
-        inv = 1.0 / jnp.sum(total, axis=0, keepdims=True)
+            acc[...] += nn(jnp.concatenate([kv_ref[at(c, 1)].T, ones], axis=0), low)
+        inv = 1.0 / acc[HD : HD + 1]
         g = jnp.where(row_used, g_cols[...].astype(jnp.float32), 0.0)
-        out = jnp.where(row_used, acc[...] * inv, 0.0)
+        out = jnp.where(row_used, acc[:HD] * inv, 0.0)
         out_ref[head] = out
         delta = jnp.sum(g * out, axis=0, keepdims=True) * inv
         gs = (g * inv).astype(jnp.bfloat16)
@@ -222,7 +221,7 @@
         scratch_shapes=[
             pltpu.VMEM((chunks, chunk, rows), jnp.float32),
             pltpu.VMEM((chunks, chunk, rows), jnp.bfloat16),
-            pltpu.VMEM((HD, rows), jnp.float32),
+            pltpu.VMEM((HD + 16, rows), jnp.float32),
             pltpu.VMEM((rows, HD), jnp.bfloat16),
             pltpu.VMEM((HD, rows), jnp.bfloat16),
         ],
@@ -274,11 +273,24 @@
     )(kv, own_k, out_t, slope, own_slope)
 
 
-def add_kernel(index_ref, got_ref, out_ref, table):
+def zeros_kernel(out_ref):
+    out_ref[...] = jnp.zeros_like(out_ref)
+
+
+def zeros(rows):
+    return pl.pallas_call(
+        zeros_kernel,
+        out_shape=jax.ShapeDtypeStruct((rows, SLICE, HD), jnp.float32),
+        out_specs=pl.BlockSpec(memory_space=pltpu.VMEM),
+        compiler_params=pltpu.CompilerParams(vmem_limit_bytes=16 * MIB),
+        name="zero_table",
+    )()
+
+
+def add_kernel(index_ref, got_ref, zeros_ref, out_ref, table):
     selected = index_ref.shape[1]
     owners, held = out_ref.shape[0], out_ref.shape[1] - TAG
     blocks = held // SLICE
-    table[...] = jnp.zeros_like(table)
 
     def step(n, carry):
         at = [index_ref[n, k] for k in range(selected)]
@@ -301,18 +313,21 @@
         out_ref[n, pl.ds(held, TAG)] = tag
 
 
-def add_up(index, got, blk_dev):
+def add_up(index, got, zeros, blk_dev):
     count = got.shape[0]
     vmem = pl.BlockSpec(memory_space=pltpu.VMEM)
     return pl.pallas_call(
         add_kernel,
-        out_shape=jax.ShapeDtypeStruct((count, blk_dev * SLICE + TAG, HD), jnp.bfloat16),
-        in_specs=[pl.BlockSpec(memory_space=pltpu.SMEM), vmem],
-        out_specs=vmem,
-        scratch_shapes=[pltpu.VMEM((count * blk_dev, SLICE, HD), jnp.float32)],
+        out_shape=(
+            jax.ShapeDtypeStruct((count, blk_dev * SLICE + TAG, HD), jnp.bfloat16),
+            jax.ShapeDtypeStruct(zeros.shape, zeros.dtype),
+        ),
+        in_specs=[pl.BlockSpec(memory_space=pltpu.SMEM), vmem, vmem],
+        out_specs=(vmem, vmem),
+        input_output_aliases={2: 1},
         compiler_params=pltpu.CompilerParams(vmem_limit_bytes=24 * MIB),
         name="add_over_readers",
-    )(index, got)
+    )(index, got, zeros)[0]
 
 
 def finish_kernel(count, *refs):
@@ -377,6 +392,7 @@
     all_blocks = block_home.shape[0]
     held = swap(split(block_ids, block_home, cart_keys, cart_values, wide_count))
     asked = held[:, blk_dev, :2, :selected].astype(jnp.int32)
+    asked, table = lax.optimization_barrier((asked, zeros(all_blocks)))
     owner, row = asked[:, 0], asked[:, 1]
     picked, used = pick(
         (owner * (blk_dev + 1) + row).reshape(-1),
@@ -388,7 +404,7 @@
         used, kv, queries[0], grad_out[0], own_keys[0], own_values[0]
     )
     got = swap(send).reshape(wide_count, selected, SLICE, HD)
-    back = swap(add_up(owner * blk_dev + row, got, blk_dev))
+    back = swap(add_up(owner * blk_dev + row, got, table, blk_dev))
     squares = back[:, -TAG:].astype(jnp.float32).reshape(2 * wide_count, TAG // 2, HD)
     squares = jnp.sum(squares, axis=0)
     mp = lax.axis_size("mp")

time: 168 us -> 168 us (level)
  waiting for transfers between devices: 31.1 us -> 28.9 us
  local copies, waits for them, and re-layouts: 0.13 us -> 2.07 us
    all_to_all x1, waiting for transfers between devices: 29.7 us -> 27.5 us  [swap(): return lax.all_to_all(a, 'wide', split_axis=0, concat_axis=0, tiled=True)]
    unnamed x8 -> x12, local copies, waits for them, and re-layouts: 0.03 us -> 1.97 us
  transfers between devices with their start and end apart: 4 -> 4, of which waited for: 3 -> 3; matrix products, arithmetic and copies ran while one was open for 0% -> 0% of each run, Pallas kernels for 1% -> 2%
where the time goes in v9:
time: 168 us
  blocking collectives  97.5 us (58%)
  waiting for transfers between devices  28.9 us (17%)
  Pallas kernels  24.8 us (15%)
  starting transfers between devices  12.9 us (8%)
  local copies, waits for them, and re-layouts  2.07 us (1%)
    all_to_all x3, blocking collectives, swap(): return lax.all_to_all(a, 'wide', split_axis=0, concat_axis=0, tiled=True)  97.5 us
    all_to_all x1, waiting for transfers between devices, swap(): return lax.all_to_all(a, 'wide', split_axis=0, concat_axis=0, tiled=True)  27.5 us
    pallas_call x1, Pallas kernels, attend(): pl.pallas_call(attend_kernel, out_shape=(jax.ShapeDtypeStruct(kv.shape, j...  13.6 us
    all_to_all x1, starting transfers between devices, swap(): return lax.all_to_all(a, 'wide', split_axis=0, concat_axis=0, tiled=True)  8.43 us
    ppermute x3, starting transfers between devices, local(): lax.ppermute(squares, 'mp', pairs)  4.5 us
  transfers between devices with their start and end apart: 4, of which 3 were waited for; matrix products, arithmetic and copies ran while one was open for 0% of the time, Pallas kernels for 2%

profile of v9, /device:TPU:0, one launch (start us, length us, event | category | flops | bytes accessed | tf_op | source)
XLA Modules:
  0.0 167.8 jit_solution(8797688740625917285)
XLA Ops:
  0.6 2.9 %split_blocks.1 = bf16[32,17,16,128]{3,2,1,0:T(8,128)(2,1)} custom-call(s32[1,16]{1,0:T(1,128)} %ids_ref.1, s32[512]{0:T(512)} %home_ref.1, bf16[16,128,256]{2,1,0:T(8,128)(2,1)} %keys_ref.1, bf16[16,128,256]{2,1,0:T(8,128)(2,1)} %values_ref.1), custom_call_target="tpu_custom_call" | custom-call | tf_op jit(solution)/shard_map/split_blocks/pallas_call | solution.py:88
  3.5 8.4 %all-to-all-start = ((bf16[32,17,16,128]{3,2,1,0:T(8,128)(2,1)}), bf16[32,17,16,128]{3,2,1,0:T(8,128)(2,1)S(1)}, u32[]{:S(2)}, u32[]{:S(2)}) async-start(bf16[32,17,16,128]{3,2,1,0:T(8,128)(2,1)} %split_blocks.1), calls=%async_computation | async-start | bytes 4456448 | tf_op jit(solution)/shard_map/all_to_all | solution.py:375
  12.0 0.3 zero_table.1.zeros_ref
  12.2 0.0 copy-start
  12.2 1.9 %copy-done = f32[512,16,128]{2,1,0:T(8,128)} copy-done((f32[512,16,128]{2,1,0:T(8,128)}, f32[512,16,128]{2,1,0:T(8,128)S(1)}, u32[]{:S(2)}) %copy-start) | copy-done | bytes 4194328
  14.8 27.5 %all-to-all-done = bf16[32,17,16,128]{3,2,1,0:T(8,128)(2,1)S(1)} async-done(((bf16[32,17,16,128]{3,2,1,0:T(8,128)(2,1)}), bf16[32,17,16,128]{3,2,1,0:T(8,128)(2,1)S(1)}, u32[]{:S(2)}, u32[]{:S(2)}) %all-to-all-start) | async-done | bytes 2228256 | tf_op jit(solution)/shard_map/all_to_all | solution.py:375
  42.4 0.1 add.13.index_ref
  42.5 1.2 pick_requested.1
  43.6 0.0 copy-start.2
  43.6 0.0 copy-start.3
  43.7 0.0 copy-start.4
  43.7 0.0 copy-start.5
  43.7 31.2 %all_to_all.20.kv_ref = bf16[32,256,128]{2,1,0:T(8,128)(2,1)S(1)} all-to-all(bf16[32,256,128]{2,1,0:T(8,128)(2,1)S(1)} %bitcast.22), channel_id=1, replica_groups=mesh['wide'=32,'mp'=4] {'wide'}, dimensions={0} | all-to-all | bytes 4194304 | tf_op jit(solution)/shard_map/all_to_all | solution.py:375
  74.9 0.0 copy-done.2
  74.9 0.0 copy-done.3
  74.9 0.0 copy-done.4
  74.9 0.0 copy-done.5
  74.9 13.6 %attend_forward_backward.1 = (bf16[32,256,128]{2,1,0:T(8,128)(2,1)S(1)}, f32[2,128,1024]{2,1,0:T(8,128)S(1)}, bf16[2,8,256,1024]{3,2,1,0:T(8,128)(2,1)S(1)}, bf16[2,128,1024]{2,1,0:T(8,128)(2,1)S(1)}) custom-call(s32[8,128]{1,0:T(8,128)S(1)} %get-tuple-element.21.length_ref, bf16[32,256,128]{2,1,0:T(8,128)(2,1)S(1)} %all_to_all.20.kv_ref, ...), custom_call_target="tpu_custom_call" | custom-call | flops 5704253440 | bytes 8388608 | tf_op jit(solution)/shard_map/attend_forward_backward/pallas_call | solution.py:211
  88.5 0.0 copy-start.1
  88.5 32.1 %all_to_all.21 = bf16[32,256,128]{2,1,0:T(8,128)(2,1)S(1)} all-to-all(bf16[32,256,128]{2,1,0:T(8,128)(2,1)S(1)} %get-tuple-element.24), channel_id=1, replica_groups=mesh['wide'=32,'mp'=4] {'wide'}, dimensions={0} | all-to-all | bytes 4194304 | tf_op jit(solution)/shard_map/all_to_all | solution.py:375
  120.7 0.0 copy-done.1
  120.7 2.0 %add_over_readers.1 = (bf16[32,272,128]{2,1,0:T(8,128)(2,1)S(1)}, f32[512,16,128]{2,1,0:T(8,128)S(1)}) custom-call(s32[32,16]{1,0:T(8,128)S(1)} %get-tuple-element.34.index_ref, bf16[32,16,16,128]{3,2,1,0:T(8,128)(2,1)S(1)} %bitcast.21, f32[512,16,128]{2,1,0:T(8,128)S(1)} %copy-done.1), custom_call_target="tpu_custom_call", output_to_operand_aliasing={{1}: (2, {})} | custom-call | tf_op jit(solution)/shard_map/add_over_readers/pallas_call | solution.py:319
  122.7 34.2 %all_to_all.22.refs_4_ = bf16[32,272,128]{2,1,0:T(8,128)(2,1)S(1)} all-to-all(bf16[32,272,128]{2,1,0:T(8,128)(2,1)S(1)} %get-tuple-element.26), channel_id=1, replica_groups=mesh['wide'=32,'mp'=4] {'wide'}, dimensions={0} | all-to-all | bytes 4456448 | tf_op jit(solution)/shard_map/all_to_all | solution.py:375
  156.9 0.1 convert_reduce_fusion.refs_0_
  157.0 2.8 %collective-permute-start.2 = (f32[8,128]{1,0:T(8,128)S(1)}, f32[8,128]{1,0:T(8,128)S(1)}, u32[]{:S(2)}, u32[]{:S(2)}) collective-permute-start(f32[8,128]{1,0:T(8,128)S(1)} %convert_reduce_fusion.refs_0_), channel_id=1, source_target_pairs={{0,3},{1,0},{2,1},{3,2},{4,7},{5,4},{6,5},{7,6},{8,11},{9,8},{10,9... | collective-permute-start | bytes 12296 | tf_op jit(solution)/shard_map/ppermute | solution.py:412
  159.8 0.8 collective-permute-start.1
  160.6 0.9 collective-permute-start
  161.5 2.5 %outputs_by_query.1 = (bf16[128,2048]{1,0:T(8,128)(2,1)}, bf16[128,2048]{1,0:T(8,128)(2,1)}) custom-call(bf16[32,256,128]{2,1,0:T(8,128)(2,1)S(1)} %all_to_all.20.kv_ref, bf16[128,256]{1,0:T(8,128)(2,1)S(1)} %bitcast.24, f32[2,128,1024]{2,1,0:T(8,128)S(1)} %get-tuple-element.27.out_t_ref, bf16[2,8,256,1024]{3,2,1,0:T(8,128)(2,1)S(1)} %get-tuple-element.28.slope_ref, ...), custom_call_target="tpu_custom_call" | custom-call | flops 2147483648 | bytes 12582912 | tf_op jit(solution)/shard_map/outputs_by_query/pallas_call | solution.py:261
  164.0 0.0 collective-permute-done.2.refs_3_
  164.0 0.9 collective-permute-done.1.refs_2_
  164.9 0.5 collective-permute-done.refs_1_
  165.4 2.3 %normalize_updates.1 = (f32[16,128,256]{2,1,0:T(8,128)}, f32[16,128,256]{2,1,0:T(8,128)}) custom-call(f32[8,128]{1,0:T(8,128)S(1)} %convert_reduce_fusion.refs_0_, f32[8,128]{1,0:T(8,128)S(1)} %collective-permute-done.refs_1_, f32[8,128]{1,0:T(8,128)S(1)} %collective-permute-done.1.refs_2_, f32[8,128]{1,0:T(8,128)S(1)} %collective-permute-done.2.refs_3_, ...), custom_call_target="tpu_custom_call" | custom-call | tf_op jit(solution)/shard_map/normalize_updates/pallas_call | solution.py:359
  (4 shorter events, 0.0 us)
Async XLA Ops:
  3.5 38.8 %all-to-all-start = ((bf16[32,17,16,128]{3,2,1,0:T(8,128)(2,1)}), bf16[32,17,16,128]{3,2,1,0:T(8,128)(2,1)S(1)}, u32[]{:S(2)}, u32[]{:S(2)}) async-start(bf16[32,17,16,128]{3,2,1,0:T(8,128)(2,1)} %split_blocks.1), calls=%async_computation | async-start | bytes 4456448 | tf_op jit(solution)/shard_map/all_to_all | solution.py:375
  12.2 1.9 %copy-start = (f32[512,16,128]{2,1,0:T(8,128)}, f32[512,16,128]{2,1,0:T(8,128)S(1)}, u32[]{:S(2)}) copy-start(f32[512,16,128]{2,1,0:T(8,128)S(1)} %zero_table.1.zeros_ref) | copy-start | bytes 12582916
  43.6 31.2 %copy-start.2 = (bf16[1,128,256]{2,1,0:T(8,128)(2,1)S(1)}, bf16[1,128,256]{2,1,0:T(8,128)(2,1)}, u32[]{:S(2)}) copy-start(bf16[1,128,256]{2,1,0:T(8,128)(2,1)} %param.10) | copy-start | bytes 196612
  43.6 31.2 %copy-start.3 = (bf16[1,128,2048]{2,1,0:T(8,128)(2,1)S(1)}, bf16[1,128,2048]{2,1,0:T(8,128)(2,1)}, u32[]{:S(2)}) copy-start(bf16[1,128,2048]{2,1,0:T(8,128)(2,1)} %param.9) | copy-start | bytes 1572868
  43.7 31.2 %copy-start.4 = (bf16[1,128,2048]{2,1,0:T(8,128)(2,1)S(1)}, bf16[1,128,2048]{2,1,0:T(8,128)(2,1)}, u32[]{:S(2)}) copy-start(bf16[1,128,2048]{2,1,0:T(8,128)(2,1)} %param.17) | copy-start | bytes 1572868
  43.7 31.2 %copy-start.5 = (bf16[1,128,256]{2,1,0:T(8,128)(2,1)S(1)}, bf16[1,128,256]{2,1,0:T(8,128)(2,1)}, u32[]{:S(2)}) copy-start(bf16[1,128,256]{2,1,0:T(8,128)(2,1)} %param.11) | copy-start | bytes 196612
  88.5 32.2 %copy-start.1 = (f32[512,16,128]{2,1,0:T(8,128)S(1)}, f32[512,16,128]{2,1,0:T(8,128)}, u32[]{:S(2)}) copy-start(f32[512,16,128]{2,1,0:T(8,128)} %copy-done) | copy-start | bytes 12582916
  157.0 7.0 %collective-permute-start.2 = (f32[8,128]{1,0:T(8,128)S(1)}, f32[8,128]{1,0:T(8,128)S(1)}, u32[]{:S(2)}, u32[]{:S(2)}) collective-permute-start(f32[8,128]{1,0:T(8,128)S(1)} %convert_reduce_fusion.refs_0_), channel_id=1, source_target_pairs={{0,3},{1,0},{2,1},{3,2},{4,7},{5,4},{6,5},{7,6},{8,11},{9,8},{10,9... | collective-permute-start | bytes 12296 | tf_op jit(solution)/shard_map/ppermute | solution.py:412
  159.8 5.1 %collective-permute-start.1 = (f32[8,128]{1,0:T(8,128)S(1)}, f32[8,128]{1,0:T(8,128)S(1)}, u32[]{:S(2)}, u32[]{:S(2)}) collective-permute-start(f32[8,128]{1,0:T(8,128)S(1)} %convert_reduce_fusion.refs_0_), channel_id=1, source_target_pairs={{0,2},{1,3},{2,0},{3,1},{4,6},{5,7},{6,4},{7,5},{8,10},{9,11},{10,... | collective-permute-start | bytes 12296 | tf_op jit(solution)/shard_map/ppermute | solution.py:412
  160.6 4.8 %collective-permute-start = (f32[8,128]{1,0:T(8,128)S(1)}, f32[8,128]{1,0:T(8,128)S(1)}, u32[]{:S(2)}, u32[]{:S(2)}) collective-permute-start(f32[8,128]{1,0:T(8,128)S(1)} %convert_reduce_fusion.refs_0_), channel_id=1, source_target_pairs={{0,1},{1,2},{2,3},{3,0},{4,5},{5,6},{6,7},{7,4},{8,9},{9,10},{10,1... | collective-permute-start | bytes 12296 | tf_op jit(solution)/shard_map/ppermute | solution.py:412

commit v10 on v7

--- a/solution.py
+++ b/solution.py
@@ -111,7 +111,7 @@
             out_ref[n * 16 + u] = held_ref[index_ref[n * 16 + u]]
         return carry
 
-    lax.fori_loop(0, out_ref.shape[0] // 16, step, 0)
+    lax.fori_loop(0, out_ref.shape[0] // 16, step, 0, unroll=2)
 
 
 def pick(index, length, held):
@@ -160,6 +160,7 @@
     row_used = position < used
     own_at = lax.broadcasted_iota(jnp.int32, (own, rows), 0)
     seen = (own_at <= position) & (own_at < used)
+    ones = jnp.ones((16, chunk), jnp.bfloat16)
     for head in range(HEADS):
         lanes = slice(head * HD, (head + 1) * HD)
         own_k = own_k_ref[:, lanes]
@@ -177,18 +178,16 @@
             top = jnp.maximum(top, jnp.max(s.reshape(chunk // 8, 8, rows), axis=0))
         top = jnp.max(top, axis=0, keepdims=True) * log2e
         e = jnp.exp2(own_s * log2e - top)
-        total = jnp.sum(e.reshape(own // 8, 8, rows), axis=0)
         own_e = e.astype(jnp.bfloat16)
-        acc[...] = nn(own_v.T, own_e)
+        acc[...] = nn(jnp.concatenate([own_v.T, ones[:, :own]], axis=0), own_e)
         for c in range(chunks):
             e = jnp.exp2(score[c] * log2e - top)
-            total = total + jnp.sum(e.reshape(chunk // 8, 8, rows), axis=0)
             low = e.astype(jnp.bfloat16)
             expo[c] = low
-            acc[...] += nn(kv_ref[at(c, 1)].T, low)
-        inv = 1.0 / jnp.sum(total, axis=0, keepdims=True)
+            acc[...] += nn(jnp.concatenate([kv_ref[at(c, 1)].T, ones], axis=0), low)
+        inv = 1.0 / acc[HD : HD + 1]
         g = jnp.where(row_used, g_cols[...].astype(jnp.float32), 0.0)
-        out = jnp.where(row_used, acc[...] * inv, 0.0)
+        out = jnp.where(row_used, acc[:HD] * inv, 0.0)
         out_ref[head] = out
         delta = jnp.sum(g * out, axis=0, keepdims=True) * inv
         gs = (g * inv).astype(jnp.bfloat16)
@@ -222,7 +221,7 @@
         scratch_shapes=[
             pltpu.VMEM((chunks, chunk, rows), jnp.float32),
             pltpu.VMEM((chunks, chunk, rows), jnp.bfloat16),
-            pltpu.VMEM((HD, rows), jnp.float32),
+            pltpu.VMEM((HD + 16, rows), jnp.float32),
             pltpu.VMEM((rows, HD), jnp.bfloat16),
             pltpu.VMEM((HD, rows), jnp.bfloat16),
         ],

time: 168 us -> 168 us (level)
  no operation moved by 1% of the time
where the time goes in v10:
time: 168 us; the launch traced here: 167 us
  blocking collectives  96.7 us (58%)
  waiting for transfers between devices  31.1 us (19%)
  Pallas kernels  24.7 us (15%)
  starting transfers between devices  12.9 us (8%)
    all_to_all x3, blocking collectives, swap(): return lax.all_to_all(a, 'wide', split_axis=0, concat_axis=0, tiled=True)  96.7 us
    all_to_all x1, waiting for transfers between devices, swap(): return lax.all_to_all(a, 'wide', split_axis=0, concat_axis=0, tiled=True)  29.7 us
    pallas_call x1, Pallas kernels, attend(): pl.pallas_call(attend_kernel, out_shape=(jax.ShapeDtypeStruct(kv.shape, j...  13.6 us
    all_to_all x1, starting transfers between devices, swap(): return lax.all_to_all(a, 'wide', split_axis=0, concat_axis=0, tiled=True)  8.43 us
    ppermute x3, starting transfers between devices, local(): lax.ppermute(squares, 'mp', pairs)  4.51 us
  transfers between devices with their start and end apart: 4, of which 3 were waited for; matrix products, arithmetic and copies ran while one was open for 0% of the time, Pallas kernels for 2%

profile of v10, /device:TPU:0, one launch (start us, length us, event | category | flops | bytes accessed | tf_op | source)
XLA Modules:
  0.0 167.2 jit_solution(12121941054813113840)
XLA Ops:
  0.6 2.9 %split_blocks.1 = bf16[32,17,16,128]{3,2,1,0:T(8,128)(2,1)} custom-call(s32[1,16]{1,0:T(1,128)} %ids_ref.1, s32[512]{0:T(512)} %home_ref.1, bf16[16,128,256]{2,1,0:T(8,128)(2,1)} %keys_ref.1, bf16[16,128,256]{2,1,0:T(8,128)(2,1)} %values_ref.1), custom_call_target="tpu_custom_call" | custom-call | tf_op jit(solution)/shard_map/split_blocks/pallas_call | solution.py:88
  3.5 8.4 %all-to-all-start = ((bf16[32,17,16,128]{3,2,1,0:T(8,128)(2,1)}), bf16[32,17,16,128]{3,2,1,0:T(8,128)(2,1)S(1)}, u32[]{:S(2)}, u32[]{:S(2)}) async-start(bf16[32,17,16,128]{3,2,1,0:T(8,128)(2,1)} %split_blocks.1), calls=%async_computation | async-start | bytes 4456448 | tf_op jit(solution)/shard_map/all_to_all | solution.py:360
  12.6 29.7 %all-to-all-done = bf16[32,17,16,128]{3,2,1,0:T(8,128)(2,1)S(1)} async-done(((bf16[32,17,16,128]{3,2,1,0:T(8,128)(2,1)}), bf16[32,17,16,128]{3,2,1,0:T(8,128)(2,1)S(1)}, u32[]{:S(2)}, u32[]{:S(2)}) %all-to-all-start) | async-done | bytes 2228256 | tf_op jit(solution)/shard_map/all_to_all | solution.py:360
  42.4 0.1 add.13.index_ref
  42.5 1.2 pick_requested.1
  43.6 0.0 copy-start
  43.6 0.0 copy-start.1
  43.6 0.0 copy-start.2
  43.7 0.0 copy-start.3
  43.7 31.2 %all_to_all.20.kv_ref = bf16[32,256,128]{2,1,0:T(8,128)(2,1)S(1)} all-to-all(bf16[32,256,128]{2,1,0:T(8,128)(2,1)S(1)} %bitcast.20), channel_id=1, replica_groups=mesh['wide'=32,'mp'=4] {'wide'}, dimensions={0} | all-to-all | bytes 4194304 | tf_op jit(solution)/shard_map/all_to_all | solution.py:360
  74.9 0.0 copy-done
  74.9 0.0 copy-done.1
  74.9 0.0 copy-done.2
  74.9 0.0 copy-done.3
  74.9 13.6 %attend_forward_backward.1 = (bf16[32,256,128]{2,1,0:T(8,128)(2,1)S(1)}, f32[2,128,1024]{2,1,0:T(8,128)S(1)}, bf16[2,8,256,1024]{3,2,1,0:T(8,128)(2,1)S(1)}, bf16[2,128,1024]{2,1,0:T(8,128)(2,1)S(1)}) custom-call(s32[8,128]{1,0:T(8,128)S(1)} %get-tuple-element.17.length_ref, bf16[32,256,128]{2,1,0:T(8,128)(2,1)S(1)} %all_to_all.20.kv_ref, ...), custom_call_target="tpu_custom_call" | custom-call | flops 5704253440 | bytes 8388608 | tf_op jit(solution)/shard_map/attend_forward_backward/pallas_call | solution.py:211
  88.5 31.9 %all_to_all.21 = bf16[32,256,128]{2,1,0:T(8,128)(2,1)S(1)} all-to-all(bf16[32,256,128]{2,1,0:T(8,128)(2,1)S(1)} %get-tuple-element.20), channel_id=1, replica_groups=mesh['wide'=32,'mp'=4] {'wide'}, dimensions={0} | all-to-all | bytes 4194304 | tf_op jit(solution)/shard_map/all_to_all | solution.py:360
  120.4 2.3 %add_over_readers.1 = bf16[32,264,128]{2,1,0:T(8,128)(2,1)S(1)} custom-call(s32[32,16]{1,0:T(8,128)S(1)} %get-tuple-element.28.index_ref, bf16[32,16,16,128]{3,2,1,0:T(8,128)(2,1)S(1)} %bitcast.19), custom_call_target="tpu_custom_call" | custom-call | tf_op jit(solution)/shard_map/add_over_readers/pallas_call | solution.py:307
  122.7 33.7 %all_to_all.22.refs_4_ = bf16[32,264,128]{2,1,0:T(8,128)(2,1)S(1)} all-to-all(bf16[32,264,128]{2,1,0:T(8,128)(2,1)S(1)} %add_over_readers.1), channel_id=1, replica_groups=mesh['wide'=32,'mp'=4] {'wide'}, dimensions={0} | all-to-all | bytes 4325376 | tf_op jit(solution)/shard_map/all_to_all | solution.py:360
  156.4 2.8 %collective-permute-start.2 = (f32[8,128]{1,0:T(8,128)S(1)}, f32[8,128]{1,0:T(8,128)S(1)}, u32[]{:S(2)}, u32[]{:S(2)}) collective-permute-start(f32[8,128]{1,0:T(8,128)S(1)} %convert_reduce_fusion.refs_0_), channel_id=1, source_target_pairs={{0,3},{1,0},{2,1},{3,2},{4,7},{5,4},{6,5},{7,6},{8,11},{9,8},{10,9... | collective-permute-start | bytes 12296 | tf_op jit(solution)/shard_map/ppermute | solution.py:395
  159.2 0.8 collective-permute-start.1
  160.0 0.9 collective-permute-start
  160.9 2.5 %outputs_by_query.1 = (bf16[128,2048]{1,0:T(8,128)(2,1)}, bf16[128,2048]{1,0:T(8,128)(2,1)}) custom-call(bf16[32,256,128]{2,1,0:T(8,128)(2,1)S(1)} %all_to_all.20.kv_ref, bf16[128,256]{1,0:T(8,128)(2,1)S(1)} %bitcast.22, f32[2,128,1024]{2,1,0:T(8,128)S(1)} %get-tuple-element.21.out_t_ref, bf16[2,8,256,1024]{3,2,1,0:T(8,128)(2,1)S(1)} %get-tuple-element.22.slope_ref, ...), custom_call_target="tpu_custom_call" | custom-call | flops 2147483648 | bytes 12582912 | tf_op jit(solution)/shard_map/outputs_by_query/pallas_call | solution.py:261
  163.4 0.0 collective-permute-done.2.refs_3_
  163.4 0.9 collective-permute-done.1.refs_2_
  164.3 0.5 collective-permute-done.refs_1_
  164.8 2.3 %normalize_updates.1 = (f32[16,128,256]{2,1,0:T(8,128)}, f32[16,128,256]{2,1,0:T(8,128)}) custom-call(f32[8,128]{1,0:T(8,128)S(1)} %convert_reduce_fusion.refs_0_, f32[8,128]{1,0:T(8,128)S(1)} %collective-permute-done.refs_1_, f32[8,128]{1,0:T(8,128)S(1)} %collective-permute-done.1.refs_2_, f32[8,128]{1,0:T(8,128)S(1)} %collective-permute-done.2.refs_3_, ...), custom_call_target="tpu_custom_call" | custom-call | tf_op jit(solution)/shard_map/normalize_updates/pallas_call | solution.py:344
  (4 shorter events, 0.1 us)
Async XLA Ops:
  3.5 38.8 %all-to-all-start = ((bf16[32,17,16,128]{3,2,1,0:T(8,128)(2,1)}), bf16[32,17,16,128]{3,2,1,0:T(8,128)(2,1)S(1)}, u32[]{:S(2)}, u32[]{:S(2)}) async-start(bf16[32,17,16,128]{3,2,1,0:T(8,128)(2,1)} %split_blocks.1), calls=%async_computation | async-start | bytes 4456448 | tf_op jit(solution)/shard_map/all_to_all | solution.py:360
  43.6 31.2 %copy-start = (bf16[1,128,256]{2,1,0:T(8,128)(2,1)S(1)}, bf16[1,128,256]{2,1,0:T(8,128)(2,1)}, u32[]{:S(2)}) copy-start(bf16[1,128,256]{2,1,0:T(8,128)(2,1)} %param.10) | copy-start | bytes 196612
  43.6 31.2 %copy-start.1 = (bf16[1,128,2048]{2,1,0:T(8,128)(2,1)S(1)}, bf16[1,128,2048]{2,1,0:T(8,128)(2,1)}, u32[]{:S(2)}) copy-start(bf16[1,128,2048]{2,1,0:T(8,128)(2,1)} %param.9) | copy-start | bytes 1572868
  43.6 31.2 %copy-start.2 = (bf16[1,128,2048]{2,1,0:T(8,128)(2,1)S(1)}, bf16[1,128,2048]{2,1,0:T(8,128)(2,1)}, u32[]{:S(2)}) copy-start(bf16[1,128,2048]{2,1,0:T(8,128)(2,1)} %param.17) | copy-start | bytes 1572868
  43.7 31.2 %copy-start.3 = (bf16[1,128,256]{2,1,0:T(8,128)(2,1)S(1)}, bf16[1,128,256]{2,1,0:T(8,128)(2,1)}, u32[]{:S(2)}) copy-start(bf16[1,128,256]{2,1,0:T(8,128)(2,1)} %param.11) | copy-start | bytes 196612
  156.4 7.0 %collective-permute-start.2 = (f32[8,128]{1,0:T(8,128)S(1)}, f32[8,128]{1,0:T(8,128)S(1)}, u32[]{:S(2)}, u32[]{:S(2)}) collective-permute-start(f32[8,128]{1,0:T(8,128)S(1)} %convert_reduce_fusion.refs_0_), channel_id=1, source_target_pairs={{0,3},{1,0},{2,1},{3,2},{4,7},{5,4},{6,5},{7,6},{8,11},{9,8},{10,9... | collective-permute-start | bytes 12296 | tf_op jit(solution)/shard_map/ppermute | solution.py:395
  159.2 5.1 %collective-permute-start.1 = (f32[8,128]{1,0:T(8,128)S(1)}, f32[8,128]{1,0:T(8,128)S(1)}, u32[]{:S(2)}, u32[]{:S(2)}) collective-permute-start(f32[8,128]{1,0:T(8,128)S(1)} %convert_reduce_fusion.refs_0_), channel_id=1, source_target_pairs={{0,2},{1,3},{2,0},{3,1},{4,6},{5,7},{6,4},{7,5},{8,10},{9,11},{10,... | collective-permute-start | bytes 12296 | tf_op jit(solution)/shard_map/ppermute | solution.py:395
  160.0 4.8 %collective-permute-start = (f32[8,128]{1,0:T(8,128)S(1)}, f32[8,128]{1,0:T(8,128)S(1)}, u32[]{:S(2)}, u32[]{:S(2)}) collective-permute-start(f32[8,128]{1,0:T(8,128)S(1)} %convert_reduce_fusion.refs_0_), channel_id=1, source_target_pairs={{0,1},{1,2},{2,3},{3,0},{4,5},{5,6},{6,7},{7,4},{8,9},{9,10},{10,1... | collective-permute-start | bytes 12296 | tf_op jit(solution)/shard_map/ppermute | solution.py:395
